TPU v7x, 256 devices: a whole 4x4x8 slice. The times are simulated.
256 devices in a mesh: dp: 16 (over z_lo, y, core), tensor: 16 (over x, z_hi).
Axes of the slice: x: 4, y: 4, z: 8 (z_hi: 4, z_lo: 2; z = z_hi * 2 + z_lo), core: 2. Of those that a mesh axis runs over, the one named last changes fastest.
Arguments:
- saved_codes: bfloat16 [3072, 4096], P(('dp', 'tensor')), may hold values from -24 to 24
- saved_scales: bfloat16 [3072, 32], P(('dp', 'tensor')), may hold values from 0.25 to 4
- gate_weight: bfloat16 [4096, 14336], P('dp', 'tensor'), may hold values from -0.09375 to 0.09375
- up_weight: bfloat16 [4096, 14336], P('dp', 'tensor'), may hold values from -0.09375 to 0.09375
- hidden_grad: bfloat16 [3072, 14336], P('dp', 'tensor'), may hold values from -6 to 6
Outputs:
- input_grad: bfloat16 [3072, 4096], P(('dp', 'tensor'))
- gate_grad: float32 [4096, 14336], P('dp', 'tensor')
- up_grad: float32 [4096, 14336], P('dp', 'tensor')
All inputs are finite; a program needn't handle non-finite values.
Results may differ from a plain program's by a relative error of at most 0.02.
Values may be sent and summed in bfloat16 or wider, within the bound.
No kernel may reach another device: no remote copies, remote signals or barrier semaphores. Data moves between devices by JAX's collectives and lax.ppermute only.
A program may use at most 128 MiB of HBM per device.

v0:
```python
import jax
import jax.numpy as jnp
from jax import lax
from jax.sharding import PartitionSpec as P


def dequantize(code_rows, scale_rows):
    row_count, features = code_rows.shape
    blocks = scale_rows.shape[1]
    values = (
        code_rows.astype(jnp.float32).reshape(row_count, blocks, features // blocks)
        * scale_rows.astype(jnp.float32)[:, :, None]
    )
    return values.reshape(row_count, features).astype(jnp.bfloat16)


def local(saved_codes, saved_scales, gate_weight, up_weight, hidden_grad):
    code_rows, scale_rows = (
        lax.all_gather(saved_codes, "tensor", axis=0, tiled=True),
        lax.all_gather(saved_scales, "tensor", axis=0, tiled=True),
    )
    inputs = dequantize(code_rows, scale_rows)
    tok_rows, features = inputs.shape
    row_share, hidden_share = gate_weight.shape
    pieces = (
        lax.all_gather(gate_weight, "dp", axis=0, tiled=True),
        lax.all_gather(up_weight, "dp", axis=0, tiled=True),
    )
    columns = inputs
    gate_sum = jnp.dot(columns, pieces[0], preferred_element_type=jnp.float32)
    up_sum = jnp.dot(columns, pieces[1], preferred_element_type=jnp.float32)
    take_gate_full = pieces[0]
    take_up_full = pieces[1]
    gate_sum, up_sum, gate_full, up_full = (gate_sum, up_sum, take_gate_full, take_up_full)
    gate_sigmoid = jax.nn.sigmoid(gate_sum)
    upstream = hidden_grad.astype(jnp.float32)
    grad_gate = (upstream * up_sum * gate_sigmoid * (1.0 + gate_sum * (1.0 - gate_sigmoid))).astype(
        jnp.bfloat16
    )
    grad_up = (upstream * gate_sum * gate_sigmoid).astype(jnp.bfloat16)
    contract = (((1,), (1,)), ((), ()))
    input_share = lax.psum_scatter(
        (
            lax.dot_general(grad_gate, gate_full, contract, preferred_element_type=jnp.float32)
            + lax.dot_general(grad_up, up_full, contract, preferred_element_type=jnp.float32)
        ).astype(jnp.bfloat16),
        "tensor",
        scatter_dimension=0,
        tiled=True,
    )
    grad_pair = jnp.concatenate([grad_gate, grad_up], axis=1)
    columns = inputs
    summed = lax.psum_scatter(
        (
            lax.dot_general(
                columns, grad_pair, (((0,), (0,)), ((), ())), preferred_element_type=jnp.float32
            )
            / tok_rows
        ).astype(jnp.bfloat16),
        "dp",
        scatter_dimension=0,
        tiled=True,
    ).astype(jnp.float32)
    return (input_share, summed[:, :hidden_share], summed[:, hidden_share:])


def solution(mesh):
    placed = (
        P(("dp", "tensor"), None),
        P(("dp", "tensor"), None),
        P("dp", "tensor"),
        P("dp", "tensor"),
        P("dp", "tensor"),
    )
    return jax.shard_map(
        local,
        mesh=mesh,
        in_specs=placed,
        out_specs=(P(("dp", "tensor"), None), P("dp", "tensor"), P("dp", "tensor")),
        check_vma=False,
    )
```

profile of v0, /device:TPU:64, one launch (start us, length us, event | category | flops | bytes accessed | tf_op | source)
XLA Modules:
  0.0 344.5 jit_solution(15363923686209221190)
XLA Ops:
  7.2 0.0 all-gather.10.cloned.1.call-start
  7.2 0.7 all-gather.10.cloned.1.call-update
  7.9 0.0 all-gather.8.cloned.1.call-start
  7.9 0.7 all-gather.8.cloned.1.call-update
  8.6 0.0 all-gather.6.cloned.1.call-start
  8.7 0.7 all-gather.6.cloned.1.call-update
  9.4 0.0 reduce-scatter.4.cloned.1.call-start
  9.4 42.4 %all-gather.1 = bf16[16,12,32]{2,1,0:T(8,128)(2,1)S(1)} all-gather(bf16[1,12,32]{2,1,0:T(8,128)(2,1)} %bitcast.21), channel_id=1, replica_groups=mesh['dp'=16,'tensor'=16] {'tensor'}, dimensions={0}, use_global_device_ids=true | all-gather | bytes 13056 | tf_op jit(solution)/shard_map/all_gather | solution.py:20
  51.9 19.3 %all-gather.10.cloned.1.call-done = bf16[16,12,4096]{2,1,0:T(8,128)(2,1)} async-done(((bf16[1,12,4096]{2,1,0:T(8,128)(2,1)}), bf16[16,12,4096]{2,1,0:T(8,128)(2,1)}) %all-gather.10.cloned.1.call-update) | async-done | bytes 1572880 | tf_op jit(solution)/shard_map/all_gather | solution.py:19
  71.1 2.4 reshape.14
  73.6 0.9 mul.29
  74.4 0.0 copy-start.2
  74.4 3.0 fusion.2
  77.4 0.0 copy-start
  77.4 44.5 %all-gather.8.cloned.1.call-done = bf16[4096,896]{1,0:T(8,128)(2,1)} async-done(((bf16[256,896]{1,0:T(8,128)(2,1)}), bf16[4096,896]{1,0:T(8,128)(2,1)}) %all-gather.8.cloned.1.call-update) | async-done | bytes 7340048 | tf_op jit(solution)/shard_map/all_gather | solution.py:26
  121.9 0.0 copy-done.2
  121.9 5.4 %fusion.7 = (bf16[192,896]{1,0:T(8,128)(2,1)S(1)}, f32[192,896]{1,0:T(8,128)S(1)}) fusion(bf16[192,896]{1,0:T(8,128)(2,1)S(1)} %copy-done.2, bf16[192,4096]{1,0:T(8,128)(2,1)} %fusion.2, bf16[4096,896]{1,0:T(8,128)(2,1)} %all-gather.8.cloned.1.call-done), kind=kOutput, calls=%fused_computation.11 | convolution fusion | flops 1410490368 | bytes 10289152 | tf_op jit(solution)/shard_map/dot_general | solution.py:30
  127.3 47.1 %all-gather.6.cloned.1.call-done = bf16[4096,896]{1,0:T(8,128)(2,1)} async-done(((bf16[256,896]{1,0:T(8,128)(2,1)}), bf16[4096,896]{1,0:T(8,128)(2,1)}) %all-gather.6.cloned.1.call-update) | async-done | bytes 7340048 | tf_op jit(solution)/shard_map/all_gather | solution.py:27
  174.5 0.0 copy-done
  174.5 5.0 %fusion.5 = bf16[192,896]{1,0:T(8,128)(2,1)S(1)} fusion(bf16[192,4096]{1,0:T(8,128)(2,1)S(1)} %copy-done, bf16[4096,896]{1,0:T(8,128)(2,1)} %all-gather.6.cloned.1.call-done, bf16[192,896]{1,0:T(8,128)(2,1)S(1)} %copy-done.2, f32[192,896]{1,0:T(8,128)S(1)} %get-tuple-element.6), kind=kOutput, calls=%fused_computation.8 | convolution fusion | flops 1411178496 | bytes 10289152 | tf_op jit(solution)/shard_map/dot_general | solution.py:31
  179.4 7.4 %multiply_convert_fusion = bf16[4096,1792]{1,0:T(8,128)(2,1)} fusion(bf16[192,4096]{1,0:T(8,128)(2,1)S(1)} %copy-done, bf16[192,896]{1,0:T(8,128)(2,1)S(1)} %get-tuple-element.5, bf16[192,896]{1,0:T(8,128)(2,1)S(1)} %fusion.5), kind=kOutput, calls=%fused_computation | convolution fusion | flops 2834628608 | bytes 16941056 | tf_op jit(solution)/shard_map/dot_general | solution.py:55
  186.8 0.0 reduce-scatter.4.cloned.1.call-update
  186.8 5.7 %fusion.13 = f32[192,4096]{1,0:T(8,128)S(1)} fusion(bf16[192,896]{1,0:T(8,128)(2,1)S(1)} %fusion.5, bf16[4096,896]{1,0:T(8,128)(2,1)} %all-gather.8.cloned.1.call-done), kind=kOutput, calls=%fused_computation.19 | convolution fusion | flops 1409286144 | bytes 10829824 | tf_op jit(solution)/shard_map/dot_general | solution.py:44
  192.5 0.0 copy-start.1
  192.5 5.7 %fusion.1 = bf16[192,4096]{1,0:T(8,128)(2,1)S(1)} fusion(f32[192,4096]{1,0:T(8,128)S(1)} %fusion.13, bf16[192,896]{1,0:T(8,128)(2,1)S(1)} %get-tuple-element.5, bf16[4096,896]{1,0:T(8,128)(2,1)} %all-gather.6.cloned.1.call-done), kind=kOutput, calls=%fused_computation.2 | convolution fusion | flops 1410859008 | bytes 12402688 | tf_op jit(solution)/shard_map/dot_general | solution.py:45
  198.2 73.7 %fusion = bf16[16,4096]{1,0:T(8,128)(2,1)S(1)} fusion(bf16[192,4096]{1,0:T(8,128)(2,1)S(1)} %fusion.1), kind=kCustom, calls=%all-reduce-scatter | all-reduce-scatter fusion | flops 1048577 | bytes 1704960
  271.9 1.9 collective-permute-start
  273.8 6.0 %collective-permute-start.1 = (bf16[16,4096]{1,0:T(8,128)(2,1)S(1)}, bf16[16,4096]{1,0:T(8,128)(2,1)S(1)}, u32[]{:S(2)}, u32[]{:S(2)}) collective-permute-start(bf16[16,4096]{1,0:T(8,128)(2,1)S(1)} %fusion), channel_id=1, source_target_pairs={{0,2},{1,3},{2,4},{3,5},{4,6},{5,7},{6,8},{7,9},{8,10},{9,11},{10,... | collective-permute-start | bytes 393224
  279.8 2.0 collective-permute-start.2
  281.8 1.4 collective-permute-start.3
  283.2 0.0 copy-done.1
  283.2 0.6 dynamic-slice.4
  284.5 3.9 %collective-permute-done.3 = bf16[12,4096]{1,0:T(8,128)(2,1)S(1)} collective-permute-done((bf16[12,4096]{1,0:T(8,128)(2,1)S(1)}, bf16[12,4096]{1,0:T(8,128)(2,1)S(1)}, u32[]{:S(2)}, u32[]{:S(2)}) %collective-permute-start.3) | collective-permute-done | bytes 98336
  288.3 0.0 collective-permute-done
  288.3 0.0 collective-permute-done.1
  288.3 0.0 collective-permute-done.2
  288.3 1.2 concatenate.4
  289.6 0.7 constant_dynamic-slice_fusion
  290.3 45.1 %reduce-scatter.4.cloned.1.call-done = bf16[256,1792]{1,0:T(8,128)(2,1)} async-done(((bf16[4096,1792]{1,0:T(8,128)(2,1)}), bf16[256,1792]{1,0:T(8,128)(2,1)}) %reduce-scatter.4.cloned.1.call-update) | async-done | bytes 917520 | tf_op jit(solution)/shard_map/reduce_scatter | solution.py:53
  335.4 2.5 fusion.12
  (2 shorter events, 0.1 us)
Async XLA Ops:
  7.2 64.0 %all-gather.10.cloned.1.call-start = ((), (), s32[]{:S(2)}) async-start(), calls=%async_computation.4 | async-start | bytes 2228224 | tf_op jit(solution)/shard_map/all_gather | solution.py:19
  7.9 114.0 %all-gather.8.cloned.1.call-start = ((), (), s32[]{:S(2)}) async-start(), calls=%async_computation.2 | async-start | bytes 7798784 | tf_op jit(solution)/shard_map/all_gather | solution.py:26
  8.6 165.8 %all-gather.6.cloned.1.call-start = ((), (), s32[]{:S(2)}) async-start(), calls=%async_computation.1 | async-start | bytes 7798784 | tf_op jit(solution)/shard_map/all_gather | solution.py:27
  9.4 326.0 %reduce-scatter.4.cloned.1.call-start = ((), (), s32[]{:S(2)}) async-start(), calls=%async_computation.3 | async-start | bytes 15597568 | tf_op jit(solution)/shard_map/reduce_scatter | solution.py:53
  74.4 47.5 %copy-start.2 = (bf16[192,896]{1,0:T(8,128)(2,1)S(1)}, bf16[192,896]{1,0:T(8,128)(2,1)}, u32[]{:S(2)}) copy-start(bf16[192,896]{1,0:T(8,128)(2,1)} %param.9) | copy-start | bytes 1032196
  77.4 97.0 %copy-start = (bf16[192,4096]{1,0:T(8,128)(2,1)S(1)}, bf16[192,4096]{1,0:T(8,128)(2,1)}, u32[]{:S(2)}) copy-start(bf16[192,4096]{1,0:T(8,128)(2,1)} %fusion.2) | copy-start | bytes 4718596
  192.5 90.8 %copy-start.1 = (u32[256]{0:T(256)S(1)}, u32[256]{0:T(256)}, u32[]{:S(2)}) copy-start(u32[256]{0:T(256)} %constant.9) | copy-start | bytes 3076
  271.9 16.5 %collective-permute-start = (bf16[16,4096]{1,0:T(8,128)(2,1)S(1)}, bf16[16,4096]{1,0:T(8,128)(2,1)S(1)}, u32[]{:S(2)}, u32[]{:S(2)}) collective-permute-start(bf16[16,4096]{1,0:T(8,128)(2,1)S(1)} %fusion), channel_id=1, source_target_pairs={{0,1},{1,2},{2,3},{3,4},{4,5},{5,6},{6,7},{7,8},{8,9},{9,10},{10,1... | collective-permute-start | bytes 393224
  273.8 14.5 %collective-permute-start.1 = (bf16[16,4096]{1,0:T(8,128)(2,1)S(1)}, bf16[16,4096]{1,0:T(8,128)(2,1)S(1)}, u32[]{:S(2)}, u32[]{:S(2)}) collective-permute-start(bf16[16,4096]{1,0:T(8,128)(2,1)S(1)} %fusion), channel_id=1, source_target_pairs={{0,2},{1,3},{2,4},{3,5},{4,6},{5,7},{6,8},{7,9},{8,10},{9,11},{10,... | collective-permute-start | bytes 393224
  279.8 8.6 %collective-permute-start.2 = (bf16[16,4096]{1,0:T(8,128)(2,1)S(1)}, bf16[16,4096]{1,0:T(8,128)(2,1)S(1)}, u32[]{:S(2)}, u32[]{:S(2)}) collective-permute-start(bf16[16,4096]{1,0:T(8,128)(2,1)S(1)} %fusion), channel_id=1, source_target_pairs={{0,3},{1,4},{2,5},{3,6},{4,7},{5,8},{6,9},{7,10},{8,11},{9,12},{10... | collective-permute-start | bytes 393224
  281.8 6.5 %collective-permute-start.3 = (bf16[12,4096]{1,0:T(8,128)(2,1)S(1)}, bf16[12,4096]{1,0:T(8,128)(2,1)S(1)}, u32[]{:S(2)}, u32[]{:S(2)}) collective-permute-start(bf16[12,4096]{1,0:T(8,128)(2,1)S(1)} %slice.10), channel_id=1, source_target_pairs={{0,4},{1,5},{2,6},{3,7},{4,8},{5,9},{6,10},{7,11},{8,12},{9,13},{1... | collective-permute-start | bytes 294920
Sparse Core Ops, SparseCore 0:
  10.4 60.6 all-gather.9
  73.0 48.8 all-gather.7
  123.8 50.6 all-gather.5
  186.9 148.4 reduce-scatter.3
where the time goes:
time: 345 us; the launch traced here: 344 us
  waiting for transfers between devices  162 us (47%)
  blocking collectives  116 us (34%)
  matrix products  29.1 us (8%)
  between operations  14.5 us (4%)
  starting transfers between devices  11.4 us (3%)
  local copies, waits for them, and re-layouts  8.37 us (2%)
    unnamed x1, blocking collectives  73.7 us
    all_gather x1, waiting for transfers between devices, local(): lax.all_gather(up_weight, 'dp', axis=0, tiled=True)  47.1 us
    reduce_scatter x1, waiting for transfers between devices, local(): lax.psum_scatter((lax.dot_general(columns, grad_pair, (((0,), (0,)), ((),...  45.1 us
    all_gather x1, waiting for transfers between devices, local(): lax.all_gather(gate_weight, 'dp', axis=0, tiled=True)  44.5 us
    all_gather x1, blocking collectives, local(): lax.all_gather(saved_scales, 'tensor', axis=0, tiled=True)  42.4 us
    all_gather x1, waiting for transfers between devices, local(): lax.all_gather(saved_codes, 'tensor', axis=0, tiled=True)  19.3 us
    unnamed x4, starting transfers between devices  11.3 us
    dot_general x1, matrix products, local(): lax.dot_general(columns, grad_pair, (((0,), (0,)), ((), ())), preferred_e...  7.35 us
  transfers between devices with their start and end apart: 8, of which 5 were waited for; matrix products, arithmetic and copies ran while one was open for 29% of the time, Pallas kernels for 0%

commit v1 on v0

v1 whole, which is shorter than its diff:
```python
import functools
import itertools

import jax
import jax.numpy as jnp
import numpy as np
from jax import lax
from jax.experimental import pallas as pl
from jax.experimental.pallas import tpu as pltpu
from jax.sharding import PartitionSpec as P

BOTH = ("dp", "tensor")
F32 = jnp.float32
BF16 = jnp.bfloat16
CHUNKS = (512, 384)
TILE = 256
VMEM_LIMIT = 16 * 1024 * 1024
VMEM = pl.BlockSpec(memory_space=pltpu.VMEM)
ANY = pl.BlockSpec(memory_space=pl.ANY)


def perm(target):
    def index(zl, y, c, x, zh):
        return ((zl * 4 + y) * 2 + c) * 16 + x * 4 + zh

    return [
        (index(*at), index(*target(*at, 3 if at[2] else 1, 1 if at[2] else 3)))
        for at in itertools.product(range(2), range(4), range(2), range(4), range(4))
    ]


TO_CORE = perm(lambda zl, y, c, x, zh, a, b: (zl, y, 1 - c, x, zh))
TO_ZL = perm(lambda zl, y, c, x, zh, a, b: (1 - zl, y, c, x, zh))
Y_A = perm(lambda zl, y, c, x, zh, a, b: (zl, y ^ a, c, x, zh))
Y_B = perm(lambda zl, y, c, x, zh, a, b: (zl, y ^ b, c, x, zh))
X_A = perm(lambda zl, y, c, x, zh, a, b: (zl, y, c, x ^ a, zh))
X_B = perm(lambda zl, y, c, x, zh, a, b: (zl, y, c, x ^ b, zh))
ZH_A = perm(lambda zl, y, c, x, zh, a, b: (zl, y, c, x, zh ^ a))
ZH_B = perm(lambda zl, y, c, x, zh, a, b: (zl, y, c, x, zh ^ b))


def send(value, pairs):
    return lax.ppermute(value, BOTH, pairs)


def fence(*values):
    return lax.optimization_barrier(values)


def call(kernel, out_shape, in_specs, out_specs, scratch=(), cost=None):
    return pl.pallas_call(
        kernel,
        out_shape=out_shape,
        in_specs=in_specs,
        out_specs=out_specs,
        scratch_shapes=list(scratch),
        cost_estimate=cost,
        compiler_params=pltpu.CompilerParams(vmem_limit_bytes=VMEM_LIMIT),
    )


def in_vmem(value):
    return pltpu.with_memory_space_constraint(value, pltpu.VMEM)


def in_hbm(value):
    return pltpu.with_memory_space_constraint(value, pltpu.HBM)


def array(shape, dtype):
    return jax.ShapeDtypeStruct(shape, dtype)


def join_kernel(gate, up, out, sems):
    width = gate.shape[1]
    copies = [
        pltpu.make_async_copy(gate, out.at[:, :width], sems.at[0]),
        pltpu.make_async_copy(up, out.at[:, width:], sems.at[1]),
    ]
    for copy in copies:
        copy.start()
    for copy in copies:
        copy.wait()


def join(gate, up):
    rows, width = gate.shape
    return call(
        join_kernel, pltpu.VMEM((rows, 2 * width), BF16), [ANY, ANY], VMEM, [pltpu.SemaphoreType.DMA((2,))]
    )(in_hbm(gate), in_hbm(up))


def places(p, first, second):
    return (p, p ^ first, p ^ second, p ^ 2)


def feature_blocks():
    dp = lax.axis_index("dp")
    zl, y, c = dp // 8, (dp // 2) % 4, dp % 2
    a, b = 1 + 2 * c, 3 - 2 * c
    blocks = [p * 2 + c for p in places(y, a, b)] + [p * 2 + 1 - c for p in places(y, b, a)]
    starts = [(zl * 8 + k) * 256 for k in blocks] + [((1 - zl) * 8 + k) * 256 for k in blocks]
    return [pl.ds(pl.multiple_of(start, 256), 256) for start in starts]


def dequantize_kernel(codes, scales, own, other, values):
    blocks = scales.shape[1]
    width = codes.shape[1] // blocks
    for b in range(blocks):
        at = slice(b * width, (b + 1) * width)
        values[:, at] = (codes[:, at].astype(F32) * scales[:, b : b + 1].astype(F32)).astype(BF16)
    spans = feature_blocks()
    for k in range(8):
        at = slice(k * 256, (k + 1) * 256)
        own[:, at] = values[:, spans[k]]
        other[:, at] = values[:, spans[8 + k]]


def dequantize(codes, scales):
    rows, features = codes.shape
    half = array((rows, features // 2), BF16)
    return call(
        dequantize_kernel, (half, half), [VMEM, VMEM], (VMEM, VMEM), [pltpu.VMEM((rows, features), BF16)]
    )(codes, scales)


def restore_kernel(own, other, out):
    spans = feature_blocks()
    for k in range(8):
        at = slice(k * 256, (k + 1) * 256)
        out[:, spans[k]] = own[:, at]
        out[:, spans[8 + k]] = other[:, at]


def restore(own, other):
    rows, half = own.shape
    return call(restore_kernel, array((rows, 2 * half), BF16), [VMEM, VMEM], VMEM)(own, other)


def token_table(rows):
    table = np.zeros((2, 4, 4, 1, 16 * rows), np.int32)
    for c, x, zh in itertools.product(range(2), range(4), range(4)):
        a, b = 1 + 2 * c, 3 - 2 * c
        at = [p * 4 + q for p in places(x, a, b) for q in places(zh, a, b)]
        table[c, x, zh, 0] = (np.array(at)[:, None] * rows + np.arange(rows)).reshape(-1)
    return table.reshape(32, 1, 16 * rows)


def arrange_kernel(table, values, out):
    source = table[lax.axis_index("dp") % 2 * 16 + lax.axis_index("tensor")]
    group = values.shape[0]
    pick = (lax.broadcasted_iota(jnp.int32, (group, group), 0) == source).astype(F32).astype(BF16)
    out[...] = lax.dot_general(
        pick, values[...], (((0,), (0,)), ((), ())), preferred_element_type=F32
    ).astype(BF16)


def arrange(values, rows):
    return call(arrange_kernel, array(values.shape, BF16), [VMEM, VMEM], VMEM)(token_table(rows), values)


def near_kernel(values, *refs):
    weights, (held, own, par, rows, sems) = refs[:8], refs[8:]
    copies = [
        pltpu.make_async_copy(weights[k], held.at[256 * k : 256 * (k + 1)], sems.at[k]) for k in range(8)
    ]
    for copy in copies:
        copy.start()
    split_rows(values, rows)
    for copy in copies:
        copy.wait()
    half = own.shape[0]
    for at in range(0, held.shape[1], TILE):
        span = slice(at, at + TILE)
        result = jnp.dot(rows[...], held[:, span], preferred_element_type=F32)
        own[:, span] = result[:half]
        par[:, span] = result[half:].astype(BF16)


def split_rows(values, rows):
    part = values.shape[0] // 4
    for q in range(2):
        for z in range(2):
            rows[(2 * z + q) * part : (2 * z + q + 1) * part, :] = values[
                (2 * q + z) * part : (2 * q + z + 1) * part, :
            ]


def near_products(values, weights):
    tokens, features = values.shape
    width = weights[0].shape[1]
    outs = (
        pltpu.VMEM((features, width), BF16),
        pltpu.VMEM((tokens // 2, width), F32),
        pltpu.VMEM((tokens // 2, width), BF16),
    )
    scratch = [pltpu.VMEM((tokens, features), BF16), pltpu.SemaphoreType.DMA((8,))]
    return call(near_kernel, outs, [VMEM] + [ANY] * 8, (VMEM,) * 3, scratch)(values, *weights)


def away_kernel(values, held, own, par, rows):
    split_rows(values, rows)
    half = own.shape[0]
    for at in range(0, held.shape[1], TILE):
        span = slice(at, at + TILE)
        result = jnp.dot(rows[...], held[:, span], preferred_element_type=F32)
        own[:, span] = result[:half]
        par[:, span] = result[half:].astype(BF16)


def away_products(values, held):
    tokens, features = values.shape
    width = held.shape[1]
    outs = (array((tokens // 2, width), F32), array((tokens // 2, width), BF16))
    return call(away_kernel, outs, [VMEM, VMEM], (VMEM,) * 2, [pltpu.VMEM((tokens, features), BF16)])(values, held)


def sort_kernel(near, away, out):
    part = near.shape[0] // 4
    for n, values in enumerate((near, away)):
        for q in range(2):
            for z in range(2):
                to = (4 * z + 2 * n + q) * part
                out[to : to + part, :] = values[(2 * q + z) * part : (2 * q + z + 1) * part, :]


def sort_rows(near, away):
    tokens, features = near.shape
    return call(sort_kernel, array((2 * tokens, features), BF16), [VMEM, VMEM], VMEM)(near, away)


def gradient_kernel(start, size, near, near_sent, away, away_sent, upstream, out):
    half = near.shape[0]
    hidden = near.shape[1] // 2
    spans = slice(start, start + size), slice(hidden + start, hidden + start + size)
    for n, (kept, sent) in enumerate(((near, near_sent), (away, away_sent))):
        rows = slice(n * half, (n + 1) * half)
        stream = upstream[rows, spans[0]].astype(F32)
        gate, up = (kept[:, at] + sent[:, at].astype(F32) for at in spans)
        sigmoid = jax.nn.sigmoid(gate)
        out[rows, :size] = (stream * up * sigmoid * (1.0 + gate * (1.0 - sigmoid))).astype(BF16)
        out[rows, size:] = (stream * gate * sigmoid).astype(BF16)


def gradient(start, size, near, near_sent, away, away_sent, upstream):
    return call(
        functools.partial(gradient_kernel, start, size),
        array((upstream.shape[0], 2 * size), BF16),
        [VMEM] * 5,
        VMEM,
    )(near, near_sent, away, away_sent, upstream)


def backward_kernel(chunks, *refs):
    parts, (held, out, grads) = refs[: len(chunks)], refs[len(chunks) :]
    hidden = held.shape[1] // 2
    start = 0
    for part, size in zip(parts, chunks):
        grads[:, start : start + size] = part[:, :size]
        grads[:, hidden + start : hidden + start + size] = part[:, size:]
        start += size
    for k in range(8):
        span = slice(256 * k, 256 * (k + 1))
        out[:, span] = lax.dot_general(
            grads[...], held[span], (((1,), (1,)), ((), ())), preferred_element_type=F32
        ).astype(BF16)


def backward(parts, held, chunks):
    group = parts[0].shape[0]
    features, width = held.shape
    return call(
        functools.partial(backward_kernel, chunks),
        array((group, features), BF16),
        [VMEM] * (len(parts) + 1),
        VMEM,
        [pltpu.VMEM((group, width), BF16)],
    )(*parts, held)


def finish_kernel(chunks, scale, *refs):
    sums, lasts, (gate, up) = refs[: len(chunks)], refs[len(chunks) : 2 * len(chunks)], refs[2 * len(chunks) :]
    start = 0
    for size, total, last in zip(chunks, sums, lasts):
        gate[:, start : start + size] = (total[:, :size] + last[:, :size].astype(F32)) * scale
        up[:, start : start + size] = (total[:, size:] + last[:, size:].astype(F32)) * scale
        start += size


def finish(sums, lasts, chunks, scale):
    out = array((sums[0].shape[0], sum(chunks)), F32)
    return call(
        functools.partial(finish_kernel, chunks, scale), (out, out), [VMEM] * (2 * len(chunks)), (VMEM, VMEM)
    )(*sums, *lasts)


def add(*values):
    total = values[0].astype(F32)
    for value in values[1:]:
        total = total + value.astype(F32)
    return total


def local(saved_codes, saved_scales, gate_weight, up_weight, hidden_grad):
    rows = saved_codes.shape[0]
    group = hidden_grad.shape[0]

    row = np.arange(8 * rows)
    taken = (row // rows % 4 * 2 + row // (4 * rows)) * rows + row % rows
    by_group = np.equal(taken[:, None], row[None, :])

    shard = join(gate_weight, up_weight)
    from_a = send(shard, Y_A)
    from_b = send(shard, Y_B)

    saved_codes, saved_scales, _ = fence(saved_codes, saved_scales, shard)
    kept, given = dequantize(saved_codes, saved_scales)
    pair = jnp.concatenate([kept, send(given, TO_ZL)], axis=0)
    (pair,) = fence(pair)
    two = jnp.concatenate([pair, send(pair, ZH_A)], axis=0)
    (two,) = fence(two)
    four = jnp.concatenate([two, send(two, ZH_B)], axis=0)
    slab = jnp.dot(by_group.astype(BF16), four, preferred_element_type=F32).astype(BF16)
    slab, from_a, from_b = fence(slab, from_a, from_b)
    from_ab = send(from_a, Y_B)
    half = 4 * rows
    first = send(slab[:half], X_A)
    second = send(slab[half:], X_A)
    *mine, _ = fence(shard, from_a, from_b, first)
    theirs = [send(piece, TO_CORE) for piece in mine]
    near = jnp.concatenate([slab, first, second], axis=0)
    (near,) = fence(near)
    half = 8 * rows
    first = send(near[:half], X_B)
    second, *theirs = fence(near[half:], *theirs)
    second = send(second, X_B)
    from_ab, _ = fence(from_ab, first)
    weights = mine + [from_ab] + theirs + [send(from_ab, TO_CORE)]
    upstream = arrange(hidden_grad, rows)

    held, near_own, near_par = near_products(near, weights)
    near_sent = send(near_par, TO_ZL)
    second, _ = fence(second, near_own)
    away = jnp.concatenate([first, second], axis=0)
    (away,) = fence(away)
    away_own, away_par = away_products(away, held)
    away_sent = send(away_par, TO_ZL)
    inputs = sort_rows(near, away)
    near_sent, inputs, away_own = fence(near_sent, inputs, away_own)

    starts = list(itertools.accumulate((0,) + CHUNKS))
    grads = [
        gradient(start, size, near_own, near_sent, away_own, away_sent, upstream)
        for start, size in zip(starts, CHUNKS)
    ]
    others = [send(grads[0], TO_ZL)]
    own_back = backward(grads, held, CHUNKS)
    grads[1], own_back = fence(grads[1], own_back)
    others.append(send(grads[1], TO_ZL))
    half = group // 2
    own_sent = send(own_back[half:], X_B)
    others[0], own_sent = fence(others[0], own_sent)

    stages = []
    for n in range(len(CHUNKS)):
        grad = jnp.concatenate([grads[n], others[n]], axis=0)
        if n == 1:
            back = backward(others, held, CHUNKS)
            back, grad = fence(back, grad)
            back_sent = send(back[half:], X_B)

        def product(first, last, grad=grad):
            return lax.dot_general(
                inputs[:, first:last], grad, (((0,), (0,)), ((), ())), preferred_element_type=F32
            )

        shown = send(product(1024, 2048).astype(BF16), TO_CORE)
        passed = add(product(512, 1024), shown[512:]).astype(BF16)
        if n == 0:
            passed, *others = fence(passed, *others)
        else:
            back_sent, passed = fence(back_sent, passed)
        stages.append((product, shown, send(passed, Y_B)))

    def second_stage(n):
        product, shown, from_b = stages[n]
        return add(product(256, 512), shown[256:512], from_b[256:]).astype(BF16)

    own_back = add(own_back[:half], own_sent)
    back = add(back[:half], back_sent)
    half = half // 2
    given = jnp.concatenate([own_back[half:], back[half:]], axis=0).astype(BF16)
    kept = jnp.concatenate([own_back[:half], back[:half]], axis=0)
    arrived = send(given, X_A)
    passed = [second_stage(0)]
    arrived, passed[0] = fence(arrived, passed[0])
    four = jnp.dot(
        by_group.T.astype(np.float32),
        add(kept, arrived),
        preferred_element_type=F32,
        precision=lax.Precision.HIGHEST,
    )
    half = 4 * rows
    arrived = send(four[half:].astype(BF16), ZH_B)
    passed.append(second_stage(1))
    arrived, passed[1] = fence(arrived, passed[1])
    four = add(four[:half], arrived)
    half = half // 2
    pair = add(four[:half], send(four[half:].astype(BF16), ZH_A)).astype(BF16)
    input_grad = restore(pair[:rows], send(pair[rows:], TO_ZL))

    lasts = [send(value, Y_A) for value in passed]
    sums = [add(product(0, 256), shown[:256], from_b[:256]) for product, shown, from_b in stages]
    gate_grad, up_grad = finish(sums, lasts, CHUNKS, 1.0 / group)
    return input_grad, gate_grad, up_grad


def solution(mesh):
    placed = (P(BOTH, None), P(BOTH, None), P("dp", "tensor"), P("dp", "tensor"), P("dp", "tensor"))
    return jax.shard_map(
        local,
        mesh=mesh,
        in_specs=placed,
        out_specs=(P(BOTH, None), P("dp", "tensor"), P("dp", "tensor")),
        check_vma=False,
    )
```

time: 345 us -> 154 us (0.45)
  blocking collectives: 116 us -> 0 us
  waiting for transfers between devices: 162 us -> 85.5 us
  starting transfers between devices: 11.4 us -> 42.8 us
  matrix products: 29.1 us -> 6.72 us
  Pallas kernels: 0 us -> 14.4 us
  between operations: 14.5 us -> 1.08 us
  local copies, waits for them, and re-layouts: 8.37 us -> 0.31 us
    all_gather x3 -> x0, waiting for transfers between devices: 111 us -> none  [the longest x1 47.1 us: local(): lax.all_gather(up_weight, 'dp', axis=0, tiled=True)]
    ppermute x0 -> x30, waiting for transfers between devices: none -> 85.5 us  [send(): return lax.ppermute(value, BOTH, pairs)]
    unnamed x1 -> x0, blocking collectives: 73.7 us -> none
    reduce_scatter x1 -> x0, waiting for transfers between devices: 45.1 us -> none  [local(): lax.psum_scatter((lax.dot_general(columns, grad_pair, (((0,), (0,)), ((),...]
    ppermute x0 -> x30, starting transfers between devices: none -> 42.8 us  [send(): return lax.ppermute(value, BOTH, pairs)]
    all_gather x1 -> x0, blocking collectives: 42.4 us -> none  [local(): lax.all_gather(saved_scales, 'tensor', axis=0, tiled=True)]
    dot_general x5 -> x11, matrix products: 29.1 us -> 6.72 us  [the longest x8 5.46 us: product(): lax.dot_general(inputs[:, first:last], grad, (((0,), (0,)), ((), ())), pr...]
    pallas_call x0 -> x12, Pallas kernels: none -> 14.4 us  [the longest x2 5.05 us: backward(): call(functools.partial(backward_kernel, chunks), array((group, features),...]
  transfers between devices with their start and end apart: 8 -> 30, of which waited for: 5 -> 23; matrix products, arithmetic and copies ran while one was open for 29% -> 3% of each run, Pallas kernels for 0% -> 4%
where the time goes in v1:
time: 154 us; the launch traced here: 151 us
  waiting for transfers between devices  85.5 us (56%)
  starting transfers between devices  42.8 us (28%)
  Pallas kernels  14.4 us (9%)
  matrix products  6.72 us (4%)
    ppermute x30, waiting for transfers between devices, send(): return lax.ppermute(value, BOTH, pairs)  85.5 us
    ppermute x30, starting transfers between devices, send(): return lax.ppermute(value, BOTH, pairs)  42.8 us
    dot_general x8, matrix products, product(): lax.dot_general(inputs[:, first:last], grad, (((0,), (0,)), ((), ())), pr...  5.46 us
    pallas_call x2, Pallas kernels, backward(): call(functools.partial(backward_kernel, chunks), array((group, features),...  5.05 us
    pallas_call x1, Pallas kernels, near_products(): call(near_kernel, outs, [VMEM] + [ANY] * 8, (VMEM,) * 3, scratch)  3.5 us
  transfers between devices with their start and end apart: 30, of which 23 were waited for; matrix products, arithmetic and copies ran while one was open for 3% of the time, Pallas kernels for 4%

profile of v1, /device:TPU:64, one launch (start us, length us, event | category | flops | bytes accessed | tf_op | source)
XLA Modules:
  0.0 151.3 jit_solution(13740762671505465058)
XLA Ops:
  0.7 1.2 shard_map.103.refs_0_
  2.1 2.0 %collective-permute-start = (bf16[12,2048]{1,0:T(8,128)(2,1)S(1)}, bf16[12,2048]{1,0:T(8,128)(2,1)S(1)}, u32[]{:S(2)}, u32[]{:S(2)}) collective-permute-start(bf16[12,2048]{1,0:T(8,128)(2,1)S(1)} %get-tuple-element.47), channel_id=1, source_target_pairs={{0,128},{1,129},{2,130},{3,131},{4,132},{5,133},{6,134},{7,135},{8... | collective-permute-start | bytes 147464 | tf_op jit(solution)/shard_map/ppermute | solution.py:43
  4.1 2.3 %collective-permute-done = bf16[12,2048]{1,0:T(8,128)(2,1)S(1)} collective-permute-done((bf16[12,2048]{1,0:T(8,128)(2,1)S(1)}, bf16[12,2048]{1,0:T(8,128)(2,1)S(1)}, u32[]{:S(2)}, u32[]{:S(2)}) %collective-permute-start) | collective-permute-done | bytes 49184 | tf_op jit(solution)/shard_map/ppermute | solution.py:43
  6.5 1.5 collective-permute-start.1
  8.2 2.2 %collective-permute-start.4 = (bf16[256,1792]{1,0:T(8,128)(2,1)S(1)}, bf16[256,1792]{1,0:T(8,128)(2,1)S(1)}, u32[]{:S(2)}, u32[]{:S(2)}) collective-permute-start(bf16[256,1792]{1,0:T(8,128)(2,1)S(1)} %shard_map.103.refs_0_), channel_id=1, source_target_pairs={{0,96},{1,97},{2,98},{3,99},{4,100},{5,101},{6,102},{7,103},{8,104... | collective-permute-start | bytes 2752520 | tf_op jit(solution)/shard_map/ppermute | solution.py:43
  10.4 2.3 %collective-permute-done.1 = bf16[24,2048]{1,0:T(8,128)(2,1)S(1)} collective-permute-done((bf16[24,2048]{1,0:T(8,128)(2,1)S(1)}, bf16[24,2048]{1,0:T(8,128)(2,1)S(1)}, u32[]{:S(2)}, u32[]{:S(2)}) %collective-permute-start.1) | collective-permute-done | bytes 98336 | tf_op jit(solution)/shard_map/ppermute | solution.py:43
  12.7 5.0 %collective-permute-start.2 = (bf16[48,2048]{1,0:T(8,128)(2,1)S(1)}, bf16[48,2048]{1,0:T(8,128)(2,1)S(1)}, u32[]{:S(2)}, u32[]{:S(2)}) collective-permute-start(bf16[48,2048]{1,0:T(8,128)(2,1)S(1)} %pad_maximum_fusion.5), channel_id=1, source_target_pairs={{0,3},{1,2},{2,1},{3,0},{4,7},{5,6},{6,5},{7,4},{8,11},{9,10},{10,... | collective-permute-start | bytes 589832 | tf_op jit(solution)/shard_map/ppermute | solution.py:43
  17.7 5.8 %collective-permute-done.2 = bf16[48,2048]{1,0:T(8,128)(2,1)S(1)} collective-permute-done((bf16[48,2048]{1,0:T(8,128)(2,1)S(1)}, bf16[48,2048]{1,0:T(8,128)(2,1)S(1)}, u32[]{:S(2)}, u32[]{:S(2)}) %collective-permute-start.2) | collective-permute-done | bytes 196640 | tf_op jit(solution)/shard_map/ppermute | solution.py:43
  23.9 3.9 %collective-permute-done.3.refs_1_ = bf16[256,1792]{1,0:T(8,128)(2,1)S(1)} collective-permute-done((bf16[256,1792]{1,0:T(8,128)(2,1)S(1)}, bf16[256,1792]{1,0:T(8,128)(2,1)S(1)}, u32[]{:S(2)}, u32[]{:S(2)}) %collective-permute-start.3) | collective-permute-done | bytes 917536 | tf_op jit(solution)/shard_map/ppermute | solution.py:43
  27.8 4.5 %collective-permute-done.4.refs_2_ = bf16[256,1792]{1,0:T(8,128)(2,1)S(1)} collective-permute-done((bf16[256,1792]{1,0:T(8,128)(2,1)S(1)}, bf16[256,1792]{1,0:T(8,128)(2,1)S(1)}, u32[]{:S(2)}, u32[]{:S(2)}) %collective-permute-start.4) | collective-permute-done | bytes 917536 | tf_op jit(solution)/shard_map/ppermute | solution.py:43
  32.4 1.6 %collective-permute-start.5 = (bf16[48,2048]{1,0:T(8,128)(2,1)S(1)}, bf16[48,2048]{1,0:T(8,128)(2,1)S(1)}, u32[]{:S(2)}, u32[]{:S(2)}) collective-permute-start(bf16[48,2048]{1,0:T(8,128)(2,1)S(1)} %get-tuple-element.87), channel_id=1, source_target_pairs={{0,4},{1,5},{2,6},{3,7},{4,0},{5,1},{6,2},{7,3},{8,12},{9,13},{10,... | collective-permute-start | bytes 589832 | tf_op jit(solution)/shard_map/ppermute | solution.py:43
  34.5 1.4 collective-permute-start.7
  35.9 2.2 %collective-permute-done.5 = bf16[48,2048]{1,0:T(8,128)(2,1)S(1)} collective-permute-done((bf16[48,2048]{1,0:T(8,128)(2,1)S(1)}, bf16[48,2048]{1,0:T(8,128)(2,1)S(1)}, u32[]{:S(2)}, u32[]{:S(2)}) %collective-permute-start.5) | collective-permute-done | bytes 196640 | tf_op jit(solution)/shard_map/ppermute | solution.py:43
  38.1 2.1 %collective-permute-done.6 = bf16[48,2048]{1,0:T(8,128)(2,1)S(1)} collective-permute-done((bf16[48,2048]{1,0:T(8,128)(2,1)S(1)}, bf16[48,2048]{1,0:T(8,128)(2,1)S(1)}, u32[]{:S(2)}, u32[]{:S(2)}) %collective-permute-start.6) | collective-permute-done | bytes 196640 | tf_op jit(solution)/shard_map/ppermute | solution.py:43
  40.4 2.8 %collective-permute-start.8 = (bf16[96,2048]{1,0:T(8,128)(2,1)S(1)}, bf16[96,2048]{1,0:T(8,128)(2,1)S(1)}, u32[]{:S(2)}, u32[]{:S(2)}) collective-permute-start(bf16[96,2048]{1,0:T(8,128)(2,1)S(1)} %get-tuple-element.86), channel_id=1, source_target_pairs={{0,12},{1,13},{2,14},{3,15},{4,8},{5,9},{6,10},{7,11},{8,4},{9,5},... | collective-permute-start | bytes 1179656 | tf_op jit(solution)/shard_map/ppermute | solution.py:43
  43.7 5.7 %collective-permute-done.8 = bf16[96,2048]{1,0:T(8,128)(2,1)S(1)} collective-permute-done((bf16[96,2048]{1,0:T(8,128)(2,1)S(1)}, bf16[96,2048]{1,0:T(8,128)(2,1)S(1)}, u32[]{:S(2)}, u32[]{:S(2)}) %collective-permute-start.8) | collective-permute-done | bytes 393248 | tf_op jit(solution)/shard_map/ppermute | solution.py:43
  49.5 2.8 %collective-permute-start.14 = (bf16[96,2048]{1,0:T(8,128)(2,1)S(1)}, bf16[96,2048]{1,0:T(8,128)(2,1)S(1)}, u32[]{:S(2)}, u32[]{:S(2)}) collective-permute-start(bf16[96,2048]{1,0:T(8,128)(2,1)S(1)} %get-tuple-element.60), channel_id=1, source_target_pairs={{0,12},{1,13},{2,14},{3,15},{4,8},{5,9},{6,10},{7,11},{8,4},{9,5},... | collective-permute-start | bytes 1179656 | tf_op jit(solution)/shard_map/ppermute | solution.py:43
  52.3 3.5 %shard_map.105 = (bf16[2048,1792]{1,0:T(8,128)(2,1)S(1)}, f32[96,1792]{1,0:T(8,128)S(1)}, bf16[96,1792]{1,0:T(8,128)(2,1)S(1)}) custom-call(bf16[192,2048]{1,0:T(8,128)(2,1)S(1)} %pad_maximum_fusion.values.near, bf16[256,1792]{1,0:T(8,128)(2,1)S(1)} %shard_map.103.refs_0_, bf16[256,1792]{1,0:T(8,128)(2,1)S(1)} %collective-permute-done.3.refs_1_, ...), custom_call_target="tpu_custom_call" | custom-call | tf_op jit(solution)/shard_map/pallas_call | solution.py:198
  55.8 2.7 %collective-permute-done.14 = bf16[96,2048]{1,0:T(8,128)(2,1)S(1)} collective-permute-done((bf16[96,2048]{1,0:T(8,128)(2,1)S(1)}, bf16[96,2048]{1,0:T(8,128)(2,1)S(1)}, u32[]{:S(2)}, u32[]{:S(2)}) %collective-permute-start.14) | collective-permute-done | bytes 393248 | tf_op jit(solution)/shard_map/ppermute | solution.py:43
  58.6 1.7 %collective-permute-start.13 = (bf16[96,1792]{1,0:T(8,128)(2,1)S(1)}, bf16[96,1792]{1,0:T(8,128)(2,1)S(1)}, u32[]{:S(2)}, u32[]{:S(2)}) collective-permute-start(bf16[96,1792]{1,0:T(8,128)(2,1)S(1)} %get-tuple-element.59), channel_id=1, source_target_pairs={{0,128},{1,129},{2,130},{3,131},{4,132},{5,133},{6,134},{7,135},{8... | collective-permute-start | bytes 1032200 | tf_op jit(solution)/shard_map/ppermute | solution.py:43
  60.3 1.6 %shard_map.107 = (f32[96,1792]{1,0:T(8,128)S(1)}, bf16[96,1792]{1,0:T(8,128)(2,1)S(1)}) custom-call(bf16[192,2048]{1,0:T(8,128)(2,1)S(1)} %pad_maximum_fusion.1.away.values, bf16[2048,1792]{1,0:T(8,128)(2,1)S(1)} %get-tuple-element.62.held.refs_2_), custom_call_target="tpu_custom_call" | custom-call | tf_op jit(solution)/shard_map/pallas_call | solution.py:215
  63.0 6.7 %collective-permute-done.13.near_sent = bf16[96,1792]{1,0:T(8,128)(2,1)S(1)} collective-permute-done((bf16[96,1792]{1,0:T(8,128)(2,1)S(1)}, bf16[96,1792]{1,0:T(8,128)(2,1)S(1)}, u32[]{:S(2)}, u32[]{:S(2)}) %collective-permute-start.13) | collective-permute-done | bytes 344096 | tf_op jit(solution)/shard_map/ppermute | solution.py:43
  69.7 4.8 %collective-permute-done.15.away_sent = bf16[96,1792]{1,0:T(8,128)(2,1)S(1)} collective-permute-done((bf16[96,1792]{1,0:T(8,128)(2,1)S(1)}, bf16[96,1792]{1,0:T(8,128)(2,1)S(1)}, u32[]{:S(2)}, u32[]{:S(2)}) %collective-permute-start.15) | collective-permute-done | bytes 344096 | tf_op jit(solution)/shard_map/ppermute | solution.py:43
  74.9 2.5 %shard_map.111 = bf16[192,2048]{1,0:T(8,128)(2,1)S(1)} custom-call(bf16[192,1024]{1,0:T(8,128)(2,1)S(1)} %shard_map.110.refs_0_, bf16[192,768]{1,0:T(8,128)(2,1)S(1)} %shard_map.109.refs_1_, bf16[2048,1792]{1,0:T(8,128)(2,1)S(1)} %get-tuple-element.62.held.refs_2_), custom_call_target="tpu_custom_call" | custom-call | tf_op jit(solution)/shard_map/pallas_call | solution.py:272
  77.4 2.9 %collective-permute-start.17 = (bf16[96,2048]{1,0:T(8,128)(2,1)S(1)}, bf16[96,2048]{1,0:T(8,128)(2,1)S(1)}, u32[]{:S(2)}, u32[]{:S(2)}) collective-permute-start(bf16[96,2048]{1,0:T(8,128)(2,1)S(1)} %slice.109), channel_id=1, source_target_pairs={{0,12},{1,13},{2,14},{3,15},{4,8},{5,9},{6,10},{7,11},{8,4},{9,5},... | collective-permute-start | bytes 1179656 | tf_op jit(solution)/shard_map/ppermute | solution.py:43
  80.3 1.6 %collective-permute-start.16 = (bf16[192,1024]{1,0:T(8,128)(2,1)S(1)}, bf16[192,1024]{1,0:T(8,128)(2,1)S(1)}, u32[]{:S(2)}, u32[]{:S(2)}) collective-permute-start(bf16[192,1024]{1,0:T(8,128)(2,1)S(1)} %shard_map.110.refs_0_), channel_id=1, source_target_pairs={{0,128},{1,129},{2,130},{3,131},{4,132},{5,133},{6,134},{7,135},{8... | collective-permute-start | bytes 1179656 | tf_op jit(solution)/shard_map/ppermute | solution.py:43
  81.9 4.6 %collective-permute-done.17 = bf16[96,2048]{1,0:T(8,128)(2,1)S(1)} collective-permute-done((bf16[96,2048]{1,0:T(8,128)(2,1)S(1)}, bf16[96,2048]{1,0:T(8,128)(2,1)S(1)}, u32[]{:S(2)}, u32[]{:S(2)}) %collective-permute-start.17) | collective-permute-done | bytes 393248 | tf_op jit(solution)/shard_map/ppermute | solution.py:43
  86.5 1.6 %collective-permute-done.16.refs_0_ = bf16[192,1024]{1,0:T(8,128)(2,1)S(1)} collective-permute-done((bf16[192,1024]{1,0:T(8,128)(2,1)S(1)}, bf16[192,1024]{1,0:T(8,128)(2,1)S(1)}, u32[]{:S(2)}, u32[]{:S(2)}) %collective-permute-start.16) | collective-permute-done | bytes 393248 | tf_op jit(solution)/shard_map/ppermute | solution.py:43
  88.2 1.3 convolution_convert_fusion
  89.6 1.7 %collective-permute-start.19 = (bf16[192,768]{1,0:T(8,128)(2,1)S(1)}, bf16[192,768]{1,0:T(8,128)(2,1)S(1)}, u32[]{:S(2)}, u32[]{:S(2)}) collective-permute-start(bf16[192,768]{1,0:T(8,128)(2,1)S(1)} %shard_map.109.refs_1_), channel_id=1, source_target_pairs={{0,128},{1,129},{2,130},{3,131},{4,132},{5,133},{6,134},{7,135},{8... | collective-permute-start | bytes 884744 | tf_op jit(solution)/shard_map/ppermute | solution.py:43
  91.3 2.4 %collective-permute-done.18 = bf16[1024,1024]{1,0:T(8,128)(2,1)S(1)} collective-permute-done((bf16[1024,1024]{1,0:T(8,128)(2,1)S(1)}, bf16[1024,1024]{1,0:T(8,128)(2,1)S(1)}, u32[]{:S(2)}, u32[]{:S(2)}) %collective-permute-start.18) | collective-permute-done | bytes 2097184 | tf_op jit(solution)/shard_map/ppermute | solution.py:43
  94.5 4.5 %collective-permute-done.19.refs_1_ = bf16[192,768]{1,0:T(8,128)(2,1)S(1)} collective-permute-done((bf16[192,768]{1,0:T(8,128)(2,1)S(1)}, bf16[192,768]{1,0:T(8,128)(2,1)S(1)}, u32[]{:S(2)}, u32[]{:S(2)}) %collective-permute-start.19) | collective-permute-done | bytes 294944 | tf_op jit(solution)/shard_map/ppermute | solution.py:43
  99.0 2.5 %shard_map.112 = bf16[192,2048]{1,0:T(8,128)(2,1)S(1)} custom-call(bf16[192,1024]{1,0:T(8,128)(2,1)S(1)} %collective-permute-done.16.refs_0_, bf16[192,768]{1,0:T(8,128)(2,1)S(1)} %collective-permute-done.19.refs_1_, bf16[2048,1792]{1,0:T(8,128)(2,1)S(1)} %get-tuple-element.62.held.refs_2_), custom_call_target="tpu_custom_call" | custom-call | tf_op jit(solution)/shard_map/pallas_call | solution.py:272
  101.6 1.0 convolution_convert_fusion.1
  102.8 2.2 %collective-permute-start.20 = (bf16[96,2048]{1,0:T(8,128)(2,1)S(1)}, bf16[96,2048]{1,0:T(8,128)(2,1)S(1)}, u32[]{:S(2)}, u32[]{:S(2)}) collective-permute-start(bf16[96,2048]{1,0:T(8,128)(2,1)S(1)} %slice.115), channel_id=1, source_target_pairs={{0,12},{1,13},{2,14},{3,15},{4,8},{5,9},{6,10},{7,11},{8,4},{9,5},... | collective-permute-start | bytes 1179656 | tf_op jit(solution)/shard_map/ppermute | solution.py:43
  105.1 2.9 %collective-permute-start.23 = (bf16[512,1024]{1,0:T(8,128)(2,1)S(1)}, bf16[512,1024]{1,0:T(8,128)(2,1)S(1)}, u32[]{:S(2)}, u32[]{:S(2)}) collective-permute-start(bf16[512,1024]{1,0:T(8,128)(2,1)S(1)} %add_convert_fusion), channel_id=1, source_target_pairs={{0,96},{1,97},{2,98},{3,99},{4,100},{5,101},{6,102},{7,103},{8,104... | collective-permute-start | bytes 3145736 | tf_op jit(solution)/shard_map/ppermute | solution.py:43
  108.6 3.2 %collective-permute-done.20 = bf16[96,2048]{1,0:T(8,128)(2,1)S(1)} collective-permute-done((bf16[96,2048]{1,0:T(8,128)(2,1)S(1)}, bf16[96,2048]{1,0:T(8,128)(2,1)S(1)}, u32[]{:S(2)}, u32[]{:S(2)}) %collective-permute-start.20) | collective-permute-done | bytes 393248 | tf_op jit(solution)/shard_map/ppermute | solution.py:43
  111.8 2.8 %collective-permute-start.25 = (bf16[512,768]{1,0:T(8,128)(2,1)S(1)}, bf16[512,768]{1,0:T(8,128)(2,1)S(1)}, u32[]{:S(2)}, u32[]{:S(2)}) collective-permute-start(bf16[512,768]{1,0:T(8,128)(2,1)S(1)} %add_convert_fusion.1), channel_id=1, source_target_pairs={{0,96},{1,97},{2,98},{3,99},{4,100},{5,101},{6,102},{7,103},{8,104... | collective-permute-start | bytes 2359304 | tf_op jit(solution)/shard_map/ppermute | solution.py:43
  115.1 6.0 %collective-permute-done.23 = bf16[512,1024]{1,0:T(8,128)(2,1)S(1)} collective-permute-done((bf16[512,1024]{1,0:T(8,128)(2,1)S(1)}, bf16[512,1024]{1,0:T(8,128)(2,1)S(1)}, u32[]{:S(2)}, u32[]{:S(2)}) %collective-permute-start.23) | collective-permute-done | bytes 1048608 | tf_op jit(solution)/shard_map/ppermute | solution.py:43
  121.7 1.2 collective-permute-done.22
  123.7 2.6 %collective-permute-start.24 = (bf16[48,2048]{1,0:T(8,128)(2,1)S(1)}, bf16[48,2048]{1,0:T(8,128)(2,1)S(1)}, u32[]{:S(2)}, u32[]{:S(2)}) collective-permute-start(bf16[48,2048]{1,0:T(8,128)(2,1)S(1)} %slice.196), channel_id=1, source_target_pairs={{0,3},{1,2},{2,1},{3,0},{4,7},{5,6},{6,5},{7,4},{8,11},{9,10},{10,... | collective-permute-start | bytes 589832 | tf_op jit(solution)/shard_map/ppermute | solution.py:43
  126.3 3.3 %collective-permute-done.25 = bf16[512,768]{1,0:T(8,128)(2,1)S(1)} collective-permute-done((bf16[512,768]{1,0:T(8,128)(2,1)S(1)}, bf16[512,768]{1,0:T(8,128)(2,1)S(1)}, u32[]{:S(2)}, u32[]{:S(2)}) %collective-permute-start.25) | collective-permute-done | bytes 786464 | tf_op jit(solution)/shard_map/ppermute | solution.py:43
  130.0 5.8 %collective-permute-done.24 = bf16[48,2048]{1,0:T(8,128)(2,1)S(1)} collective-permute-done((bf16[48,2048]{1,0:T(8,128)(2,1)S(1)}, bf16[48,2048]{1,0:T(8,128)(2,1)S(1)}, u32[]{:S(2)}, u32[]{:S(2)}) %collective-permute-start.24) | collective-permute-done | bytes 196640 | tf_op jit(solution)/shard_map/ppermute | solution.py:43
  136.5 2.0 %collective-permute-start.29 = (bf16[256,768]{1,0:T(8,128)(2,1)S(1)}, bf16[256,768]{1,0:T(8,128)(2,1)S(1)}, u32[]{:S(2)}, u32[]{:S(2)}) collective-permute-start(bf16[256,768]{1,0:T(8,128)(2,1)S(1)} %fusion.7), channel_id=1, source_target_pairs={{0,32},{1,33},{2,34},{3,35},{4,36},{5,37},{6,38},{7,39},{8,40},{9,... | collective-permute-start | bytes 1179656 | tf_op jit(solution)/shard_map/ppermute | solution.py:43
  138.5 2.9 %collective-permute-done.26 = bf16[24,2048]{1,0:T(8,128)(2,1)S(1)} collective-permute-done((bf16[24,2048]{1,0:T(8,128)(2,1)S(1)}, bf16[24,2048]{1,0:T(8,128)(2,1)S(1)}, u32[]{:S(2)}, u32[]{:S(2)}) %collective-permute-start.26) | collective-permute-done | bytes 98336 | tf_op jit(solution)/shard_map/ppermute | solution.py:43
  142.3 3.5 %collective-permute-done.27.other = bf16[12,2048]{1,0:T(8,128)(2,1)S(1)} collective-permute-done((bf16[12,2048]{1,0:T(8,128)(2,1)S(1)}, bf16[12,2048]{1,0:T(8,128)(2,1)S(1)}, u32[]{:S(2)}, u32[]{:S(2)}) %collective-permute-start.27) | collective-permute-done | bytes 49184 | tf_op jit(solution)/shard_map/ppermute | solution.py:43
  146.5 3.4 %collective-permute-done.29.refs_3_ = bf16[256,768]{1,0:T(8,128)(2,1)S(1)} collective-permute-done((bf16[256,768]{1,0:T(8,128)(2,1)S(1)}, bf16[256,768]{1,0:T(8,128)(2,1)S(1)}, u32[]{:S(2)}, u32[]{:S(2)}) %collective-permute-start.29) | collective-permute-done | bytes 393248 | tf_op jit(solution)/shard_map/ppermute | solution.py:43
  149.9 1.4 shard_map.114
  (73 shorter events, 9.9 us)
Async XLA Ops:
  0.6 22.8 %copy-start.6 = (bf16[96,48]{1,0:T(8,128)(2,1)S(1)}, bf16[96,48]{1,0:T(8,128)(2,1)}, u32[]{:S(2)}) copy-start(bf16[96,48]{1,0:T(8,128)(2,1)} %constant.12) | copy-start | bytes 27652
  0.6 23.0 %copy-start.7 = (bf16[96,48]{1,0:T(8,128)(2,1)S(1)}, bf16[96,48]{1,0:T(8,128)(2,1)}, u32[]{:S(2)}) copy-start(bf16[96,48]{1,0:T(8,128)(2,1)} %constant.11) | copy-start | bytes 27652
  0.7 1.2 copy-start.1
  0.7 1.2 copy-start.3
  2.1 4.4 %collective-permute-start = (bf16[12,2048]{1,0:T(8,128)(2,1)S(1)}, bf16[12,2048]{1,0:T(8,128)(2,1)S(1)}, u32[]{:S(2)}, u32[]{:S(2)}) collective-permute-start(bf16[12,2048]{1,0:T(8,128)(2,1)S(1)} %get-tuple-element.47), channel_id=1, source_target_pairs={{0,128},{1,129},{2,130},{3,131},{4,132},{5,133},{6,134},{7,135},{8... | collective-permute-start | bytes 147464 | tf_op jit(solution)/shard_map/ppermute | solution.py:43
  6.5 6.2 %collective-permute-start.1 = (bf16[24,2048]{1,0:T(8,128)(2,1)S(1)}, bf16[24,2048]{1,0:T(8,128)(2,1)S(1)}, u32[]{:S(2)}, u32[]{:S(2)}) collective-permute-start(bf16[24,2048]{1,0:T(8,128)(2,1)S(1)} %pad_maximum_fusion.6), channel_id=1, source_target_pairs={{0,1},{1,0},{2,3},{3,2},{4,5},{5,4},{6,7},{7,6},{8,9},{9,8},{10,11... | collective-permute-start | bytes 294920 | tf_op jit(solution)/shard_map/ppermute | solution.py:43
  7.9 19.9 %collective-permute-start.3 = (bf16[256,1792]{1,0:T(8,128)(2,1)S(1)}, bf16[256,1792]{1,0:T(8,128)(2,1)S(1)}, u32[]{:S(2)}, u32[]{:S(2)}) collective-permute-start(bf16[256,1792]{1,0:T(8,128)(2,1)S(1)} %shard_map.103.refs_0_), channel_id=1, source_target_pairs={{0,32},{1,33},{2,34},{3,35},{4,36},{5,37},{6,38},{7,39},{8,40},{9,... | collective-permute-start | bytes 2752520 | tf_op jit(solution)/shard_map/ppermute | solution.py:43
  8.2 24.1 %collective-permute-start.4 = (bf16[256,1792]{1,0:T(8,128)(2,1)S(1)}, bf16[256,1792]{1,0:T(8,128)(2,1)S(1)}, u32[]{:S(2)}, u32[]{:S(2)}) collective-permute-start(bf16[256,1792]{1,0:T(8,128)(2,1)S(1)} %shard_map.103.refs_0_), channel_id=1, source_target_pairs={{0,96},{1,97},{2,98},{3,99},{4,100},{5,101},{6,102},{7,103},{8,104... | collective-permute-start | bytes 2752520 | tf_op jit(solution)/shard_map/ppermute | solution.py:43
  12.7 10.7 %collective-permute-start.2 = (bf16[48,2048]{1,0:T(8,128)(2,1)S(1)}, bf16[48,2048]{1,0:T(8,128)(2,1)S(1)}, u32[]{:S(2)}, u32[]{:S(2)}) collective-permute-start(bf16[48,2048]{1,0:T(8,128)(2,1)S(1)} %pad_maximum_fusion.5), channel_id=1, source_target_pairs={{0,3},{1,2},{2,1},{3,0},{4,7},{5,6},{6,5},{7,4},{8,11},{9,10},{10,... | collective-permute-start | bytes 589832 | tf_op jit(solution)/shard_map/ppermute | solution.py:43
  32.4 5.8 %collective-permute-start.5 = (bf16[48,2048]{1,0:T(8,128)(2,1)S(1)}, bf16[48,2048]{1,0:T(8,128)(2,1)S(1)}, u32[]{:S(2)}, u32[]{:S(2)}) collective-permute-start(bf16[48,2048]{1,0:T(8,128)(2,1)S(1)} %get-tuple-element.87), channel_id=1, source_target_pairs={{0,4},{1,5},{2,6},{3,7},{4,0},{5,1},{6,2},{7,3},{8,12},{9,13},{10,... | collective-permute-start | bytes 589832 | tf_op jit(solution)/shard_map/ppermute | solution.py:43
  34.0 6.3 %collective-permute-start.6 = (bf16[48,2048]{1,0:T(8,128)(2,1)S(1)}, bf16[48,2048]{1,0:T(8,128)(2,1)S(1)}, u32[]{:S(2)}, u32[]{:S(2)}) collective-permute-start(bf16[48,2048]{1,0:T(8,128)(2,1)S(1)} %get-tuple-element.88), channel_id=1, source_target_pairs={{0,4},{1,5},{2,6},{3,7},{4,0},{5,1},{6,2},{7,3},{8,12},{9,13},{10,... | collective-permute-start | bytes 589832 | tf_op jit(solution)/shard_map/ppermute | solution.py:43
  34.5 14.9 %collective-permute-start.7 = (bf16[256,1792]{1,0:T(8,128)(2,1)S(1)}, bf16[256,1792]{1,0:T(8,128)(2,1)S(1)}, u32[]{:S(2)}, u32[]{:S(2)}) collective-permute-start(bf16[256,1792]{1,0:T(8,128)(2,1)S(1)} %collective-permute-done.3.refs_1_), channel_id=1, source_target_pairs={{0,96},{1,97},{2,98},{3,99},{4,100},{5,101},{6,102},{7,103},{8,104... | collective-permute-start | bytes 2752520 | tf_op jit(solution)/shard_map/ppermute | solution.py:43
  40.4 9.1 %collective-permute-start.8 = (bf16[96,2048]{1,0:T(8,128)(2,1)S(1)}, bf16[96,2048]{1,0:T(8,128)(2,1)S(1)}, u32[]{:S(2)}, u32[]{:S(2)}) collective-permute-start(bf16[96,2048]{1,0:T(8,128)(2,1)S(1)} %get-tuple-element.86), channel_id=1, source_target_pairs={{0,12},{1,13},{2,14},{3,15},{4,8},{5,9},{6,10},{7,11},{8,4},{9,5},... | collective-permute-start | bytes 1179656 | tf_op jit(solution)/shard_map/ppermute | solution.py:43
  43.2 6.2 %collective-permute-start.10 = (bf16[256,1792]{1,0:T(8,128)(2,1)S(1)}, bf16[256,1792]{1,0:T(8,128)(2,1)S(1)}, u32[]{:S(2)}, u32[]{:S(2)}) collective-permute-start(bf16[256,1792]{1,0:T(8,128)(2,1)S(1)} %collective-permute-done.3.refs_1_), channel_id=1, source_target_pairs={{0,16},{1,17},{2,18},{3,19},{4,20},{5,21},{6,22},{7,23},{8,24},{9,... | collective-permute-start | bytes 2752520 | tf_op jit(solution)/shard_map/ppermute | solution.py:43
  43.2 6.2 %collective-permute-start.11 = (bf16[256,1792]{1,0:T(8,128)(2,1)S(1)}, bf16[256,1792]{1,0:T(8,128)(2,1)S(1)}, u32[]{:S(2)}, u32[]{:S(2)}) collective-permute-start(bf16[256,1792]{1,0:T(8,128)(2,1)S(1)} %collective-permute-done.4.refs_2_), channel_id=1, source_target_pairs={{0,16},{1,17},{2,18},{3,19},{4,20},{5,21},{6,22},{7,23},{8,24},{9,... | collective-permute-start | bytes 2752520 | tf_op jit(solution)/shard_map/ppermute | solution.py:43
  43.7 5.7 %collective-permute-start.9 = (bf16[256,1792]{1,0:T(8,128)(2,1)S(1)}, bf16[256,1792]{1,0:T(8,128)(2,1)S(1)}, u32[]{:S(2)}, u32[]{:S(2)}) collective-permute-start(bf16[256,1792]{1,0:T(8,128)(2,1)S(1)} %shard_map.103.refs_0_), channel_id=1, source_target_pairs={{0,16},{1,17},{2,18},{3,19},{4,20},{5,21},{6,22},{7,23},{8,24},{9,... | collective-permute-start | bytes 2752520 | tf_op jit(solution)/shard_map/ppermute | solution.py:43
  49.4 2.9 %collective-permute-start.12 = (bf16[256,1792]{1,0:T(8,128)(2,1)S(1)}, bf16[256,1792]{1,0:T(8,128)(2,1)S(1)}, u32[]{:S(2)}, u32[]{:S(2)}) collective-permute-start(bf16[256,1792]{1,0:T(8,128)(2,1)S(1)} %collective-permute-done.7.refs_3_), channel_id=1, source_target_pairs={{0,16},{1,17},{2,18},{3,19},{4,20},{5,21},{6,22},{7,23},{8,24},{9,... | collective-permute-start | bytes 2752520 | tf_op jit(solution)/shard_map/ppermute | solution.py:43
  49.5 9.1 %collective-permute-start.14 = (bf16[96,2048]{1,0:T(8,128)(2,1)S(1)}, bf16[96,2048]{1,0:T(8,128)(2,1)S(1)}, u32[]{:S(2)}, u32[]{:S(2)}) collective-permute-start(bf16[96,2048]{1,0:T(8,128)(2,1)S(1)} %get-tuple-element.60), channel_id=1, source_target_pairs={{0,12},{1,13},{2,14},{3,15},{4,8},{5,9},{6,10},{7,11},{8,4},{9,5},... | collective-permute-start | bytes 1179656 | tf_op jit(solution)/shard_map/ppermute | solution.py:43
  58.6 11.1 %collective-permute-start.13 = (bf16[96,1792]{1,0:T(8,128)(2,1)S(1)}, bf16[96,1792]{1,0:T(8,128)(2,1)S(1)}, u32[]{:S(2)}, u32[]{:S(2)}) collective-permute-start(bf16[96,1792]{1,0:T(8,128)(2,1)S(1)} %get-tuple-element.59), channel_id=1, source_target_pairs={{0,128},{1,129},{2,130},{3,131},{4,132},{5,133},{6,134},{7,135},{8... | collective-permute-start | bytes 1032200 | tf_op jit(solution)/shard_map/ppermute | solution.py:43
  60.3 2.3 %copy-start = (bf16[192,896]{1,0:T(8,128)(2,1)S(1)}, bf16[192,896]{1,0:T(8,128)(2,1)}, u32[]{:S(2)}) copy-start(bf16[192,896]{1,0:T(8,128)(2,1)} %values.1) | copy-start | bytes 1032196
  60.3 2.3 %copy-start.2 = (s32[32,1,192]{2,1,0:T(1,128)S(1)}, s32[32,1,192]{2,1,0:T(1,128)}, u32[]{:S(2)}) copy-start(s32[32,1,192]{2,1,0:T(1,128)} %constant.7.clone.table) | copy-start | bytes 73732
  61.9 12.5 %collective-permute-start.15 = (bf16[96,1792]{1,0:T(8,128)(2,1)S(1)}, bf16[96,1792]{1,0:T(8,128)(2,1)S(1)}, u32[]{:S(2)}, u32[]{:S(2)}) collective-permute-start(bf16[96,1792]{1,0:T(8,128)(2,1)S(1)} %get-tuple-element.66), channel_id=1, source_target_pairs={{0,128},{1,129},{2,130},{3,131},{4,132},{5,133},{6,134},{7,135},{8... | collective-permute-start | bytes 1032200 | tf_op jit(solution)/shard_map/ppermute | solution.py:43
  77.4 9.1 %collective-permute-start.17 = (bf16[96,2048]{1,0:T(8,128)(2,1)S(1)}, bf16[96,2048]{1,0:T(8,128)(2,1)S(1)}, u32[]{:S(2)}, u32[]{:S(2)}) collective-permute-start(bf16[96,2048]{1,0:T(8,128)(2,1)S(1)} %slice.109), channel_id=1, source_target_pairs={{0,12},{1,13},{2,14},{3,15},{4,8},{5,9},{6,10},{7,11},{8,4},{9,5},... | collective-permute-start | bytes 1179656 | tf_op jit(solution)/shard_map/ppermute | solution.py:43
  80.3 7.9 %collective-permute-start.16 = (bf16[192,1024]{1,0:T(8,128)(2,1)S(1)}, bf16[192,1024]{1,0:T(8,128)(2,1)S(1)}, u32[]{:S(2)}, u32[]{:S(2)}) collective-permute-start(bf16[192,1024]{1,0:T(8,128)(2,1)S(1)} %shard_map.110.refs_0_), channel_id=1, source_target_pairs={{0,128},{1,129},{2,130},{3,131},{4,132},{5,133},{6,134},{7,135},{8... | collective-permute-start | bytes 1179656 | tf_op jit(solution)/shard_map/ppermute | solution.py:43
  89.5 4.2 %collective-permute-start.18 = (bf16[1024,1024]{1,0:T(8,128)(2,1)S(1)}, bf16[1024,1024]{1,0:T(8,128)(2,1)S(1)}, u32[]{:S(2)}, u32[]{:S(2)}) collective-permute-start(bf16[1024,1024]{1,0:T(8,128)(2,1)S(1)} %convolution_convert_fusion), channel_id=1, source_target_pairs={{0,16},{1,17},{2,18},{3,19},{4,20},{5,21},{6,22},{7,23},{8,24},{9,... | collective-permute-start | bytes 6291464 | tf_op jit(solution)/shard_map/ppermute | solution.py:43
  89.6 9.4 %collective-permute-start.19 = (bf16[192,768]{1,0:T(8,128)(2,1)S(1)}, bf16[192,768]{1,0:T(8,128)(2,1)S(1)}, u32[]{:S(2)}, u32[]{:S(2)}) collective-permute-start(bf16[192,768]{1,0:T(8,128)(2,1)S(1)} %shard_map.109.refs_1_), channel_id=1, source_target_pairs={{0,128},{1,129},{2,130},{3,131},{4,132},{5,133},{6,134},{7,135},{8... | collective-permute-start | bytes 884744 | tf_op jit(solution)/shard_map/ppermute | solution.py:43
  102.6 5.3 %collective-permute-start.21 = (bf16[1024,768]{1,0:T(8,128)(2,1)S(1)}, bf16[1024,768]{1,0:T(8,128)(2,1)S(1)}, u32[]{:S(2)}, u32[]{:S(2)}) collective-permute-start(bf16[1024,768]{1,0:T(8,128)(2,1)S(1)} %convolution_convert_fusion.1), channel_id=1, source_target_pairs={{0,16},{1,17},{2,18},{3,19},{4,20},{5,21},{6,22},{7,23},{8,24},{9,... | collective-permute-start | bytes 4718600 | tf_op jit(solution)/shard_map/ppermute | solution.py:43
  102.8 9.1 %collective-permute-start.20 = (bf16[96,2048]{1,0:T(8,128)(2,1)S(1)}, bf16[96,2048]{1,0:T(8,128)(2,1)S(1)}, u32[]{:S(2)}, u32[]{:S(2)}) collective-permute-start(bf16[96,2048]{1,0:T(8,128)(2,1)S(1)} %slice.115), channel_id=1, source_target_pairs={{0,12},{1,13},{2,14},{3,15},{4,8},{5,9},{6,10},{7,11},{8,4},{9,5},... | collective-permute-start | bytes 1179656 | tf_op jit(solution)/shard_map/ppermute | solution.py:43
  105.0 10.1 %copy-start.4 = (f32[96,2048]{1,0:T(8,128)}, f32[96,2048]{1,0:T(8,128)S(1)}, u32[]{:S(2)}) copy-start(f32[96,2048]{1,0:T(8,128)S(1)} %convert_add_fusion.1) | copy-start | bytes 2359300
  105.1 16.1 %collective-permute-start.23 = (bf16[512,1024]{1,0:T(8,128)(2,1)S(1)}, bf16[512,1024]{1,0:T(8,128)(2,1)S(1)}, u32[]{:S(2)}, u32[]{:S(2)}) collective-permute-start(bf16[512,1024]{1,0:T(8,128)(2,1)S(1)} %add_convert_fusion), channel_id=1, source_target_pairs={{0,96},{1,97},{2,98},{3,99},{4,100},{5,101},{6,102},{7,103},{8,104... | collective-permute-start | bytes 3145736 | tf_op jit(solution)/shard_map/ppermute | solution.py:43
  111.8 17.8 %collective-permute-start.25 = (bf16[512,768]{1,0:T(8,128)(2,1)S(1)}, bf16[512,768]{1,0:T(8,128)(2,1)S(1)}, u32[]{:S(2)}, u32[]{:S(2)}) collective-permute-start(bf16[512,768]{1,0:T(8,128)(2,1)S(1)} %add_convert_fusion.1), channel_id=1, source_target_pairs={{0,96},{1,97},{2,98},{3,99},{4,100},{5,101},{6,102},{7,103},{8,104... | collective-permute-start | bytes 2359304 | tf_op jit(solution)/shard_map/ppermute | solution.py:43
  114.8 8.1 %collective-permute-start.22 = (bf16[96,2048]{1,0:T(8,128)(2,1)S(1)}, bf16[96,2048]{1,0:T(8,128)(2,1)S(1)}, u32[]{:S(2)}, u32[]{:S(2)}) collective-permute-start(bf16[96,2048]{1,0:T(8,128)(2,1)S(1)} %pad_maximum_fusion.4), channel_id=1, source_target_pairs={{0,4},{1,5},{2,6},{3,7},{4,0},{5,1},{6,2},{7,3},{8,12},{9,13},{10,... | collective-permute-start | bytes 1179656 | tf_op jit(solution)/shard_map/ppermute | solution.py:43
  115.1 7.8 %slice-start = ((f32[96,2048]{1,0:T(8,128)}), f32[48,2048]{1,0:T(8,128)S(1)}, s32[]{:S(2)}) async-start(f32[96,2048]{1,0:T(8,128)} %copy-done.4), calls=%async_computation | async-start | bytes 786432 | tf_op jit(solution)/shard_map/slice | solution.py:393
  115.1 7.7 %copy-start.5 = (f32[96,96]{1,0:T(8,128)S(1)}, f32[96,96]{1,0:T(8,128)}, u32[]{:S(2)}) copy-start(f32[96,96]{1,0:T(8,128)} %constant.8.clone) | copy-start | bytes 110596
  123.7 12.1 %collective-permute-start.24 = (bf16[48,2048]{1,0:T(8,128)(2,1)S(1)}, bf16[48,2048]{1,0:T(8,128)(2,1)S(1)}, u32[]{:S(2)}, u32[]{:S(2)}) collective-permute-start(bf16[48,2048]{1,0:T(8,128)(2,1)S(1)} %slice.196), channel_id=1, source_target_pairs={{0,3},{1,2},{2,1},{3,0},{4,7},{5,6},{6,5},{7,4},{8,11},{9,10},{10,... | collective-permute-start | bytes 589832 | tf_op jit(solution)/shard_map/ppermute | solution.py:43
  135.8 5.6 %collective-permute-start.26 = (bf16[24,2048]{1,0:T(8,128)(2,1)S(1)}, bf16[24,2048]{1,0:T(8,128)(2,1)S(1)}, u32[]{:S(2)}, u32[]{:S(2)}) collective-permute-start(bf16[24,2048]{1,0:T(8,128)(2,1)S(1)} %slice.199), channel_id=1, source_target_pairs={{0,1},{1,0},{2,3},{3,2},{4,5},{5,4},{6,7},{7,6},{8,9},{9,8},{10,11... | collective-permute-start | bytes 294920 | tf_op jit(solution)/shard_map/ppermute | solution.py:43
  136.4 10.1 %collective-permute-start.28 = (bf16[256,1024]{1,0:T(8,128)(2,1)S(1)}, bf16[256,1024]{1,0:T(8,128)(2,1)S(1)}, u32[]{:S(2)}, u32[]{:S(2)}) collective-permute-start(bf16[256,1024]{1,0:T(8,128)(2,1)S(1)} %fusion.4), channel_id=1, source_target_pairs={{0,32},{1,33},{2,34},{3,35},{4,36},{5,37},{6,38},{7,39},{8,40},{9,... | collective-permute-start | bytes 1572872 | tf_op jit(solution)/shard_map/ppermute | solution.py:43
  136.5 13.4 %collective-permute-start.29 = (bf16[256,768]{1,0:T(8,128)(2,1)S(1)}, bf16[256,768]{1,0:T(8,128)(2,1)S(1)}, u32[]{:S(2)}, u32[]{:S(2)}) collective-permute-start(bf16[256,768]{1,0:T(8,128)(2,1)S(1)} %fusion.7), channel_id=1, source_target_pairs={{0,32},{1,33},{2,34},{3,35},{4,36},{5,37},{6,38},{7,39},{8,40},{9,... | collective-permute-start | bytes 1179656 | tf_op jit(solution)/shard_map/ppermute | solution.py:43
  141.5 4.4 %collective-permute-start.27 = (bf16[12,2048]{1,0:T(8,128)(2,1)S(1)}, bf16[12,2048]{1,0:T(8,128)(2,1)S(1)}, u32[]{:S(2)}, u32[]{:S(2)}) collective-permute-start(bf16[12,2048]{1,0:T(8,128)(2,1)S(1)} %get-tuple-element.89), channel_id=1, source_target_pairs={{0,128},{1,129},{2,130},{3,131},{4,132},{5,133},{6,134},{7,135},{8... | collective-permute-start | bytes 147464 | tf_op jit(solution)/shard_map/ppermute | solution.py:43

commit v2 on v1

v2 whole, which is shorter than its diff:
```python
import functools
import itertools

import jax
import jax.numpy as jnp
import numpy as np
from jax import lax
from jax.experimental import pallas as pl
from jax.experimental.pallas import tpu as pltpu
from jax.sharding import PartitionSpec as P

BOTH = ("dp", "tensor")
F32 = jnp.float32
BF16 = jnp.bfloat16
TILE = 256
VMEM_LIMIT = 16 * 1024 * 1024
VMEM = pl.BlockSpec(memory_space=pltpu.VMEM)
ANY = pl.BlockSpec(memory_space=pl.ANY)


def perm(target):
    def index(zl, y, c, x, zh):
        return ((zl * 4 + y) * 2 + c) * 16 + x * 4 + zh

    return [
        (index(*at), index(*target(*at, 3 if at[2] else 1, 1 if at[2] else 3)))
        for at in itertools.product(range(2), range(4), range(2), range(4), range(4))
    ]


TO_CORE = perm(lambda zl, y, c, x, zh, a, b: (zl, y, 1 - c, x, zh))
TO_ZL = perm(lambda zl, y, c, x, zh, a, b: (1 - zl, y, c, x, zh))
TO_ZL_ZH_A = perm(lambda zl, y, c, x, zh, a, b: (1 - zl, y, c, x, zh ^ a))
Y_A = perm(lambda zl, y, c, x, zh, a, b: (zl, y ^ a, c, x, zh))
Y_B = perm(lambda zl, y, c, x, zh, a, b: (zl, y ^ b, c, x, zh))
X_A = perm(lambda zl, y, c, x, zh, a, b: (zl, y, c, x ^ a, zh))
X_B = perm(lambda zl, y, c, x, zh, a, b: (zl, y, c, x ^ b, zh))
ZH_A = perm(lambda zl, y, c, x, zh, a, b: (zl, y, c, x, zh ^ a))
ZH_B = perm(lambda zl, y, c, x, zh, a, b: (zl, y, c, x, zh ^ b))


def send(value, pairs):
    return lax.ppermute(value, BOTH, pairs)


def fence(*values):
    return lax.optimization_barrier(values)


def call(kernel, out_shape, in_specs, out_specs, scratch=(), cost=None):
    return pl.pallas_call(
        kernel,
        out_shape=out_shape,
        in_specs=in_specs,
        out_specs=out_specs,
        scratch_shapes=list(scratch),
        cost_estimate=cost,
        compiler_params=pltpu.CompilerParams(vmem_limit_bytes=VMEM_LIMIT),
    )


def in_vmem(value):
    return pltpu.with_memory_space_constraint(value, pltpu.VMEM)


def in_hbm(value):
    return pltpu.with_memory_space_constraint(value, pltpu.HBM)


def array(shape, dtype):
    return jax.ShapeDtypeStruct(shape, dtype)


def join_kernel(gate, up, out, sems):
    width = gate.shape[1]
    copies = [
        pltpu.make_async_copy(gate, out.at[:, :width], sems.at[0]),
        pltpu.make_async_copy(up, out.at[:, width:], sems.at[1]),
    ]
    for copy in copies:
        copy.start()
    for copy in copies:
        copy.wait()


def join(gate, up):
    rows, width = gate.shape
    return call(
        join_kernel, pltpu.VMEM((rows, 2 * width), BF16), [ANY, ANY], VMEM, [pltpu.SemaphoreType.DMA((2,))]
    )(in_hbm(gate), in_hbm(up))


def places(p, first, second):
    return (p, p ^ first, p ^ second, p ^ 2)


def feature_blocks():
    dp = lax.axis_index("dp")
    zl, y, c = dp // 8, (dp // 2) % 4, dp % 2
    a, b = 1 + 2 * c, 3 - 2 * c
    blocks = [p * 2 + c for p in places(y, a, b)] + [p * 2 + 1 - c for p in places(y, b, a)]
    starts = [(zl * 8 + k) * 256 for k in blocks] + [((1 - zl) * 8 + k) * 256 for k in blocks]
    return [pl.ds(pl.multiple_of(start, 256), 256) for start in starts]


def dequantize_kernel(codes, scales, own, other, values):
    blocks = scales.shape[1]
    width = codes.shape[1] // blocks
    for b in range(blocks):
        at = slice(b * width, (b + 1) * width)
        values[:, at] = (codes[:, at].astype(F32) * scales[:, b : b + 1].astype(F32)).astype(BF16)
    spans = feature_blocks()
    for k in range(8):
        at = slice(k * 256, (k + 1) * 256)
        own[:, at] = values[:, spans[k]]
        other[:, at] = values[:, spans[8 + k]]


def dequantize(codes, scales):
    rows, features = codes.shape
    half = array((rows, features // 2), BF16)
    return call(
        dequantize_kernel, (half, half), [VMEM, VMEM], (VMEM, VMEM), [pltpu.VMEM((rows, features), BF16)]
    )(codes, scales)


def restore_kernel(kept, from_zl, from_a, from_both, out):
    own = (kept[...] + from_a[...].astype(F32)).astype(BF16)
    other = (from_zl[...].astype(F32) + from_both[...].astype(F32)).astype(BF16)
    spans = feature_blocks()
    for k in range(8):
        at = slice(k * 256, (k + 1) * 256)
        out[:, spans[k]] = own[:, at]
        out[:, spans[8 + k]] = other[:, at]


def restore(kept, *arrived):
    rows, half = kept.shape
    return call(restore_kernel, array((rows, 2 * half), BF16), [VMEM] * 4, VMEM)(kept, *arrived)


def token_table(rows):
    table = np.zeros((2, 4, 4, 1, 16 * rows), np.int32)
    for c, x, zh in itertools.product(range(2), range(4), range(4)):
        a, b = 1 + 2 * c, 3 - 2 * c
        at = [p * 4 + q for p in places(x, a, b) for q in places(zh, a, b)]
        table[c, x, zh, 0] = (np.array(at)[:, None] * rows + np.arange(rows)).reshape(-1)
    return table.reshape(32, 1, 16 * rows)


def arrange_kernel(table, values, out):
    source = table[lax.axis_index("dp") % 2 * 16 + lax.axis_index("tensor")]
    group = values.shape[0]
    pick = (lax.broadcasted_iota(jnp.int32, (group, group), 0) == source).astype(F32).astype(BF16)
    out[...] = lax.dot_general(
        pick, values[...], (((0,), (0,)), ((), ())), preferred_element_type=F32
    ).astype(BF16)


def arrange(values, rows):
    return call(arrange_kernel, array(values.shape, BF16), [VMEM, VMEM], VMEM)(token_table(rows), values)


def stack_kernel(*refs):
    *pieces, out, sems = refs
    copies = []
    at = 0
    for n, piece in enumerate(pieces):
        copies.append(pltpu.make_async_copy(piece, out.at[at : at + piece.shape[0]], sems.at[n]))
        at += piece.shape[0]
    for copy in copies:
        copy.start()
    for copy in copies:
        copy.wait()


def stack(*pieces):
    out = pltpu.VMEM((sum(piece.shape[0] for piece in pieces), pieces[0].shape[1]), BF16)
    return call(stack_kernel, out, [ANY] * len(pieces), VMEM, [pltpu.SemaphoreType.DMA((len(pieces),))])(*pieces)


def forward_kernel(near, away, mine, *refs):
    pieces, (rows, theirs, own, par, sems) = refs[:-5], refs[-5:]
    copies = []
    at = 0
    for n, piece in enumerate(pieces):
        copies.append(pltpu.make_async_copy(piece, theirs.at[at : at + piece.shape[0]], sems.at[n]))
        at += piece.shape[0]
    for copy in copies:
        copy.start()
    part = near.shape[0] // 4
    for n, values in enumerate((near, away)):
        for q in range(2):
            for z in range(2):
                to = (4 * z + 2 * n + q) * part
                rows[to : to + part, :] = values[(2 * q + z) * part : (2 * q + z + 1) * part, :]
    for copy in copies:
        copy.wait()
    group = own.shape[0]
    half = mine.shape[0]
    for at in range(0, mine.shape[1], TILE):
        span = slice(at, at + TILE)
        result = jnp.dot(rows[:, :half], mine[:, span], preferred_element_type=F32)
        result += jnp.dot(rows[:, half:], theirs[:, span], preferred_element_type=F32)
        own[:, span] = result[:group]
        par[:, span] = result[group:].astype(BF16)


def forward(near, away, mine, pieces):
    group, features = near.shape
    width = mine.shape[1]
    outs = (
        pltpu.VMEM((2 * group, features), BF16),
        pltpu.VMEM(mine.shape, BF16),
        pltpu.VMEM((group, width), F32),
        pltpu.VMEM((group, width), BF16),
    )
    inputs, theirs, own, par = call(
        forward_kernel,
        outs,
        [VMEM] * 3 + [ANY] * len(pieces),
        (VMEM,) * 4,
        [pltpu.SemaphoreType.DMA((len(pieces),))],
    )(near, away, mine, *pieces)
    return inputs, (mine, theirs), own, par


def gradient_kernel(own, sent, upstream, out):
    hidden = upstream.shape[1]
    stream = upstream[...].astype(F32)
    gate = own[:, :hidden] + sent[:, :hidden].astype(F32)
    up = own[:, hidden:] + sent[:, hidden:].astype(F32)
    sigmoid = jax.nn.sigmoid(gate)
    out[:, :hidden] = (stream * up * sigmoid * (1.0 + gate * (1.0 - sigmoid))).astype(BF16)
    out[:, hidden:] = (stream * gate * sigmoid).astype(BF16)


def gradient(own, sent, upstream):
    return call(gradient_kernel, array(own.shape, BF16), [VMEM] * 3, VMEM)(own, sent, upstream)


def backward_kernel(grad, mine, theirs, *refs):
    half = grad.shape[0] // 2
    if len(refs) == 3:
        before, near, away = refs
        near[:half] = before[:half]
        away[:half] = before[half:]
    for k in range(8):
        span = slice(256 * k, 256 * (k + 1))
        held = (mine, theirs)[k // 4][256 * (k % 4) : 256 * (k % 4 + 1)]
        result = lax.dot_general(
            grad[...], held, (((1,), (1,)), ((), ())), preferred_element_type=F32
        ).astype(BF16)
        if len(refs) == 3:
            near[half:, span] = result[:half]
            away[half:, span] = result[half:]
        else:
            refs[0][:, span] = result


def backward(grad, held, *before):
    out = array((grad.shape[0], 2 * held[0].shape[0]), BF16)
    outs, specs = ((out, out), (VMEM, VMEM)) if before else (out, VMEM)
    return call(backward_kernel, outs, [VMEM] * (3 + len(before)), specs)(grad, *held, *before)


def finish_kernel(scale, total, last, gate, up):
    width = gate.shape[1]
    for out, span in ((gate, slice(0, width)), (up, slice(width, 2 * width))):
        out[...] = (total[:, span] + last[:, span].astype(F32)) * scale


def finish(total, last, scale):
    rows, width = total.shape
    out = array((rows, width // 2), F32)
    return call(functools.partial(finish_kernel, scale), (out, out), [VMEM, VMEM], (VMEM, VMEM))(total, last)


def add(*values):
    total = values[0].astype(F32)
    for value in values[1:]:
        total = total + value.astype(F32)
    return total


def local(saved_codes, saved_scales, gate_weight, up_weight, hidden_grad):
    rows = saved_codes.shape[0]
    group = hidden_grad.shape[0]

    row = np.arange(8 * rows)
    taken = (row // rows % 4 * 2 + row // (4 * rows)) * rows + row % rows
    by_group = np.equal(taken[:, None], row[None, :])

    shard = join(gate_weight, up_weight)
    from_a = send(shard, Y_A)
    from_b = send(shard, Y_B)
    theirs = [send(shard, TO_CORE)]

    saved_codes, saved_scales, _ = fence(saved_codes, saved_scales, shard)
    kept, given = dequantize(saved_codes, saved_scales)
    two = jnp.concatenate([kept, send(given, TO_ZL), send(kept, ZH_A), send(given, TO_ZL_ZH_A)], axis=0)
    (two,) = fence(two)
    arrived, from_a, from_b, theirs[0] = fence(send(two, ZH_B), from_a, from_b, theirs[0])
    four = jnp.concatenate([two, arrived], axis=0)
    slab = jnp.dot(by_group.astype(BF16), four, preferred_element_type=F32).astype(BF16)
    slab, from_a = fence(slab, from_a)
    far = send(from_a, Y_B)
    near = jnp.concatenate([slab, send(slab, X_A)], axis=0)
    (near,) = fence(near)
    away = send(near, X_B)

    from_a, from_b, _ = fence(from_a, from_b, near)
    part = shard.shape[0] // 2
    theirs += [send(piece[at : at + part], TO_CORE) for piece in (from_a, from_b) for at in (0, part)]
    mine = stack(shard, from_a, from_b, far)
    far, mine = fence(far, mine)
    theirs.append(send(far, TO_CORE))
    upstream = arrange(hidden_grad, rows)

    inputs, held, own, par = forward(near, away, mine, theirs)
    sent = send(par, TO_ZL)

    grad = gradient(own, sent, upstream)
    other = send(grad, TO_ZL)
    own_back = backward(grad, held)
    other, own_back = fence(other, own_back)

    def product(first, last):
        both = jnp.concatenate([grad, other], axis=0)
        return lax.dot_general(
            inputs[:, first:last], both, (((0,), (0,)), ((), ())), preferred_element_type=F32
        )

    given = product(1536, 2048).astype(BF16)
    given, other = fence(given, other)
    shown_high = send(given, TO_CORE)
    kept, passed = backward(other, held, own_back)
    arrived = send(passed, X_B)
    shown_high, other, _ = fence(shown_high, other, kept)
    passed = add(product(512, 1024), shown_high).astype(BF16)
    from_b = send(passed, Y_B)
    other, _ = fence(other, passed)
    shown_low = send(product(1024, 1536).astype(BF16), TO_CORE)

    back = add(kept, arrived)
    half, part = group // 2, group // 4
    passed = jnp.concatenate([back[part:half], back[half + part :]], axis=0).astype(BF16)
    kept = jnp.concatenate([back[:part], back[half : half + part]], axis=0)
    four = jnp.dot(
        by_group.T.astype(np.float32),
        add(kept, send(passed, X_A)),
        preferred_element_type=F32,
        precision=lax.Precision.HIGHEST,
    )
    half = 4 * rows
    two = add(four[:half], send(four[half:].astype(BF16), ZH_B))
    kept, *passed = (two[at : at + rows] for at in range(0, half, rows))
    arrived = [send(v.astype(BF16), pairs) for v, pairs in zip(passed, (TO_ZL, ZH_A, TO_ZL_ZH_A))]
    input_grad = restore(kept, *arrived)

    passed = add(product(256, 512), shown_low[256:], from_b[256:]).astype(BF16)
    last = send(passed, Y_A)
    total = add(product(0, 256), shown_low[:256], from_b[:256])
    gate_grad, up_grad = finish(total, last, 1.0 / group)
    return input_grad, gate_grad, up_grad


def solution(mesh):
    placed = (P(BOTH, None), P(BOTH, None), P("dp", "tensor"), P("dp", "tensor"), P("dp", "tensor"))
    return jax.shard_map(
        local,
        mesh=mesh,
        in_specs=placed,
        out_specs=(P(BOTH, None), P("dp", "tensor"), P("dp", "tensor")),
        check_vma=False,
    )
```

time: 154 us -> 137 us (0.89); the launches traced: 151 us -> 136 us
  starting transfers between devices: 42.8 us -> 29.5 us
  waiting for transfers between devices: 85.5 us -> 83.7 us
    ppermute x30 -> x27, starting transfers between devices: 42.8 us -> 29.5 us  [send(): return lax.ppermute(value, BOTH, pairs)]
    ppermute x30 -> x27, waiting for transfers between devices: 85.5 us -> 83.7 us  [send(): return lax.ppermute(value, BOTH, pairs)]
    dot_general x9 -> x6, matrix products: 6.26 us -> 5.71 us  [the longest x5 4.93 us: product(): lax.dot_general(inputs[:, first:last], both, (((0,), (0,)), ((), ())), pr...]
    pallas_call x9 -> x7, Pallas kernels: 12.7 us -> 13.1 us  [the longest x2 5.01 us: backward(): call(backward_kernel, outs, [VMEM] * (3 + len(before)), specs)]
  transfers between devices with their start and end apart: 30 -> 27, of which waited for: 23 -> 18; matrix products, arithmetic and copies ran while one was open for 3% -> 4% of each run, Pallas kernels for 4% -> 5%
where the time goes in v2:
time: 137 us; the launch traced here: 136 us
  waiting for transfers between devices  83.7 us (61%)
  starting transfers between devices  29.5 us (22%)
  Pallas kernels  14.8 us (11%)
  matrix products  6.17 us (5%)
    ppermute x27, waiting for transfers between devices, send(): return lax.ppermute(value, BOTH, pairs)  83.7 us
    ppermute x27, starting transfers between devices, send(): return lax.ppermute(value, BOTH, pairs)  29.5 us
    pallas_call x2, Pallas kernels, backward(): call(backward_kernel, outs, [VMEM] * (3 + len(before)), specs)  5.01 us
    dot_general x5, matrix products, product(): lax.dot_general(inputs[:, first:last], both, (((0,), (0,)), ((), ())), pr...  4.93 us
    pallas_call x1, Pallas kernels, forward(): call(forward_kernel, outs, [VMEM] * 3 + [ANY] * len(pieces), (VMEM,) * 4,...  4.69 us
  transfers between devices with their start and end apart: 27, of which 18 were waited for; matrix products, arithmetic and copies ran while one was open for 4% of the time, Pallas kernels for 5%

profile of v2, /device:TPU:64, one launch (start us, length us, event | category | flops | bytes accessed | tf_op | source)
XLA Modules:
  0.0 135.9 jit_solution(8775850526238949657)
XLA Ops:
  0.7 1.2 shard_map.103.refs_0_
  1.9 1.7 %collective-permute-start.4 = (bf16[256,1792]{1,0:T(8,128)(2,1)S(1)}, bf16[256,1792]{1,0:T(8,128)(2,1)S(1)}, u32[]{:S(2)}, u32[]{:S(2)}) collective-permute-start(bf16[256,1792]{1,0:T(8,128)(2,1)S(1)} %shard_map.103.refs_0_), channel_id=1, source_target_pairs={{0,32},{1,33},{2,34},{3,35},{4,36},{5,37},{6,38},{7,39},{8,40},{9,... | collective-permute-start | bytes 2752520 | tf_op jit(solution)/shard_map/ppermute | solution.py:43
  3.6 2.2 %collective-permute-start.5 = (bf16[256,1792]{1,0:T(8,128)(2,1)S(1)}, bf16[256,1792]{1,0:T(8,128)(2,1)S(1)}, u32[]{:S(2)}, u32[]{:S(2)}) collective-permute-start(bf16[256,1792]{1,0:T(8,128)(2,1)S(1)} %shard_map.103.refs_0_), channel_id=1, source_target_pairs={{0,96},{1,97},{2,98},{3,99},{4,100},{5,101},{6,102},{7,103},{8,104... | collective-permute-start | bytes 2752520 | tf_op jit(solution)/shard_map/ppermute | solution.py:43
  5.9 2.0 %collective-permute-start = (bf16[12,2048]{1,0:T(8,128)(2,1)S(1)}, bf16[12,2048]{1,0:T(8,128)(2,1)S(1)}, u32[]{:S(2)}, u32[]{:S(2)}) collective-permute-start(bf16[12,2048]{1,0:T(8,128)(2,1)S(1)} %get-tuple-element.35), channel_id=1, source_target_pairs={{0,128},{1,129},{2,130},{3,131},{4,132},{5,133},{6,134},{7,135},{8... | collective-permute-start | bytes 147464 | tf_op jit(solution)/shard_map/ppermute | solution.py:43
  7.9 2.8 %collective-permute-done = bf16[12,2048]{1,0:T(8,128)(2,1)S(1)} collective-permute-done((bf16[12,2048]{1,0:T(8,128)(2,1)S(1)}, bf16[12,2048]{1,0:T(8,128)(2,1)S(1)}, u32[]{:S(2)}, u32[]{:S(2)}) %collective-permute-start) | collective-permute-done | bytes 49184 | tf_op jit(solution)/shard_map/ppermute | solution.py:43
  10.7 2.4 %collective-permute-done.1 = bf16[12,2048]{1,0:T(8,128)(2,1)S(1)} collective-permute-done((bf16[12,2048]{1,0:T(8,128)(2,1)S(1)}, bf16[12,2048]{1,0:T(8,128)(2,1)S(1)}, u32[]{:S(2)}, u32[]{:S(2)}) %collective-permute-start.1) | collective-permute-done | bytes 49184 | tf_op jit(solution)/shard_map/ppermute | solution.py:43
  13.1 1.9 %collective-permute-done.2 = bf16[12,2048]{1,0:T(8,128)(2,1)S(1)} collective-permute-done((bf16[12,2048]{1,0:T(8,128)(2,1)S(1)}, bf16[12,2048]{1,0:T(8,128)(2,1)S(1)}, u32[]{:S(2)}, u32[]{:S(2)}) %collective-permute-start.2) | collective-permute-done | bytes 49184 | tf_op jit(solution)/shard_map/ppermute | solution.py:43
  15.0 7.3 %collective-permute-start.3 = (bf16[48,2048]{1,0:T(8,128)(2,1)S(1)}, bf16[48,2048]{1,0:T(8,128)(2,1)S(1)}, u32[]{:S(2)}, u32[]{:S(2)}) collective-permute-start(bf16[48,2048]{1,0:T(8,128)(2,1)S(1)} %pad_maximum_fusion.10), channel_id=1, source_target_pairs={{0,3},{1,2},{2,1},{3,0},{4,7},{5,6},{6,5},{7,4},{8,11},{9,10},{10,... | collective-permute-start | bytes 589832 | tf_op jit(solution)/shard_map/ppermute | solution.py:43
  22.3 5.8 %collective-permute-done.3 = bf16[48,2048]{1,0:T(8,128)(2,1)S(1)} collective-permute-done((bf16[48,2048]{1,0:T(8,128)(2,1)S(1)}, bf16[48,2048]{1,0:T(8,128)(2,1)S(1)}, u32[]{:S(2)}, u32[]{:S(2)}) %collective-permute-start.3) | collective-permute-done | bytes 196640 | tf_op jit(solution)/shard_map/ppermute | solution.py:43
  28.5 1.6 %collective-permute-start.7 = (bf16[96,2048]{1,0:T(8,128)(2,1)S(1)}, bf16[96,2048]{1,0:T(8,128)(2,1)S(1)}, u32[]{:S(2)}, u32[]{:S(2)}) collective-permute-start(bf16[96,2048]{1,0:T(8,128)(2,1)S(1)} %fusion.4), channel_id=1, source_target_pairs={{0,4},{1,5},{2,6},{3,7},{4,0},{5,1},{6,2},{7,3},{8,12},{9,13},{10,... | collective-permute-start | bytes 1179656 | tf_op jit(solution)/shard_map/ppermute | solution.py:43
  30.1 1.1 collective-permute-start.9
  31.2 5.2 %collective-permute-done.7 = bf16[96,2048]{1,0:T(8,128)(2,1)S(1)} collective-permute-done((bf16[96,2048]{1,0:T(8,128)(2,1)S(1)}, bf16[96,2048]{1,0:T(8,128)(2,1)S(1)}, u32[]{:S(2)}, u32[]{:S(2)}) %collective-permute-start.7) | collective-permute-done | bytes 393248 | tf_op jit(solution)/shard_map/ppermute | solution.py:43
  36.5 2.8 %collective-permute-start.8 = (bf16[192,2048]{1,0:T(8,128)(2,1)S(1)}, bf16[192,2048]{1,0:T(8,128)(2,1)S(1)}, u32[]{:S(2)}, u32[]{:S(2)}) collective-permute-start(bf16[192,2048]{1,0:T(8,128)(2,1)S(1)} %pad_maximum_fusion.5.near), channel_id=1, source_target_pairs={{0,12},{1,13},{2,14},{3,15},{4,8},{5,9},{6,10},{7,11},{8,4},{9,5},... | collective-permute-start | bytes 2359304 | tf_op jit(solution)/shard_map/ppermute | solution.py:43
  39.5 0.5 collective-permute-start.11
  40.0 4.8 %collective-permute-done.9.refs_3_ = bf16[256,1792]{1,0:T(8,128)(2,1)S(1)} collective-permute-done((bf16[256,1792]{1,0:T(8,128)(2,1)S(1)}, bf16[256,1792]{1,0:T(8,128)(2,1)S(1)}, u32[]{:S(2)}, u32[]{:S(2)}) %collective-permute-start.9) | collective-permute-done | bytes 917536 | tf_op jit(solution)/shard_map/ppermute | solution.py:43
  44.7 0.9 shard_map.105.mine
  45.8 0.6 collective-permute-start.12
  46.6 2.3 %collective-permute-done.12.refs_3_ = bf16[128,1792]{1,0:T(8,128)(2,1)S(1)} collective-permute-done((bf16[128,1792]{1,0:T(8,128)(2,1)S(1)}, bf16[128,1792]{1,0:T(8,128)(2,1)S(1)}, u32[]{:S(2)}, u32[]{:S(2)}) %collective-permute-start.12) | collective-permute-done | bytes 458784 | tf_op jit(solution)/shard_map/ppermute | solution.py:43
  48.9 0.7 collective-permute-done.13.refs_4_
  49.8 4.7 %shard_map.106 = (bf16[384,2048]{1,0:T(8,128)(2,1)S(1)}, bf16[1024,1792]{1,0:T(8,128)(2,1)S(1)}, f32[192,1792]{1,0:T(8,128)S(1)}, bf16[192,1792]{1,0:T(8,128)(2,1)S(1)}) custom-call(bf16[192,2048]{1,0:T(8,128)(2,1)S(1)} %pad_maximum_fusion.5.near, bf16[192,2048]{1,0:T(8,128)(2,1)S(1)} %collective-permute-done.8.away, ...), custom_call_target="tpu_custom_call" | custom-call | tf_op jit(solution)/shard_map/pallas_call | solution.py:218
  54.8 0.3 shard_map.107.upstream
  55.1 16.9 %collective-permute-done.15.sent = bf16[192,1792]{1,0:T(8,128)(2,1)S(1)} collective-permute-done((bf16[192,1792]{1,0:T(8,128)(2,1)S(1)}, bf16[192,1792]{1,0:T(8,128)(2,1)S(1)}, u32[]{:S(2)}, u32[]{:S(2)}) %collective-permute-start.15) | collective-permute-done | bytes 688160 | tf_op jit(solution)/shard_map/ppermute | solution.py:43
  72.0 0.4 shard_map.108.grad
  72.4 0.4 collective-permute-start.16
  72.8 2.5 %shard_map.109.refs_0_ = bf16[192,2048]{1,0:T(8,128)(2,1)S(1)} custom-call(bf16[192,1792]{1,0:T(8,128)(2,1)S(1)} %shard_map.108.grad, bf16[1024,1792]{1,0:T(8,128)(2,1)S(1)} %shard_map.105.mine, bf16[1024,1792]{1,0:T(8,128)(2,1)S(1)} %get-tuple-element.49.theirs), custom_call_target="tpu_custom_call" | custom-call | tf_op jit(solution)/shard_map/pallas_call | solution.py:264
  75.3 13.6 %collective-permute-done.16.grad = bf16[192,1792]{1,0:T(8,128)(2,1)S(1)} collective-permute-done((bf16[192,1792]{1,0:T(8,128)(2,1)S(1)}, bf16[192,1792]{1,0:T(8,128)(2,1)S(1)}, u32[]{:S(2)}, u32[]{:S(2)}) %collective-permute-start.16) | collective-permute-done | bytes 688160 | tf_op jit(solution)/shard_map/ppermute | solution.py:43
  88.9 1.2 convolution_convert_fusion.1
  90.2 2.5 %shard_map.110 = (bf16[192,2048]{1,0:T(8,128)(2,1)S(1)}, bf16[192,2048]{1,0:T(8,128)(2,1)S(1)}) custom-call(bf16[192,1792]{1,0:T(8,128)(2,1)S(1)} %collective-permute-done.16.grad, bf16[1024,1792]{1,0:T(8,128)(2,1)S(1)} %shard_map.105.mine, bf16[1024,1792]{1,0:T(8,128)(2,1)S(1)} %get-tuple-element.49.theirs, bf16[192,2048]{1,0:T(8,128)(2,1)S(1)} %shard_map.109.refs_0_), custom_call_target="tpu_custom_call" | custom-call | tf_op jit(solution)/shard_map/pallas_call | solution.py:264
  92.7 1.4 %collective-permute-start.17 = (bf16[192,2048]{1,0:T(8,128)(2,1)S(1)}, bf16[192,2048]{1,0:T(8,128)(2,1)S(1)}, u32[]{:S(2)}, u32[]{:S(2)}) collective-permute-start(bf16[192,2048]{1,0:T(8,128)(2,1)S(1)} %get-tuple-element.54), channel_id=1, source_target_pairs={{0,12},{1,13},{2,14},{3,15},{4,8},{5,9},{6,10},{7,11},{8,4},{9,5},... | collective-permute-start | bytes 2359304 | tf_op jit(solution)/shard_map/ppermute | solution.py:43
  94.1 1.2 add_convert_fusion
  95.3 1.1 collective-permute-start.25
  96.4 1.2 convolution_convert_fusion
  97.7 8.2 %collective-permute-done.17 = bf16[192,2048]{1,0:T(8,128)(2,1)S(1)} collective-permute-done((bf16[192,2048]{1,0:T(8,128)(2,1)S(1)}, bf16[192,2048]{1,0:T(8,128)(2,1)S(1)}, u32[]{:S(2)}, u32[]{:S(2)}) %collective-permute-start.17) | collective-permute-done | bytes 786464 | tf_op jit(solution)/shard_map/ppermute | solution.py:43
  106.0 0.3 fusion.22
  106.5 7.7 %collective-permute-done.18 = bf16[96,2048]{1,0:T(8,128)(2,1)S(1)} collective-permute-done((bf16[96,2048]{1,0:T(8,128)(2,1)S(1)}, bf16[96,2048]{1,0:T(8,128)(2,1)S(1)}, u32[]{:S(2)}, u32[]{:S(2)}) %collective-permute-start.18) | collective-permute-done | bytes 393248 | tf_op jit(solution)/shard_map/ppermute | solution.py:43
  114.2 0.8 fusion.7
  115.0 2.3 %collective-permute-start.19 = (bf16[48,2048]{1,0:T(8,128)(2,1)S(1)}, bf16[48,2048]{1,0:T(8,128)(2,1)S(1)}, u32[]{:S(2)}, u32[]{:S(2)}) collective-permute-start(bf16[48,2048]{1,0:T(8,128)(2,1)S(1)} %slice.130), channel_id=1, source_target_pairs={{0,3},{1,2},{2,1},{3,0},{4,7},{5,6},{6,5},{7,4},{8,11},{9,10},{10,... | collective-permute-start | bytes 589832 | tf_op jit(solution)/shard_map/ppermute | solution.py:43
  117.3 2.5 %collective-permute-done.25 = bf16[512,1792]{1,0:T(8,128)(2,1)S(1)} collective-permute-done((bf16[512,1792]{1,0:T(8,128)(2,1)S(1)}, bf16[512,1792]{1,0:T(8,128)(2,1)S(1)}, u32[]{:S(2)}, u32[]{:S(2)}) %collective-permute-start.25) | collective-permute-done | bytes 1835040 | tf_op jit(solution)/shard_map/ppermute | solution.py:43
  119.8 0.7 fusion.2
  120.7 4.5 %collective-permute-done.19 = bf16[48,2048]{1,0:T(8,128)(2,1)S(1)} collective-permute-done((bf16[48,2048]{1,0:T(8,128)(2,1)S(1)}, bf16[48,2048]{1,0:T(8,128)(2,1)S(1)}, u32[]{:S(2)}, u32[]{:S(2)}) %collective-permute-start.19) | collective-permute-done | bytes 196640 | tf_op jit(solution)/shard_map/ppermute | solution.py:43
  125.3 0.4 collective-permute-start.20
  125.9 3.0 %collective-permute-start.22 = (bf16[12,2048]{1,0:T(8,128)(2,1)S(1)}, bf16[12,2048]{1,0:T(8,128)(2,1)S(1)}, u32[]{:S(2)}, u32[]{:S(2)}) collective-permute-start(bf16[12,2048]{1,0:T(8,128)(2,1)S(1)} %get-tuple-element.73), channel_id=1, source_target_pairs={{0,129},{1,128},{2,131},{3,130},{4,133},{5,132},{6,135},{7,134},{8... | collective-permute-start | bytes 147464 | tf_op jit(solution)/shard_map/ppermute | solution.py:43
  128.9 0.9 collective-permute-done.20.from_zl
  129.8 1.7 %collective-permute-done.21.from_a = bf16[12,2048]{1,0:T(8,128)(2,1)S(1)} collective-permute-done((bf16[12,2048]{1,0:T(8,128)(2,1)S(1)}, bf16[12,2048]{1,0:T(8,128)(2,1)S(1)}, u32[]{:S(2)}, u32[]{:S(2)}) %collective-permute-start.21) | collective-permute-done | bytes 49184 | tf_op jit(solution)/shard_map/ppermute | solution.py:43
  131.4 1.7 %collective-permute-done.22.from_both = bf16[12,2048]{1,0:T(8,128)(2,1)S(1)} collective-permute-done((bf16[12,2048]{1,0:T(8,128)(2,1)S(1)}, bf16[12,2048]{1,0:T(8,128)(2,1)S(1)}, u32[]{:S(2)}, u32[]{:S(2)}) %collective-permute-start.22) | collective-permute-done | bytes 49184 | tf_op jit(solution)/shard_map/ppermute | solution.py:43
  133.1 0.7 shard_map.111
  133.8 0.7 fusion.1.total
  134.5 1.4 %shard_map.112 = (f32[256,896]{1,0:T(8,128)}, f32[256,896]{1,0:T(8,128)}) custom-call(f32[256,1792]{1,0:T(8,128)S(1)} %fusion.1.total, bf16[256,1792]{1,0:T(8,128)(2,1)S(1)} %collective-permute-done.26.last), custom_call_target="tpu_custom_call" | custom-call | tf_op jit(solution)/shard_map/pallas_call | solution.py:276
  (50 shorter events, 2.4 us)
Async XLA Ops:
  0.6 27.4 %copy-start.5 = (bf16[96,48]{1,0:T(8,128)(2,1)S(1)}, bf16[96,48]{1,0:T(8,128)(2,1)}, u32[]{:S(2)}) copy-start(bf16[96,48]{1,0:T(8,128)(2,1)} %constant.12) | copy-start | bytes 27652
  0.6 27.7 %copy-start.6 = (bf16[96,48]{1,0:T(8,128)(2,1)S(1)}, bf16[96,48]{1,0:T(8,128)(2,1)}, u32[]{:S(2)}) copy-start(bf16[96,48]{1,0:T(8,128)(2,1)} %constant.11) | copy-start | bytes 27652
  0.7 5.1 %copy-start.1 = (bf16[12,4096]{1,0:T(8,128)(2,1)S(1)}, bf16[12,4096]{1,0:T(8,128)(2,1)}, u32[]{:S(2)}) copy-start(bf16[12,4096]{1,0:T(8,128)(2,1)} %codes) | copy-start | bytes 294916
  0.7 5.1 %copy-start.3 = (bf16[12,32]{1,0:T(8,128)(2,1)S(1)}, bf16[12,32]{1,0:T(8,128)(2,1)}, u32[]{:S(2)}) copy-start(bf16[12,32]{1,0:T(8,128)(2,1)} %scales) | copy-start | bytes 2308
  1.9 26.1 %collective-permute-start.4 = (bf16[256,1792]{1,0:T(8,128)(2,1)S(1)}, bf16[256,1792]{1,0:T(8,128)(2,1)S(1)}, u32[]{:S(2)}, u32[]{:S(2)}) collective-permute-start(bf16[256,1792]{1,0:T(8,128)(2,1)S(1)} %shard_map.103.refs_0_), channel_id=1, source_target_pairs={{0,32},{1,33},{2,34},{3,35},{4,36},{5,37},{6,38},{7,39},{8,40},{9,... | collective-permute-start | bytes 2752520 | tf_op jit(solution)/shard_map/ppermute | solution.py:43
  3.6 24.5 %collective-permute-start.5 = (bf16[256,1792]{1,0:T(8,128)(2,1)S(1)}, bf16[256,1792]{1,0:T(8,128)(2,1)S(1)}, u32[]{:S(2)}, u32[]{:S(2)}) collective-permute-start(bf16[256,1792]{1,0:T(8,128)(2,1)S(1)} %shard_map.103.refs_0_), channel_id=1, source_target_pairs={{0,96},{1,97},{2,98},{3,99},{4,100},{5,101},{6,102},{7,103},{8,104... | collective-permute-start | bytes 2752520 | tf_op jit(solution)/shard_map/ppermute | solution.py:43
  5.7 22.3 %collective-permute-start.6 = (bf16[256,1792]{1,0:T(8,128)(2,1)S(1)}, bf16[256,1792]{1,0:T(8,128)(2,1)S(1)}, u32[]{:S(2)}, u32[]{:S(2)}) collective-permute-start(bf16[256,1792]{1,0:T(8,128)(2,1)S(1)} %shard_map.103.refs_0_), channel_id=1, source_target_pairs={{0,16},{1,17},{2,18},{3,19},{4,20},{5,21},{6,22},{7,23},{8,24},{9,... | collective-permute-start | bytes 2752520 | tf_op jit(solution)/shard_map/ppermute | solution.py:43
  5.9 4.8 %collective-permute-start = (bf16[12,2048]{1,0:T(8,128)(2,1)S(1)}, bf16[12,2048]{1,0:T(8,128)(2,1)S(1)}, u32[]{:S(2)}, u32[]{:S(2)}) collective-permute-start(bf16[12,2048]{1,0:T(8,128)(2,1)S(1)} %get-tuple-element.35), channel_id=1, source_target_pairs={{0,128},{1,129},{2,130},{3,131},{4,132},{5,133},{6,134},{7,135},{8... | collective-permute-start | bytes 147464 | tf_op jit(solution)/shard_map/ppermute | solution.py:43
  7.9 5.2 %collective-permute-start.1 = (bf16[12,2048]{1,0:T(8,128)(2,1)S(1)}, bf16[12,2048]{1,0:T(8,128)(2,1)S(1)}, u32[]{:S(2)}, u32[]{:S(2)}) collective-permute-start(bf16[12,2048]{1,0:T(8,128)(2,1)S(1)} %get-tuple-element.34), channel_id=1, source_target_pairs={{0,1},{1,0},{2,3},{3,2},{4,5},{5,4},{6,7},{7,6},{8,9},{9,8},{10,11... | collective-permute-start | bytes 147464 | tf_op jit(solution)/shard_map/ppermute | solution.py:43
  10.7 4.3 %collective-permute-start.2 = (bf16[12,2048]{1,0:T(8,128)(2,1)S(1)}, bf16[12,2048]{1,0:T(8,128)(2,1)S(1)}, u32[]{:S(2)}, u32[]{:S(2)}) collective-permute-start(bf16[12,2048]{1,0:T(8,128)(2,1)S(1)} %get-tuple-element.35), channel_id=1, source_target_pairs={{0,129},{1,128},{2,131},{3,130},{4,133},{5,132},{6,135},{7,134},{8... | collective-permute-start | bytes 147464 | tf_op jit(solution)/shard_map/ppermute | solution.py:43
  15.0 13.0 %collective-permute-start.3 = (bf16[48,2048]{1,0:T(8,128)(2,1)S(1)}, bf16[48,2048]{1,0:T(8,128)(2,1)S(1)}, u32[]{:S(2)}, u32[]{:S(2)}) collective-permute-start(bf16[48,2048]{1,0:T(8,128)(2,1)S(1)} %pad_maximum_fusion.10), channel_id=1, source_target_pairs={{0,3},{1,2},{2,1},{3,0},{4,7},{5,6},{6,5},{7,4},{8,11},{9,10},{10,... | collective-permute-start | bytes 589832 | tf_op jit(solution)/shard_map/ppermute | solution.py:43
  28.5 7.9 %collective-permute-start.7 = (bf16[96,2048]{1,0:T(8,128)(2,1)S(1)}, bf16[96,2048]{1,0:T(8,128)(2,1)S(1)}, u32[]{:S(2)}, u32[]{:S(2)}) collective-permute-start(bf16[96,2048]{1,0:T(8,128)(2,1)S(1)} %fusion.4), channel_id=1, source_target_pairs={{0,4},{1,5},{2,6},{3,7},{4,0},{5,1},{6,2},{7,3},{8,12},{9,13},{10,... | collective-permute-start | bytes 1179656 | tf_op jit(solution)/shard_map/ppermute | solution.py:43
  30.1 14.6 %collective-permute-start.9 = (bf16[256,1792]{1,0:T(8,128)(2,1)S(1)}, bf16[256,1792]{1,0:T(8,128)(2,1)S(1)}, u32[]{:S(2)}, u32[]{:S(2)}) collective-permute-start(bf16[256,1792]{1,0:T(8,128)(2,1)S(1)} %collective-permute-done.4.refs_1_), channel_id=1, source_target_pairs={{0,96},{1,97},{2,98},{3,99},{4,100},{5,101},{6,102},{7,103},{8,104... | collective-permute-start | bytes 2752520 | tf_op jit(solution)/shard_map/ppermute | solution.py:43
  36.5 13.3 %collective-permute-start.8 = (bf16[192,2048]{1,0:T(8,128)(2,1)S(1)}, bf16[192,2048]{1,0:T(8,128)(2,1)S(1)}, u32[]{:S(2)}, u32[]{:S(2)}) collective-permute-start(bf16[192,2048]{1,0:T(8,128)(2,1)S(1)} %pad_maximum_fusion.5.near), channel_id=1, source_target_pairs={{0,12},{1,13},{2,14},{3,15},{4,8},{5,9},{6,10},{7,11},{8,4},{9,5},... | collective-permute-start | bytes 2359304 | tf_op jit(solution)/shard_map/ppermute | solution.py:43
  39.4 7.0 %collective-permute-start.10 = (bf16[128,1792]{1,0:T(8,128)(2,1)S(1)}, bf16[128,1792]{1,0:T(8,128)(2,1)S(1)}, u32[]{:S(2)}, u32[]{:S(2)}) collective-permute-start(bf16[128,1792]{1,0:T(8,128)(2,1)S(1)} %get-tuple-element.70), channel_id=1, source_target_pairs={{0,16},{1,17},{2,18},{3,19},{4,20},{5,21},{6,22},{7,23},{8,24},{9,... | collective-permute-start | bytes 1376264 | tf_op jit(solution)/shard_map/ppermute | solution.py:43
  39.5 7.1 %collective-permute-start.11 = (bf16[128,1792]{1,0:T(8,128)(2,1)S(1)}, bf16[128,1792]{1,0:T(8,128)(2,1)S(1)}, u32[]{:S(2)}, u32[]{:S(2)}) collective-permute-start(bf16[128,1792]{1,0:T(8,128)(2,1)S(1)} %get-tuple-element.69), channel_id=1, source_target_pairs={{0,16},{1,17},{2,18},{3,19},{4,20},{5,21},{6,22},{7,23},{8,24},{9,... | collective-permute-start | bytes 1376264 | tf_op jit(solution)/shard_map/ppermute | solution.py:43
  45.7 4.1 %collective-permute-start.14 = (bf16[256,1792]{1,0:T(8,128)(2,1)S(1)}, bf16[256,1792]{1,0:T(8,128)(2,1)S(1)}, u32[]{:S(2)}, u32[]{:S(2)}) collective-permute-start(bf16[256,1792]{1,0:T(8,128)(2,1)S(1)} %collective-permute-done.9.refs_3_), channel_id=1, source_target_pairs={{0,16},{1,17},{2,18},{3,19},{4,20},{5,21},{6,22},{7,23},{8,24},{9,... | collective-permute-start | bytes 2752520 | tf_op jit(solution)/shard_map/ppermute | solution.py:43
  45.8 3.0 %collective-permute-start.12 = (bf16[128,1792]{1,0:T(8,128)(2,1)S(1)}, bf16[128,1792]{1,0:T(8,128)(2,1)S(1)}, u32[]{:S(2)}, u32[]{:S(2)}) collective-permute-start(bf16[128,1792]{1,0:T(8,128)(2,1)S(1)} %get-tuple-element.68), channel_id=1, source_target_pairs={{0,16},{1,17},{2,18},{3,19},{4,20},{5,21},{6,22},{7,23},{8,24},{9,... | collective-permute-start | bytes 1376264 | tf_op jit(solution)/shard_map/ppermute | solution.py:43
  46.4 8.3 %copy-start = (bf16[192,896]{1,0:T(8,128)(2,1)S(1)}, bf16[192,896]{1,0:T(8,128)(2,1)}, u32[]{:S(2)}) copy-start(bf16[192,896]{1,0:T(8,128)(2,1)} %values.1) | copy-start | bytes 1032196
  46.4 8.3 %copy-start.2 = (s32[32,1,192]{2,1,0:T(1,128)S(1)}, s32[32,1,192]{2,1,0:T(1,128)}, u32[]{:S(2)}) copy-start(s32[32,1,192]{2,1,0:T(1,128)} %constant.7.clone.table) | copy-start | bytes 73732
  46.4 3.1 %collective-permute-start.13 = (bf16[128,1792]{1,0:T(8,128)(2,1)S(1)}, bf16[128,1792]{1,0:T(8,128)(2,1)S(1)}, u32[]{:S(2)}, u32[]{:S(2)}) collective-permute-start(bf16[128,1792]{1,0:T(8,128)(2,1)S(1)} %get-tuple-element.67), channel_id=1, source_target_pairs={{0,16},{1,17},{2,18},{3,19},{4,20},{5,21},{6,22},{7,23},{8,24},{9,... | collective-permute-start | bytes 1376264 | tf_op jit(solution)/shard_map/ppermute | solution.py:43
  54.5 17.5 %collective-permute-start.15 = (bf16[192,1792]{1,0:T(8,128)(2,1)S(1)}, bf16[192,1792]{1,0:T(8,128)(2,1)S(1)}, u32[]{:S(2)}, u32[]{:S(2)}) collective-permute-start(bf16[192,1792]{1,0:T(8,128)(2,1)S(1)} %get-tuple-element.48), channel_id=1, source_target_pairs={{0,128},{1,129},{2,130},{3,131},{4,132},{5,133},{6,134},{7,135},{8... | collective-permute-start | bytes 2064392 | tf_op jit(solution)/shard_map/ppermute | solution.py:43
  72.4 16.5 %collective-permute-start.16 = (bf16[192,1792]{1,0:T(8,128)(2,1)S(1)}, bf16[192,1792]{1,0:T(8,128)(2,1)S(1)}, u32[]{:S(2)}, u32[]{:S(2)}) collective-permute-start(bf16[192,1792]{1,0:T(8,128)(2,1)S(1)} %shard_map.108.grad), channel_id=1, source_target_pairs={{0,128},{1,129},{2,130},{3,131},{4,132},{5,133},{6,134},{7,135},{8... | collective-permute-start | bytes 2064392 | tf_op jit(solution)/shard_map/ppermute | solution.py:43
  90.1 4.1 %collective-permute-start.23 = (bf16[512,1792]{1,0:T(8,128)(2,1)S(1)}, bf16[512,1792]{1,0:T(8,128)(2,1)S(1)}, u32[]{:S(2)}, u32[]{:S(2)}) collective-permute-start(bf16[512,1792]{1,0:T(8,128)(2,1)S(1)} %convolution_convert_fusion.1), channel_id=1, source_target_pairs={{0,16},{1,17},{2,18},{3,19},{4,20},{5,21},{6,22},{7,23},{8,24},{9,... | collective-permute-start | bytes 5505032 | tf_op jit(solution)/shard_map/ppermute | solution.py:43
  92.7 13.3 %collective-permute-start.17 = (bf16[192,2048]{1,0:T(8,128)(2,1)S(1)}, bf16[192,2048]{1,0:T(8,128)(2,1)S(1)}, u32[]{:S(2)}, u32[]{:S(2)}) collective-permute-start(bf16[192,2048]{1,0:T(8,128)(2,1)S(1)} %get-tuple-element.54), channel_id=1, source_target_pairs={{0,12},{1,13},{2,14},{3,15},{4,8},{5,9},{6,10},{7,11},{8,4},{9,5},... | collective-permute-start | bytes 2359304 | tf_op jit(solution)/shard_map/ppermute | solution.py:43
  95.3 24.5 %collective-permute-start.25 = (bf16[512,1792]{1,0:T(8,128)(2,1)S(1)}, bf16[512,1792]{1,0:T(8,128)(2,1)S(1)}, u32[]{:S(2)}, u32[]{:S(2)}) collective-permute-start(bf16[512,1792]{1,0:T(8,128)(2,1)S(1)} %add_convert_fusion), channel_id=1, source_target_pairs={{0,96},{1,97},{2,98},{3,99},{4,100},{5,101},{6,102},{7,103},{8,104... | collective-permute-start | bytes 5505032 | tf_op jit(solution)/shard_map/ppermute | solution.py:43
  97.6 19.7 %collective-permute-start.24 = (bf16[512,1792]{1,0:T(8,128)(2,1)S(1)}, bf16[512,1792]{1,0:T(8,128)(2,1)S(1)}, u32[]{:S(2)}, u32[]{:S(2)}) collective-permute-start(bf16[512,1792]{1,0:T(8,128)(2,1)S(1)} %convolution_convert_fusion), channel_id=1, source_target_pairs={{0,16},{1,17},{2,18},{3,19},{4,20},{5,21},{6,22},{7,23},{8,24},{9,... | collective-permute-start | bytes 5505032 | tf_op jit(solution)/shard_map/ppermute | solution.py:43
  106.3 8.0 %copy-start.4 = (f32[96,96]{1,0:T(8,128)S(1)}, f32[96,96]{1,0:T(8,128)}, u32[]{:S(2)}) copy-start(f32[96,96]{1,0:T(8,128)} %constant.8.clone) | copy-start | bytes 110596
  106.3 7.9 %collective-permute-start.18 = (bf16[96,2048]{1,0:T(8,128)(2,1)S(1)}, bf16[96,2048]{1,0:T(8,128)(2,1)S(1)}, u32[]{:S(2)}, u32[]{:S(2)}) collective-permute-start(bf16[96,2048]{1,0:T(8,128)(2,1)S(1)} %pad_maximum_fusion.9), channel_id=1, source_target_pairs={{0,4},{1,5},{2,6},{3,7},{4,0},{5,1},{6,2},{7,3},{8,12},{9,13},{10,... | collective-permute-start | bytes 1179656 | tf_op jit(solution)/shard_map/ppermute | solution.py:43
  115.0 10.2 %collective-permute-start.19 = (bf16[48,2048]{1,0:T(8,128)(2,1)S(1)}, bf16[48,2048]{1,0:T(8,128)(2,1)S(1)}, u32[]{:S(2)}, u32[]{:S(2)}) collective-permute-start(bf16[48,2048]{1,0:T(8,128)(2,1)S(1)} %slice.130), channel_id=1, source_target_pairs={{0,3},{1,2},{2,1},{3,0},{4,7},{5,6},{6,5},{7,4},{8,11},{9,10},{10,... | collective-permute-start | bytes 589832 | tf_op jit(solution)/shard_map/ppermute | solution.py:43
  120.6 13.9 %collective-permute-start.26 = (bf16[256,1792]{1,0:T(8,128)(2,1)S(1)}, bf16[256,1792]{1,0:T(8,128)(2,1)S(1)}, u32[]{:S(2)}, u32[]{:S(2)}) collective-permute-start(bf16[256,1792]{1,0:T(8,128)(2,1)S(1)} %fusion.2), channel_id=1, source_target_pairs={{0,32},{1,33},{2,34},{3,35},{4,36},{5,37},{6,38},{7,39},{8,40},{9,... | collective-permute-start | bytes 2752520 | tf_op jit(solution)/shard_map/ppermute | solution.py:43
  125.3 4.4 %collective-permute-start.20 = (bf16[12,2048]{1,0:T(8,128)(2,1)S(1)}, bf16[12,2048]{1,0:T(8,128)(2,1)S(1)}, u32[]{:S(2)}, u32[]{:S(2)}) collective-permute-start(bf16[12,2048]{1,0:T(8,128)(2,1)S(1)} %get-tuple-element.75), channel_id=1, source_target_pairs={{0,128},{1,129},{2,130},{3,131},{4,132},{5,133},{6,134},{7,135},{8... | collective-permute-start | bytes 147464 | tf_op jit(solution)/shard_map/ppermute | solution.py:43
  125.8 5.7 %collective-permute-start.21 = (bf16[12,2048]{1,0:T(8,128)(2,1)S(1)}, bf16[12,2048]{1,0:T(8,128)(2,1)S(1)}, u32[]{:S(2)}, u32[]{:S(2)}) collective-permute-start(bf16[12,2048]{1,0:T(8,128)(2,1)S(1)} %get-tuple-element.74), channel_id=1, source_target_pairs={{0,1},{1,0},{2,3},{3,2},{4,5},{5,4},{6,7},{7,6},{8,9},{9,8},{10,11... | collective-permute-start | bytes 147464 | tf_op jit(solution)/shard_map/ppermute | solution.py:43
  125.9 7.2 %collective-permute-start.22 = (bf16[12,2048]{1,0:T(8,128)(2,1)S(1)}, bf16[12,2048]{1,0:T(8,128)(2,1)S(1)}, u32[]{:S(2)}, u32[]{:S(2)}) collective-permute-start(bf16[12,2048]{1,0:T(8,128)(2,1)S(1)} %get-tuple-element.73), channel_id=1, source_target_pairs={{0,129},{1,128},{2,131},{3,130},{4,133},{5,132},{6,135},{7,134},{8... | collective-permute-start | bytes 147464 | tf_op jit(solution)/shard_map/ppermute | solution.py:43

commit v3 on v2

--- a/solution.py
+++ b/solution.py
@@ -12,6 +12,7 @@
 BOTH = ("dp", "tensor")
 F32 = jnp.float32
 BF16 = jnp.bfloat16
+FIRST, SECOND = (0, 384), (384, 896)
 TILE = 256
 VMEM_LIMIT = 16 * 1024 * 1024
 VMEM = pl.BlockSpec(memory_space=pltpu.VMEM)
@@ -45,6 +46,10 @@
 
 def fence(*values):
     return lax.optimization_barrier(values)
+
+
+def after(value, *others):
+    return lax.optimization_barrier((value, *others))[0]
 
 
 def call(kernel, out_shape, in_specs, out_specs, scratch=(), cost=None):
@@ -179,8 +184,29 @@
     return call(stack_kernel, out, [ANY] * len(pieces), VMEM, [pltpu.SemaphoreType.DMA((len(pieces),))])(*pieces)
 
 
-def forward_kernel(near, away, mine, *refs):
-    pieces, (rows, theirs, own, par, sems) = refs[:-5], refs[-5:]
+def columns_of(chunk, hidden):
+    first, last = chunk
+    return [slice(first, last), slice(hidden + first, hidden + last)]
+
+
+def tiles_of(chunk, hidden):
+    to = 0
+    for span in columns_of(chunk, hidden):
+        for at in range(span.start, span.stop, TILE):
+            wide = min(TILE, span.stop - at)
+            yield slice(at, at + wide), slice(to, to + wide)
+            to += wide
+
+
+def products(rows, mine, theirs, span):
+    half = mine.shape[0]
+    return jnp.dot(rows[:, :half], mine[:, span], preferred_element_type=F32) + jnp.dot(
+        rows[:, half:], theirs[:, span], preferred_element_type=F32
+    )
+
+
+def first_kernel(near, away, mine, *refs):
+    pieces, (rows, theirs, kept, given, sems) = refs[:-5], refs[-5:]
     copies = []
     at = 0
     for n, piece in enumerate(pieces):
@@ -196,84 +222,100 @@
                 rows[to : to + part, :] = values[(2 * q + z) * part : (2 * q + z + 1) * part, :]
     for copy in copies:
         copy.wait()
-    group = own.shape[0]
-    half = mine.shape[0]
-    for at in range(0, mine.shape[1], TILE):
-        span = slice(at, at + TILE)
-        result = jnp.dot(rows[:, :half], mine[:, span], preferred_element_type=F32)
-        result += jnp.dot(rows[:, half:], theirs[:, span], preferred_element_type=F32)
-        own[:, span] = result[:group]
-        par[:, span] = result[group:].astype(BF16)
-
-
-def forward(near, away, mine, pieces):
+    for span, to in tiles_of(FIRST, mine.shape[1] // 2):
+        result = products(rows, mine, theirs, span)
+        kept[:, to] = result
+        given[:, to] = result.astype(BF16)
+
+
+def first_products(near, away, mine, pieces):
     group, features = near.shape
-    width = mine.shape[1]
+    width = 2 * (FIRST[1] - FIRST[0])
     outs = (
         pltpu.VMEM((2 * group, features), BF16),
         pltpu.VMEM(mine.shape, BF16),
-        pltpu.VMEM((group, width), F32),
-        pltpu.VMEM((group, width), BF16),
-    )
-    inputs, theirs, own, par = call(
-        forward_kernel,
+        pltpu.VMEM((2 * group, width), F32),
+        pltpu.VMEM((2 * group, width), BF16),
+    )
+    return call(
+        first_kernel,
         outs,
         [VMEM] * 3 + [ANY] * len(pieces),
         (VMEM,) * 4,
         [pltpu.SemaphoreType.DMA((len(pieces),))],
     )(near, away, mine, *pieces)
-    return inputs, (mine, theirs), own, par
-
-
-def gradient_kernel(own, sent, upstream, out):
-    hidden = upstream.shape[1]
-    stream = upstream[...].astype(F32)
-    gate = own[:, :hidden] + sent[:, :hidden].astype(F32)
-    up = own[:, hidden:] + sent[:, hidden:].astype(F32)
-    sigmoid = jax.nn.sigmoid(gate)
-    out[:, :hidden] = (stream * up * sigmoid * (1.0 + gate * (1.0 - sigmoid))).astype(BF16)
-    out[:, hidden:] = (stream * gate * sigmoid).astype(BF16)
-
-
-def gradient(own, sent, upstream):
-    return call(gradient_kernel, array(own.shape, BF16), [VMEM] * 3, VMEM)(own, sent, upstream)
-
-
-def backward_kernel(grad, mine, theirs, *refs):
-    half = grad.shape[0] // 2
-    if len(refs) == 3:
-        before, near, away = refs
-        near[:half] = before[:half]
-        away[:half] = before[half:]
+
+
+def second_kernel(rows, mine, theirs, kept, given):
+    for span, to in tiles_of(SECOND, mine.shape[1] // 2):
+        result = products(rows, mine, theirs, span)
+        kept[:, to] = result
+        given[:, to] = result.astype(BF16)
+
+
+def second_products(rows, mine, theirs):
+    shape = (rows.shape[0], 2 * (SECOND[1] - SECOND[0]))
+    outs = (pltpu.VMEM(shape, F32), pltpu.VMEM(shape, BF16))
+    return call(second_kernel, outs, [VMEM] * 3, (VMEM,) * 2)(rows, mine, theirs)
+
+
+def gradient_kernel(start, kept, sent, own_stream, other_stream, out):
+    rows, width = sent.shape[0] // 2, sent.shape[1] // 2
+    for z, stream in enumerate((own_stream, other_stream)):
+        held = slice(z * rows, (z + 1) * rows)
+        came = slice((1 - z) * rows, (2 - z) * rows)
+        upstream = stream[:, start : start + width].astype(F32)
+        gate = kept[held, :width] + sent[came, :width].astype(F32)
+        up = kept[held, width:] + sent[came, width:].astype(F32)
+        sigmoid = jax.nn.sigmoid(gate)
+        out[held, :width] = (upstream * up * sigmoid * (1.0 + gate * (1.0 - sigmoid))).astype(BF16)
+        out[held, width:] = (upstream * gate * sigmoid).astype(BF16)
+
+
+def gradient(chunk, kept, sent, own_stream, other_stream):
+    return call(functools.partial(gradient_kernel, chunk[0]), array(sent.shape, BF16), [VMEM] * 4, VMEM)(
+        kept, sent, own_stream, other_stream
+    )
+
+
+def backward_kernel(side, first, second, mine, theirs, out, grads):
+    group, rows = first.shape[0] // 2, first.shape[0] // 4
+    for chunk, part in ((FIRST, first), (SECOND, second)):
+        width = chunk[1] - chunk[0]
+        for m, span in enumerate(columns_of(chunk, mine.shape[1] // 2)):
+            for z in range(2):
+                at = z * group + side * rows
+                grads[z * rows : (z + 1) * rows, span] = part[at : at + rows, m * width : (m + 1) * width]
     for k in range(8):
-        span = slice(256 * k, 256 * (k + 1))
         held = (mine, theirs)[k // 4][256 * (k % 4) : 256 * (k % 4 + 1)]
-        result = lax.dot_general(
-            grad[...], held, (((1,), (1,)), ((), ())), preferred_element_type=F32
+        out[:, 256 * k : 256 * (k + 1)] = lax.dot_general(
+            grads[...], held, (((1,), (1,)), ((), ())), preferred_element_type=F32
         ).astype(BF16)
-        if len(refs) == 3:
-            near[half:, span] = result[:half]
-            away[half:, span] = result[half:]
-        else:
-            refs[0][:, span] = result
-
-
-def backward(grad, held, *before):
-    out = array((grad.shape[0], 2 * held[0].shape[0]), BF16)
-    outs, specs = ((out, out), (VMEM, VMEM)) if before else (out, VMEM)
-    return call(backward_kernel, outs, [VMEM] * (3 + len(before)), specs)(grad, *held, *before)
-
-
-def finish_kernel(scale, total, last, gate, up):
-    width = gate.shape[1]
-    for out, span in ((gate, slice(0, width)), (up, slice(width, 2 * width))):
-        out[...] = (total[:, span] + last[:, span].astype(F32)) * scale
-
-
-def finish(total, last, scale):
-    rows, width = total.shape
-    out = array((rows, width // 2), F32)
-    return call(functools.partial(finish_kernel, scale), (out, out), [VMEM, VMEM], (VMEM, VMEM))(total, last)
+
+
+def backward(side, first, second, mine, theirs):
+    rows, width = first.shape[0] // 2, mine.shape[1]
+    return call(
+        functools.partial(backward_kernel, side),
+        array((rows, 2 * mine.shape[0]), BF16),
+        [VMEM] * 4,
+        VMEM,
+        [pltpu.VMEM((rows, width), BF16)],
+    )(first, second, mine, theirs)
+
+
+def finish_kernel(scale, first, second, first_last, second_last, gate, up):
+    hidden = gate.shape[1]
+    for chunk, total, last in ((FIRST, first, first_last), (SECOND, second, second_last)):
+        width = chunk[1] - chunk[0]
+        for m, out in enumerate((gate, up)):
+            at = slice(m * width, (m + 1) * width)
+            out[:, chunk[0] : chunk[1]] = (total[:, at] + last[:, at].astype(F32)) * scale
+
+
+def finish(sums, lasts, scale):
+    out = array((sums[0].shape[0], SECOND[1]), F32)
+    return call(functools.partial(finish_kernel, scale), (out, out), [VMEM] * 4, (VMEM, VMEM))(*sums, *lasts)
 
 
 def add(*values):
@@ -294,74 +336,93 @@
     shard = join(gate_weight, up_weight)
     from_a = send(shard, Y_A)
     from_b = send(shard, Y_B)
-    theirs = [send(shard, TO_CORE)]
 
     saved_codes, saved_scales, _ = fence(saved_codes, saved_scales, shard)
     kept, given = dequantize(saved_codes, saved_scales)
     two = jnp.concatenate([kept, send(given, TO_ZL), send(kept, ZH_A), send(given, TO_ZL_ZH_A)], axis=0)
-    (two,) = fence(two)
-    arrived, from_a, from_b, theirs[0] = fence(send(two, ZH_B), from_a, from_b, theirs[0])
+    two, shown = fence(two, shard)
+    theirs = [send(shown, TO_CORE)]
+    arrived = after(send(two, ZH_B), from_a)
     four = jnp.concatenate([two, arrived], axis=0)
     slab = jnp.dot(by_group.astype(BF16), four, preferred_element_type=F32).astype(BF16)
-    slab, from_a = fence(slab, from_a)
+    (slab,) = fence(slab)
     far = send(from_a, Y_B)
-    near = jnp.concatenate([slab, send(slab, X_A)], axis=0)
+    arrived, from_b, theirs[0] = fence(send(slab, X_A), from_b, theirs[0])
+    near = jnp.concatenate([slab, arrived], axis=0)
     (near,) = fence(near)
     away = send(near, X_B)
 
-    from_a, from_b, _ = fence(from_a, from_b, near)
-    part = shard.shape[0] // 2
-    theirs += [send(piece[at : at + part], TO_CORE) for piece in (from_a, from_b) for at in (0, part)]
+    both = stack(after(from_a, near), from_b)
+    theirs += [send(both[at : at + 192], TO_CORE) for at in range(0, both.shape[0], 192)]
     mine = stack(shard, from_a, from_b, far)
-    far, mine = fence(far, mine)
-    theirs.append(send(far, TO_CORE))
+    theirs.append(send(after(far, mine), TO_CORE))
+
     upstream = arrange(hidden_grad, rows)
-
-    inputs, held, own, par = forward(near, away, mine, theirs)
-    sent = send(par, TO_ZL)
-
-    grad = gradient(own, sent, upstream)
-    other = send(grad, TO_ZL)
-    own_back = backward(grad, held)
-    other, own_back = fence(other, own_back)
-
-    def product(first, last):
-        both = jnp.concatenate([grad, other], axis=0)
+    near, away, other_upstream = fence(near, away, send(upstream, TO_ZL))
+
+    inputs, theirs, kept_first, given = first_products(near, away, mine, theirs)
+    sent_first = send(given, TO_ZL)
+    kept_second, given = second_products(inputs, mine, theirs)
+    sent_second = send(given, TO_ZL)
+    sent_first = after(sent_first, kept_second)
+    half, part = group // 2, group // 4
+
+    def product(first, last, grad):
         return lax.dot_general(
-            inputs[:, first:last], both, (((0,), (0,)), ((), ())), preferred_element_type=F32
+            inputs[:, first:last], grad, (((0,), (0,)), ((), ())), preferred_element_type=F32
         )
 
-    given = product(1536, 2048).astype(BF16)
-    given, other = fence(given, other)
-    shown_high = send(given, TO_CORE)
-    kept, passed = backward(other, held, own_back)
-    arrived = send(passed, X_B)
-    shown_high, other, _ = fence(shown_high, other, kept)
-    passed = add(product(512, 1024), shown_high).astype(BF16)
-    from_b = send(passed, Y_B)
-    other, _ = fence(other, passed)
-    shown_low = send(product(1024, 1536).astype(BF16), TO_CORE)
-
-    back = add(kept, arrived)
-    half, part = group // 2, group // 4
+    def show(value):
+        (value,) = fence(value.astype(BF16))
+        pieces = [send(value[at : at + 128], TO_CORE) for at in range(0, value.shape[0], 128)]
+        return jnp.concatenate(pieces, axis=0)
+
+    first = gradient(FIRST, kept_first, sent_first, upstream, other_upstream)
+    high = show(product(1536, 2048, first))
+    passed = add(product(512, 1024, first), high).astype(BF16)
+    first_b = send(passed, Y_B)
+
+    second = gradient(SECOND, kept_second, sent_second, upstream, other_upstream)
+    back_away = backward(1, first, second, mine, theirs)
+    back_sent = send(back_away, X_B)
+    back = backward(0, first, after(second, first_b, back_away), mine, theirs)
+    first_low = send(product(1024, 1536, after(first, back_away)).astype(BF16), TO_CORE)
+    second = after(second, back)
+    high = show(product(1536, 2048, second))
+    passed = add(product(512, 1024, second), high).astype(BF16)
+    second_b = send(passed, Y_B)
+    low = product(1024, 1536, after(second, passed)).astype(BF16)
+    second_low = send(low, TO_CORE)
+    back_sent = after(back_sent, low)
+
+    def second_sum(grad, shown, from_b):
+        return add(product(256, 512, grad), shown[256:], from_b[256:]).astype(BF16)
+
+    def own_sum(grad, shown, from_b):
+        return add(product(0, 256, grad), shown[:256], from_b[:256])
+
+    back = add(back, back_sent)
     passed = jnp.concatenate([back[part:half], back[half + part :]], axis=0).astype(BF16)
     kept = jnp.concatenate([back[:part], back[half : half + part]], axis=0)
+    arrived = send(passed, X_A)
+    first_last = send(second_sum(first, first_low, first_b), Y_A)
     four = jnp.dot(
         by_group.T.astype(np.float32),
-        add(kept, send(passed, X_A)),
+        add(kept, arrived),
         preferred_element_type=F32,
         precision=lax.Precision.HIGHEST,
     )
-    half = 4 * rows
-    two = add(four[:half], send(four[half:].astype(BF16), ZH_B))
-    kept, *passed = (two[at : at + rows] for at in range(0, half, rows))
+    part = 4 * rows
+    passed = second_sum(second, second_low, second_b)
+    arrived = after(send(four[part:].astype(BF16), ZH_B), first_last, passed)
+    second_last = send(passed, Y_A)
+    two = add(four[:part], arrived)
+    kept, *passed = (two[at : at + rows] for at in range(0, part, rows))
     arrived = [send(v.astype(BF16), pairs) for v, pairs in zip(passed, (TO_ZL, ZH_A, TO_ZL_ZH_A))]
+    arrived[0] = after(arrived[0], second_last)
     input_grad = restore(kept, *arrived)
-
-    passed = add(product(256, 512), shown_low[256:], from_b[256:]).astype(BF16)
-    last = send(passed, Y_A)
-    total = add(product(0, 256), shown_low[:256], from_b[:256])
-    gate_grad, up_grad = finish(total, last, 1.0 / group)
+    sums = [own_sum(first, first_low, first_b), own_sum(second, second_low, second_b)]
+    gate_grad, up_grad = finish(sums, [first_last, second_last], 1.0 / group)
     return input_grad, gate_grad, up_grad
 
 

time: 137 us -> 127 us (0.927)
  waiting for transfers between devices: 83.7 us -> 50.5 us
  starting transfers between devices: 29.5 us -> 51 us
    ppermute x27 -> x37, waiting for transfers between devices: 83.7 us -> 50.5 us  [send(): return lax.ppermute(value, BOTH, pairs)]
    ppermute x27 -> x37, starting transfers between devices: 29.5 us -> 51 us  [send(): return lax.ppermute(value, BOTH, pairs)]
    dot_general x6 -> x11, matrix products: 5.71 us -> 6.52 us  [the longest x10 5.74 us: product(): lax.dot_general(inputs[:, first:last], grad, (((0,), (0,)), ((), ())), pr...]
    pallas_call x5 -> x7, Pallas kernels: 11.5 us -> 12.2 us  [the longest x2 5.05 us: backward(): call(functools.partial(backward_kernel, side), array((rows, 2 * mine.shap...]
  transfers between devices with their start and end apart: 27 -> 37, of which waited for: 18 -> 16; matrix products, arithmetic and copies ran while one was open for 4% -> 6% of each run, Pallas kernels for 5% -> 9%
where the time goes in v3:
time: 127 us; the launch traced here: 126 us
  starting transfers between devices  51 us (40%)
  waiting for transfers between devices  50.5 us (40%)
  Pallas kernels  15.9 us (13%)
  matrix products  6.99 us (6%)
    ppermute x37, starting transfers between devices, send(): return lax.ppermute(value, BOTH, pairs)  51 us
    ppermute x37, waiting for transfers between devices, send(): return lax.ppermute(value, BOTH, pairs)  50.5 us
    dot_general x10, matrix products, product(): lax.dot_general(inputs[:, first:last], grad, (((0,), (0,)), ((), ())), pr...  5.74 us
    pallas_call x2, Pallas kernels, backward(): call(functools.partial(backward_kernel, side), array((rows, 2 * mine.shap...  5.05 us
    pallas_call x1, Pallas kernels, first_products(): call(first_kernel, outs, [VMEM] * 3 + [ANY] * len(pieces), (VMEM,) * 4, [...  3.15 us
  transfers between devices with their start and end apart: 37, of which 16 were waited for; matrix products, arithmetic and copies ran while one was open for 6% of the time, Pallas kernels for 9%

profile of v3, /device:TPU:64, one launch (start us, length us, event | category | flops | bytes accessed | tf_op | source)
XLA Modules:
  0.0 126.5 jit_solution(2073584178960401553)
XLA Ops:
  0.7 1.2 shard_map.103.refs_0_
  1.9 1.7 %collective-permute-start.4 = (bf16[256,1792]{1,0:T(8,128)(2,1)S(1)}, bf16[256,1792]{1,0:T(8,128)(2,1)S(1)}, u32[]{:S(2)}, u32[]{:S(2)}) collective-permute-start(bf16[256,1792]{1,0:T(8,128)(2,1)S(1)} %shard_map.103.refs_0_), channel_id=1, source_target_pairs={{0,32},{1,33},{2,34},{3,35},{4,36},{5,37},{6,38},{7,39},{8,40},{9,... | collective-permute-start | bytes 2752520 | tf_op jit(solution)/shard_map/ppermute | solution.py:44
  3.8 3.4 %collective-permute-start.2 = (bf16[12,2048]{1,0:T(8,128)(2,1)S(1)}, bf16[12,2048]{1,0:T(8,128)(2,1)S(1)}, u32[]{:S(2)}, u32[]{:S(2)}) collective-permute-start(bf16[12,2048]{1,0:T(8,128)(2,1)S(1)} %get-tuple-element.37), channel_id=1, source_target_pairs={{0,129},{1,128},{2,131},{3,130},{4,133},{5,132},{6,135},{7,134},{8... | collective-permute-start | bytes 147464 | tf_op jit(solution)/shard_map/ppermute | solution.py:44
  7.2 1.0 collective-permute-start
  8.2 2.2 %collective-permute-start.6 = (bf16[256,1792]{1,0:T(8,128)(2,1)S(1)}, bf16[256,1792]{1,0:T(8,128)(2,1)S(1)}, u32[]{:S(2)}, u32[]{:S(2)}) collective-permute-start(bf16[256,1792]{1,0:T(8,128)(2,1)S(1)} %shard_map.103.refs_0_), channel_id=1, source_target_pairs={{0,96},{1,97},{2,98},{3,99},{4,100},{5,101},{6,102},{7,103},{8,104... | collective-permute-start | bytes 2752520 | tf_op jit(solution)/shard_map/ppermute | solution.py:44
  10.4 0.7 collective-permute-done.2
  11.1 0.8 collective-permute-done
  11.9 4.7 %collective-permute-start.7 = (bf16[256,1792]{1,0:T(8,128)(2,1)S(1)}, bf16[256,1792]{1,0:T(8,128)(2,1)S(1)}, u32[]{:S(2)}, u32[]{:S(2)}) collective-permute-start(bf16[256,1792]{1,0:T(8,128)(2,1)S(1)} %shard_map.103.refs_0_), channel_id=1, source_target_pairs={{0,16},{1,17},{2,18},{3,19},{4,20},{5,21},{6,22},{7,23},{8,24},{9,... | collective-permute-start | bytes 2752520 | tf_op jit(solution)/shard_map/ppermute | solution.py:44
  16.6 1.6 %collective-permute-start.3 = (bf16[48,2048]{1,0:T(8,128)(2,1)S(1)}, bf16[48,2048]{1,0:T(8,128)(2,1)S(1)}, u32[]{:S(2)}, u32[]{:S(2)}) collective-permute-start(bf16[48,2048]{1,0:T(8,128)(2,1)S(1)} %pad_maximum_fusion.2), channel_id=1, source_target_pairs={{0,3},{1,2},{2,1},{3,0},{4,7},{5,6},{6,5},{7,4},{8,11},{9,10},{10,... | collective-permute-start | bytes 589832 | tf_op jit(solution)/shard_map/ppermute | solution.py:44
  18.3 0.5 collective-permute-done.4.refs_1_.refs_0_
  18.8 5.3 %collective-permute-start.10 = (bf16[256,1792]{1,0:T(8,128)(2,1)S(1)}, bf16[256,1792]{1,0:T(8,128)(2,1)S(1)}, u32[]{:S(2)}, u32[]{:S(2)}) collective-permute-start(bf16[256,1792]{1,0:T(8,128)(2,1)S(1)} %collective-permute-done.4.refs_1_.refs_0_), channel_id=1, source_target_pairs={{0,96},{1,97},{2,98},{3,99},{4,100},{5,101},{6,102},{7,103},{8,104... | collective-permute-start | bytes 2752520 | tf_op jit(solution)/shard_map/ppermute | solution.py:44
  24.7 1.6 %collective-permute-start.5 = (bf16[96,2048]{1,0:T(8,128)(2,1)S(1)}, bf16[96,2048]{1,0:T(8,128)(2,1)S(1)}, u32[]{:S(2)}, u32[]{:S(2)}) collective-permute-start(bf16[96,2048]{1,0:T(8,128)(2,1)S(1)} %fusion.1), channel_id=1, source_target_pairs={{0,4},{1,5},{2,6},{3,7},{4,0},{5,1},{6,2},{7,3},{8,12},{9,13},{10,... | collective-permute-start | bytes 1179656 | tf_op jit(solution)/shard_map/ppermute | solution.py:44
  26.6 2.0 %collective-permute-start.9 = (bf16[192,896]{1,0:T(8,128)(2,1)S(1)}, bf16[192,896]{1,0:T(8,128)(2,1)S(1)}, u32[]{:S(2)}, u32[]{:S(2)}) collective-permute-start(bf16[192,896]{1,0:T(8,128)(2,1)S(1)} %shard_map.105.own_stream), channel_id=1, source_target_pairs={{0,128},{1,129},{2,130},{3,131},{4,132},{5,133},{6,134},{7,135},{8... | collective-permute-start | bytes 1032200 | tf_op jit(solution)/shard_map/ppermute | solution.py:44
  28.7 3.9 %collective-permute-done.5 = bf16[96,2048]{1,0:T(8,128)(2,1)S(1)} collective-permute-done((bf16[96,2048]{1,0:T(8,128)(2,1)S(1)}, bf16[96,2048]{1,0:T(8,128)(2,1)S(1)}, u32[]{:S(2)}, u32[]{:S(2)}) %collective-permute-start.5) | collective-permute-done | bytes 393248 | tf_op jit(solution)/shard_map/ppermute | solution.py:44
  32.7 2.8 %collective-permute-start.8 = (bf16[192,2048]{1,0:T(8,128)(2,1)S(1)}, bf16[192,2048]{1,0:T(8,128)(2,1)S(1)}, u32[]{:S(2)}, u32[]{:S(2)}) collective-permute-start(bf16[192,2048]{1,0:T(8,128)(2,1)S(1)} %pad_maximum_fusion.near), channel_id=1, source_target_pairs={{0,12},{1,13},{2,14},{3,15},{4,8},{5,9},{6,10},{7,11},{8,4},{9,5},... | collective-permute-start | bytes 2359304 | tf_op jit(solution)/shard_map/ppermute | solution.py:44
  36.0 0.9 shard_map.106.mine
  37.1 0.6 collective-permute-start.12
  37.9 0.5 collective-permute-start.13
  38.4 7.6 %collective-permute-done.8.away = bf16[192,2048]{1,0:T(8,128)(2,1)S(1)} collective-permute-done((bf16[192,2048]{1,0:T(8,128)(2,1)S(1)}, bf16[192,2048]{1,0:T(8,128)(2,1)S(1)}, u32[]{:S(2)}, u32[]{:S(2)}) %collective-permute-start.8) | collective-permute-done | bytes 786464 | tf_op jit(solution)/shard_map/ppermute | solution.py:44
  46.0 3.2 %shard_map.108 = (bf16[384,2048]{1,0:T(8,128)(2,1)S(1)}, bf16[1024,1792]{1,0:T(8,128)(2,1)S(1)}, f32[384,768]{1,0:T(8,128)S(1)}, bf16[384,768]{1,0:T(8,128)(2,1)S(1)}) custom-call(bf16[192,2048]{1,0:T(8,128)(2,1)S(1)} %pad_maximum_fusion.near, bf16[192,2048]{1,0:T(8,128)(2,1)S(1)} %collective-permute-done.8.away, bf16[1024,1792]{1,0:T(8,128)(2,1)S(1)} %shard_map.106.mine, ...), custom_call_target="tpu_custom_call" | custom-call | tf_op jit(solution)/shard_map/pallas_call | solution.py:240
  49.1 2.2 %collective-permute-start.15 = (bf16[384,768]{1,0:T(8,128)(2,1)S(1)}, bf16[384,768]{1,0:T(8,128)(2,1)S(1)}, u32[]{:S(2)}, u32[]{:S(2)}) collective-permute-start(bf16[384,768]{1,0:T(8,128)(2,1)S(1)} %get-tuple-element.49), channel_id=1, source_target_pairs={{0,128},{1,129},{2,130},{3,131},{4,132},{5,133},{6,134},{7,135},{8... | collective-permute-start | bytes 1769480 | tf_op jit(solution)/shard_map/ppermute | solution.py:44
  51.4 1.8 %shard_map.109 = (f32[384,1024]{1,0:T(8,128)S(1)}, bf16[384,1024]{1,0:T(8,128)(2,1)S(1)}) custom-call(bf16[384,2048]{1,0:T(8,128)(2,1)S(1)} %get-tuple-element.50.rows, bf16[1024,1792]{1,0:T(8,128)(2,1)S(1)} %shard_map.106.mine, bf16[1024,1792]{1,0:T(8,128)(2,1)S(1)} %get-tuple-element.51.theirs), custom_call_target="tpu_custom_call" | custom-call | tf_op jit(solution)/shard_map/pallas_call | solution.py:259
  53.3 12.4 %collective-permute-done.15.sent = bf16[384,768]{1,0:T(8,128)(2,1)S(1)} collective-permute-done((bf16[384,768]{1,0:T(8,128)(2,1)S(1)}, bf16[384,768]{1,0:T(8,128)(2,1)S(1)}, u32[]{:S(2)}, u32[]{:S(2)}) %collective-permute-start.15) | collective-permute-done | bytes 589856 | tf_op jit(solution)/shard_map/ppermute | solution.py:44
  66.0 0.6 convolution_convert_fusion.3
  66.8 0.5 collective-permute-start.20
  69.1 0.6 add_convert_fusion.1
  69.7 1.8 %collective-permute-start.21 = (bf16[512,768]{1,0:T(8,128)(2,1)S(1)}, bf16[512,768]{1,0:T(8,128)(2,1)S(1)}, u32[]{:S(2)}, u32[]{:S(2)}) collective-permute-start(bf16[512,768]{1,0:T(8,128)(2,1)S(1)} %add_convert_fusion.1), channel_id=1, source_target_pairs={{0,96},{1,97},{2,98},{3,99},{4,100},{5,101},{6,102},{7,103},{8,104... | collective-permute-start | bytes 2359304 | tf_op jit(solution)/shard_map/ppermute | solution.py:44
  71.5 6.5 %collective-permute-done.16.sent = bf16[384,1024]{1,0:T(8,128)(2,1)S(1)} collective-permute-done((bf16[384,1024]{1,0:T(8,128)(2,1)S(1)}, bf16[384,1024]{1,0:T(8,128)(2,1)S(1)}, u32[]{:S(2)}, u32[]{:S(2)}) %collective-permute-start.16) | collective-permute-done | bytes 786464 | tf_op jit(solution)/shard_map/ppermute | solution.py:44
  78.5 2.5 %shard_map.112 = bf16[192,2048]{1,0:T(8,128)(2,1)S(1)} custom-call(bf16[384,768]{1,0:T(8,128)(2,1)S(1)} %shard_map.110.first, bf16[384,1024]{1,0:T(8,128)(2,1)S(1)} %shard_map.111.second, bf16[1024,1792]{1,0:T(8,128)(2,1)S(1)} %shard_map.106.mine, bf16[1024,1792]{1,0:T(8,128)(2,1)S(1)} %get-tuple-element.51.theirs), custom_call_target="tpu_custom_call" | custom-call | tf_op jit(solution)/shard_map/pallas_call | solution.py:298
  81.0 0.6 convolution_convert_fusion.2
  81.7 2.8 %collective-permute-start.22 = (bf16[192,2048]{1,0:T(8,128)(2,1)S(1)}, bf16[192,2048]{1,0:T(8,128)(2,1)S(1)}, u32[]{:S(2)}, u32[]{:S(2)}) collective-permute-start(bf16[192,2048]{1,0:T(8,128)(2,1)S(1)} %shard_map.112), channel_id=1, source_target_pairs={{0,12},{1,13},{2,14},{3,15},{4,8},{5,9},{6,10},{7,11},{8,4},{9,5},... | collective-permute-start | bytes 2359304 | tf_op jit(solution)/shard_map/ppermute | solution.py:44
  84.5 2.5 %shard_map.113 = bf16[192,2048]{1,0:T(8,128)(2,1)S(1)} custom-call(bf16[384,768]{1,0:T(8,128)(2,1)S(1)} %shard_map.110.first, bf16[384,1024]{1,0:T(8,128)(2,1)S(1)} %shard_map.111.second, bf16[1024,1792]{1,0:T(8,128)(2,1)S(1)} %shard_map.106.mine, bf16[1024,1792]{1,0:T(8,128)(2,1)S(1)} %get-tuple-element.51.theirs), custom_call_target="tpu_custom_call" | custom-call | tf_op jit(solution)/shard_map/pallas_call | solution.py:298
  87.1 0.7 convolution_convert_fusion.1
  88.0 0.5 collective-permute-start.26
  90.6 0.7 add_convert_fusion
  91.4 3.0 %collective-permute-start.32 = (bf16[512,1024]{1,0:T(8,128)(2,1)S(1)}, bf16[512,1024]{1,0:T(8,128)(2,1)S(1)}, u32[]{:S(2)}, u32[]{:S(2)}) collective-permute-start(bf16[512,1024]{1,0:T(8,128)(2,1)S(1)} %add_convert_fusion), channel_id=1, source_target_pairs={{0,96},{1,97},{2,98},{3,99},{4,100},{5,101},{6,102},{7,103},{8,104... | collective-permute-start | bytes 3145736 | tf_op jit(solution)/shard_map/ppermute | solution.py:44
  94.3 0.7 convolution_convert_fusion
  95.9 7.5 %collective-permute-done.27 = bf16[96,2048]{1,0:T(8,128)(2,1)S(1)} collective-permute-done((bf16[96,2048]{1,0:T(8,128)(2,1)S(1)}, bf16[96,2048]{1,0:T(8,128)(2,1)S(1)}, u32[]{:S(2)}, u32[]{:S(2)}) %collective-permute-start.27) | collective-permute-done | bytes 393248 | tf_op jit(solution)/shard_map/ppermute | solution.py:44
  103.4 0.8 fusion.8
  104.3 6.6 %collective-permute-start.28 = (bf16[48,2048]{1,0:T(8,128)(2,1)S(1)}, bf16[48,2048]{1,0:T(8,128)(2,1)S(1)}, u32[]{:S(2)}, u32[]{:S(2)}) collective-permute-start(bf16[48,2048]{1,0:T(8,128)(2,1)S(1)} %slice.208), channel_id=1, source_target_pairs={{0,3},{1,2},{2,1},{3,0},{4,7},{5,6},{6,5},{7,4},{8,11},{9,10},{10,... | collective-permute-start | bytes 589832 | tf_op jit(solution)/shard_map/ppermute | solution.py:44
  110.8 0.5 fusion.4
  111.4 5.1 %collective-permute-done.28 = bf16[48,2048]{1,0:T(8,128)(2,1)S(1)} collective-permute-done((bf16[48,2048]{1,0:T(8,128)(2,1)S(1)}, bf16[48,2048]{1,0:T(8,128)(2,1)S(1)}, u32[]{:S(2)}, u32[]{:S(2)}) %collective-permute-start.28) | collective-permute-done | bytes 196640 | tf_op jit(solution)/shard_map/ppermute | solution.py:44
  116.7 1.1 collective-permute-start.36
  117.8 2.4 %collective-permute-start.35 = (bf16[12,2048]{1,0:T(8,128)(2,1)S(1)}, bf16[12,2048]{1,0:T(8,128)(2,1)S(1)}, u32[]{:S(2)}, u32[]{:S(2)}) collective-permute-start(bf16[12,2048]{1,0:T(8,128)(2,1)S(1)} %get-tuple-element.84), channel_id=1, source_target_pairs={{0,1},{1,0},{2,3},{3,2},{4,5},{5,4},{6,7},{7,6},{8,9},{9,8},{10,11... | collective-permute-start | bytes 147464 | tf_op jit(solution)/shard_map/ppermute | solution.py:44
  120.2 0.5 fusion.2.second
  120.7 3.6 %collective-permute-done.33.from_zl = bf16[12,2048]{1,0:T(8,128)(2,1)S(1)} collective-permute-done((bf16[12,2048]{1,0:T(8,128)(2,1)S(1)}, bf16[12,2048]{1,0:T(8,128)(2,1)S(1)}, u32[]{:S(2)}, u32[]{:S(2)}) %collective-permute-start.33) | collective-permute-done | bytes 49184 | tf_op jit(solution)/shard_map/ppermute | solution.py:44
  124.4 1.4 %shard_map.115 = (f32[256,896]{1,0:T(8,128)}, f32[256,896]{1,0:T(8,128)}) custom-call(f32[256,768]{1,0:T(8,128)S(1)} %fusion.6.first, f32[256,1024]{1,0:T(8,128)S(1)} %fusion.2.second, bf16[256,768]{1,0:T(8,128)(2,1)S(1)} %collective-permute-done.30.first_last, bf16[256,1024]{1,0:T(8,128)(2,1)S(1)} %collective-permute-done.34.second_last), custom_call_target="tpu_custom_call" | custom-call | tf_op jit(solution)/shard_map/pallas_call | solution.py:318
  125.8 0.7 shard_map.114
  (80 shorter events, 8.6 us)
Async XLA Ops:
  0.6 23.5 %copy-start.5 = (bf16[96,48]{1,0:T(8,128)(2,1)S(1)}, bf16[96,48]{1,0:T(8,128)(2,1)}, u32[]{:S(2)}) copy-start(bf16[96,48]{1,0:T(8,128)(2,1)} %constant.11) | copy-start | bytes 27652
  0.6 23.9 %copy-start.6 = (bf16[96,48]{1,0:T(8,128)(2,1)S(1)}, bf16[96,48]{1,0:T(8,128)(2,1)}, u32[]{:S(2)}) copy-start(bf16[96,48]{1,0:T(8,128)(2,1)} %constant.12) | copy-start | bytes 27652
  0.7 2.9 %copy-start.3 = (bf16[12,32]{1,0:T(8,128)(2,1)S(1)}, bf16[12,32]{1,0:T(8,128)(2,1)}, u32[]{:S(2)}) copy-start(bf16[12,32]{1,0:T(8,128)(2,1)} %scales) | copy-start | bytes 2308
  0.7 2.9 %copy-start.1 = (bf16[12,4096]{1,0:T(8,128)(2,1)S(1)}, bf16[12,4096]{1,0:T(8,128)(2,1)}, u32[]{:S(2)}) copy-start(bf16[12,4096]{1,0:T(8,128)(2,1)} %codes) | copy-start | bytes 294916
  1.9 24.4 %copy-start = (bf16[192,896]{1,0:T(8,128)(2,1)S(1)}, bf16[192,896]{1,0:T(8,128)(2,1)}, u32[]{:S(2)}) copy-start(bf16[192,896]{1,0:T(8,128)(2,1)} %values.1) | copy-start | bytes 1032196
  1.9 24.4 %copy-start.2 = (s32[32,1,192]{2,1,0:T(1,128)S(1)}, s32[32,1,192]{2,1,0:T(1,128)}, u32[]{:S(2)}) copy-start(s32[32,1,192]{2,1,0:T(1,128)} %constant.7.clone.table) | copy-start | bytes 73732
  1.9 16.8 %collective-permute-start.4 = (bf16[256,1792]{1,0:T(8,128)(2,1)S(1)}, bf16[256,1792]{1,0:T(8,128)(2,1)S(1)}, u32[]{:S(2)}, u32[]{:S(2)}) collective-permute-start(bf16[256,1792]{1,0:T(8,128)(2,1)S(1)} %shard_map.103.refs_0_), channel_id=1, source_target_pairs={{0,32},{1,33},{2,34},{3,35},{4,36},{5,37},{6,38},{7,39},{8,40},{9,... | collective-permute-start | bytes 2752520 | tf_op jit(solution)/shard_map/ppermute | solution.py:44
  3.7 6.7 %collective-permute-start.1 = (bf16[12,2048]{1,0:T(8,128)(2,1)S(1)}, bf16[12,2048]{1,0:T(8,128)(2,1)S(1)}, u32[]{:S(2)}, u32[]{:S(2)}) collective-permute-start(bf16[12,2048]{1,0:T(8,128)(2,1)S(1)} %get-tuple-element.36), channel_id=1, source_target_pairs={{0,1},{1,0},{2,3},{3,2},{4,5},{5,4},{6,7},{7,6},{8,9},{9,8},{10,11... | collective-permute-start | bytes 147464 | tf_op jit(solution)/shard_map/ppermute | solution.py:44
  3.8 7.3 %collective-permute-start.2 = (bf16[12,2048]{1,0:T(8,128)(2,1)S(1)}, bf16[12,2048]{1,0:T(8,128)(2,1)S(1)}, u32[]{:S(2)}, u32[]{:S(2)}) collective-permute-start(bf16[12,2048]{1,0:T(8,128)(2,1)S(1)} %get-tuple-element.37), channel_id=1, source_target_pairs={{0,129},{1,128},{2,131},{3,130},{4,133},{5,132},{6,135},{7,134},{8... | collective-permute-start | bytes 147464 | tf_op jit(solution)/shard_map/ppermute | solution.py:44
  7.2 4.7 %collective-permute-start = (bf16[12,2048]{1,0:T(8,128)(2,1)S(1)}, bf16[12,2048]{1,0:T(8,128)(2,1)S(1)}, u32[]{:S(2)}, u32[]{:S(2)}) collective-permute-start(bf16[12,2048]{1,0:T(8,128)(2,1)S(1)} %get-tuple-element.37), channel_id=1, source_target_pairs={{0,128},{1,129},{2,130},{3,131},{4,132},{5,133},{6,134},{7,135},{8... | collective-permute-start | bytes 147464 | tf_op jit(solution)/shard_map/ppermute | solution.py:44
  8.2 20.5 %collective-permute-start.6 = (bf16[256,1792]{1,0:T(8,128)(2,1)S(1)}, bf16[256,1792]{1,0:T(8,128)(2,1)S(1)}, u32[]{:S(2)}, u32[]{:S(2)}) collective-permute-start(bf16[256,1792]{1,0:T(8,128)(2,1)S(1)} %shard_map.103.refs_0_), channel_id=1, source_target_pairs={{0,96},{1,97},{2,98},{3,99},{4,100},{5,101},{6,102},{7,103},{8,104... | collective-permute-start | bytes 2752520 | tf_op jit(solution)/shard_map/ppermute | solution.py:44
  11.9 16.8 %collective-permute-start.7 = (bf16[256,1792]{1,0:T(8,128)(2,1)S(1)}, bf16[256,1792]{1,0:T(8,128)(2,1)S(1)}, u32[]{:S(2)}, u32[]{:S(2)}) collective-permute-start(bf16[256,1792]{1,0:T(8,128)(2,1)S(1)} %shard_map.103.refs_0_), channel_id=1, source_target_pairs={{0,16},{1,17},{2,18},{3,19},{4,20},{5,21},{6,22},{7,23},{8,24},{9,... | collective-permute-start | bytes 2752520 | tf_op jit(solution)/shard_map/ppermute | solution.py:44
  16.6 7.9 %collective-permute-start.3 = (bf16[48,2048]{1,0:T(8,128)(2,1)S(1)}, bf16[48,2048]{1,0:T(8,128)(2,1)S(1)}, u32[]{:S(2)}, u32[]{:S(2)}) collective-permute-start(bf16[48,2048]{1,0:T(8,128)(2,1)S(1)} %pad_maximum_fusion.2), channel_id=1, source_target_pairs={{0,3},{1,2},{2,1},{3,0},{4,7},{5,6},{6,5},{7,4},{8,11},{9,10},{10,... | collective-permute-start | bytes 589832 | tf_op jit(solution)/shard_map/ppermute | solution.py:44
  18.8 17.2 %collective-permute-start.10 = (bf16[256,1792]{1,0:T(8,128)(2,1)S(1)}, bf16[256,1792]{1,0:T(8,128)(2,1)S(1)}, u32[]{:S(2)}, u32[]{:S(2)}) collective-permute-start(bf16[256,1792]{1,0:T(8,128)(2,1)S(1)} %collective-permute-done.4.refs_1_.refs_0_), channel_id=1, source_target_pairs={{0,96},{1,97},{2,98},{3,99},{4,100},{5,101},{6,102},{7,103},{8,104... | collective-permute-start | bytes 2752520 | tf_op jit(solution)/shard_map/ppermute | solution.py:44
  24.7 7.9 %collective-permute-start.5 = (bf16[96,2048]{1,0:T(8,128)(2,1)S(1)}, bf16[96,2048]{1,0:T(8,128)(2,1)S(1)}, u32[]{:S(2)}, u32[]{:S(2)}) collective-permute-start(bf16[96,2048]{1,0:T(8,128)(2,1)S(1)} %fusion.1), channel_id=1, source_target_pairs={{0,4},{1,5},{2,6},{3,7},{4,0},{5,1},{6,2},{7,3},{8,12},{9,13},{10,... | collective-permute-start | bytes 1179656 | tf_op jit(solution)/shard_map/ppermute | solution.py:44
  26.6 11.2 %collective-permute-start.9 = (bf16[192,896]{1,0:T(8,128)(2,1)S(1)}, bf16[192,896]{1,0:T(8,128)(2,1)S(1)}, u32[]{:S(2)}, u32[]{:S(2)}) collective-permute-start(bf16[192,896]{1,0:T(8,128)(2,1)S(1)} %shard_map.105.own_stream), channel_id=1, source_target_pairs={{0,128},{1,129},{2,130},{3,131},{4,132},{5,133},{6,134},{7,135},{8... | collective-permute-start | bytes 1032200 | tf_op jit(solution)/shard_map/ppermute | solution.py:44
  32.7 13.3 %collective-permute-start.8 = (bf16[192,2048]{1,0:T(8,128)(2,1)S(1)}, bf16[192,2048]{1,0:T(8,128)(2,1)S(1)}, u32[]{:S(2)}, u32[]{:S(2)}) collective-permute-start(bf16[192,2048]{1,0:T(8,128)(2,1)S(1)} %pad_maximum_fusion.near), channel_id=1, source_target_pairs={{0,12},{1,13},{2,14},{3,15},{4,8},{5,9},{6,10},{7,11},{8,4},{9,5},... | collective-permute-start | bytes 2359304 | tf_op jit(solution)/shard_map/ppermute | solution.py:44
  36.9 9.0 %collective-permute-start.14 = (bf16[256,1792]{1,0:T(8,128)(2,1)S(1)}, bf16[256,1792]{1,0:T(8,128)(2,1)S(1)}, u32[]{:S(2)}, u32[]{:S(2)}) collective-permute-start(bf16[256,1792]{1,0:T(8,128)(2,1)S(1)} %collective-permute-done.10.refs_3_), channel_id=1, source_target_pairs={{0,16},{1,17},{2,18},{3,19},{4,20},{5,21},{6,22},{7,23},{8,24},{9,... | collective-permute-start | bytes 2752520 | tf_op jit(solution)/shard_map/ppermute | solution.py:44
  37.1 8.8 %collective-permute-start.12 = (bf16[192,1792]{1,0:T(8,128)(2,1)S(1)}, bf16[192,1792]{1,0:T(8,128)(2,1)S(1)}, u32[]{:S(2)}, u32[]{:S(2)}) collective-permute-start(bf16[192,1792]{1,0:T(8,128)(2,1)S(1)} %get-tuple-element.67), channel_id=1, source_target_pairs={{0,16},{1,17},{2,18},{3,19},{4,20},{5,21},{6,22},{7,23},{8,24},{9,... | collective-permute-start | bytes 2064392 | tf_op jit(solution)/shard_map/ppermute | solution.py:44
  37.7 8.3 %collective-permute-start.11 = (bf16[192,1792]{1,0:T(8,128)(2,1)S(1)}, bf16[192,1792]{1,0:T(8,128)(2,1)S(1)}, u32[]{:S(2)}, u32[]{:S(2)}) collective-permute-start(bf16[192,1792]{1,0:T(8,128)(2,1)S(1)} %get-tuple-element.68), channel_id=1, source_target_pairs={{0,16},{1,17},{2,18},{3,19},{4,20},{5,21},{6,22},{7,23},{8,24},{9,... | collective-permute-start | bytes 2064392 | tf_op jit(solution)/shard_map/ppermute | solution.py:44
  37.9 8.1 %collective-permute-start.13 = (bf16[128,1792]{1,0:T(8,128)(2,1)S(1)}, bf16[128,1792]{1,0:T(8,128)(2,1)S(1)}, u32[]{:S(2)}, u32[]{:S(2)}) collective-permute-start(bf16[128,1792]{1,0:T(8,128)(2,1)S(1)} %slice.151), channel_id=1, source_target_pairs={{0,16},{1,17},{2,18},{3,19},{4,20},{5,21},{6,22},{7,23},{8,24},{9,... | collective-permute-start | bytes 1376264 | tf_op jit(solution)/shard_map/ppermute | solution.py:44
  49.1 16.5 %collective-permute-start.15 = (bf16[384,768]{1,0:T(8,128)(2,1)S(1)}, bf16[384,768]{1,0:T(8,128)(2,1)S(1)}, u32[]{:S(2)}, u32[]{:S(2)}) collective-permute-start(bf16[384,768]{1,0:T(8,128)(2,1)S(1)} %get-tuple-element.49), channel_id=1, source_target_pairs={{0,128},{1,129},{2,130},{3,131},{4,132},{5,133},{6,134},{7,135},{8... | collective-permute-start | bytes 1769480 | tf_op jit(solution)/shard_map/ppermute | solution.py:44
  53.1 24.8 %collective-permute-start.16 = (bf16[384,1024]{1,0:T(8,128)(2,1)S(1)}, bf16[384,1024]{1,0:T(8,128)(2,1)S(1)}, u32[]{:S(2)}, u32[]{:S(2)}) collective-permute-start(bf16[384,1024]{1,0:T(8,128)(2,1)S(1)} %get-tuple-element.55), channel_id=1, source_target_pairs={{0,128},{1,129},{2,130},{3,131},{4,132},{5,133},{6,134},{7,135},{8... | collective-permute-start | bytes 2359304 | tf_op jit(solution)/shard_map/ppermute | solution.py:44
  66.7 1.5 %collective-permute-start.17 = (bf16[128,768]{1,0:T(8,128)(2,1)S(1)}, bf16[128,768]{1,0:T(8,128)(2,1)S(1)}, u32[]{:S(2)}, u32[]{:S(2)}) collective-permute-start(bf16[128,768]{1,0:T(8,128)(2,1)S(1)} %get-tuple-element.79), channel_id=1, source_target_pairs={{0,16},{1,17},{2,18},{3,19},{4,20},{5,21},{6,22},{7,23},{8,24},{9,... | collective-permute-start | bytes 589832 | tf_op jit(solution)/shard_map/ppermute | solution.py:44
  66.8 1.7 %collective-permute-start.20 = (bf16[128,768]{1,0:T(8,128)(2,1)S(1)}, bf16[128,768]{1,0:T(8,128)(2,1)S(1)}, u32[]{:S(2)}, u32[]{:S(2)}) collective-permute-start(bf16[128,768]{1,0:T(8,128)(2,1)S(1)} %get-tuple-element.80), channel_id=1, source_target_pairs={{0,16},{1,17},{2,18},{3,19},{4,20},{5,21},{6,22},{7,23},{8,24},{9,... | collective-permute-start | bytes 589832 | tf_op jit(solution)/shard_map/ppermute | solution.py:44
  67.3 1.5 %collective-permute-start.19 = (bf16[128,768]{1,0:T(8,128)(2,1)S(1)}, bf16[128,768]{1,0:T(8,128)(2,1)S(1)}, u32[]{:S(2)}, u32[]{:S(2)}) collective-permute-start(bf16[128,768]{1,0:T(8,128)(2,1)S(1)} %get-tuple-element.81), channel_id=1, source_target_pairs={{0,16},{1,17},{2,18},{3,19},{4,20},{5,21},{6,22},{7,23},{8,24},{9,... | collective-permute-start | bytes 589832 | tf_op jit(solution)/shard_map/ppermute | solution.py:44
  67.4 1.7 %collective-permute-start.18 = (bf16[128,768]{1,0:T(8,128)(2,1)S(1)}, bf16[128,768]{1,0:T(8,128)(2,1)S(1)}, u32[]{:S(2)}, u32[]{:S(2)}) collective-permute-start(bf16[128,768]{1,0:T(8,128)(2,1)S(1)} %get-tuple-element.82), channel_id=1, source_target_pairs={{0,16},{1,17},{2,18},{3,19},{4,20},{5,21},{6,22},{7,23},{8,24},{9,... | collective-permute-start | bytes 589832 | tf_op jit(solution)/shard_map/ppermute | solution.py:44
  69.7 14.8 %collective-permute-start.21 = (bf16[512,768]{1,0:T(8,128)(2,1)S(1)}, bf16[512,768]{1,0:T(8,128)(2,1)S(1)}, u32[]{:S(2)}, u32[]{:S(2)}) collective-permute-start(bf16[512,768]{1,0:T(8,128)(2,1)S(1)} %add_convert_fusion.1), channel_id=1, source_target_pairs={{0,96},{1,97},{2,98},{3,99},{4,100},{5,101},{6,102},{7,103},{8,104... | collective-permute-start | bytes 2359304 | tf_op jit(solution)/shard_map/ppermute | solution.py:44
  81.6 7.2 %collective-permute-start.29 = (bf16[512,768]{1,0:T(8,128)(2,1)S(1)}, bf16[512,768]{1,0:T(8,128)(2,1)S(1)}, u32[]{:S(2)}, u32[]{:S(2)}) collective-permute-start(bf16[512,768]{1,0:T(8,128)(2,1)S(1)} %convolution_convert_fusion.2), channel_id=1, source_target_pairs={{0,16},{1,17},{2,18},{3,19},{4,20},{5,21},{6,22},{7,23},{8,24},{9,... | collective-permute-start | bytes 2359304 | tf_op jit(solution)/shard_map/ppermute | solution.py:44
  81.7 13.5 %collective-permute-start.22 = (bf16[192,2048]{1,0:T(8,128)(2,1)S(1)}, bf16[192,2048]{1,0:T(8,128)(2,1)S(1)}, u32[]{:S(2)}, u32[]{:S(2)}) collective-permute-start(bf16[192,2048]{1,0:T(8,128)(2,1)S(1)} %shard_map.112), channel_id=1, source_target_pairs={{0,12},{1,13},{2,14},{3,15},{4,8},{5,9},{6,10},{7,11},{8,4},{9,5},... | collective-permute-start | bytes 2359304 | tf_op jit(solution)/shard_map/ppermute | solution.py:44
  87.9 1.9 %collective-permute-start.23 = (bf16[128,1024]{1,0:T(8,128)(2,1)S(1)}, bf16[128,1024]{1,0:T(8,128)(2,1)S(1)}, u32[]{:S(2)}, u32[]{:S(2)}) collective-permute-start(bf16[128,1024]{1,0:T(8,128)(2,1)S(1)} %get-tuple-element.73), channel_id=1, source_target_pairs={{0,16},{1,17},{2,18},{3,19},{4,20},{5,21},{6,22},{7,23},{8,24},{9,... | collective-permute-start | bytes 786440 | tf_op jit(solution)/shard_map/ppermute | solution.py:44
  88.0 2.2 %collective-permute-start.26 = (bf16[128,1024]{1,0:T(8,128)(2,1)S(1)}, bf16[128,1024]{1,0:T(8,128)(2,1)S(1)}, u32[]{:S(2)}, u32[]{:S(2)}) collective-permute-start(bf16[128,1024]{1,0:T(8,128)(2,1)S(1)} %get-tuple-element.74), channel_id=1, source_target_pairs={{0,16},{1,17},{2,18},{3,19},{4,20},{5,21},{6,22},{7,23},{8,24},{9,... | collective-permute-start | bytes 786440 | tf_op jit(solution)/shard_map/ppermute | solution.py:44
  88.5 1.8 %collective-permute-start.25 = (bf16[128,1024]{1,0:T(8,128)(2,1)S(1)}, bf16[128,1024]{1,0:T(8,128)(2,1)S(1)}, u32[]{:S(2)}, u32[]{:S(2)}) collective-permute-start(bf16[128,1024]{1,0:T(8,128)(2,1)S(1)} %get-tuple-element.75), channel_id=1, source_target_pairs={{0,16},{1,17},{2,18},{3,19},{4,20},{5,21},{6,22},{7,23},{8,24},{9,... | collective-permute-start | bytes 786440 | tf_op jit(solution)/shard_map/ppermute | solution.py:44
  88.8 1.8 %collective-permute-start.24 = (bf16[128,1024]{1,0:T(8,128)(2,1)S(1)}, bf16[128,1024]{1,0:T(8,128)(2,1)S(1)}, u32[]{:S(2)}, u32[]{:S(2)}) collective-permute-start(bf16[128,1024]{1,0:T(8,128)(2,1)S(1)} %get-tuple-element.76), channel_id=1, source_target_pairs={{0,16},{1,17},{2,18},{3,19},{4,20},{5,21},{6,22},{7,23},{8,24},{9,... | collective-permute-start | bytes 786440 | tf_op jit(solution)/shard_map/ppermute | solution.py:44
  89.8 21.6 %collective-permute-start.30 = (bf16[256,768]{1,0:T(8,128)(2,1)S(1)}, bf16[256,768]{1,0:T(8,128)(2,1)S(1)}, u32[]{:S(2)}, u32[]{:S(2)}) collective-permute-start(bf16[256,768]{1,0:T(8,128)(2,1)S(1)} %fusion.7), channel_id=1, source_target_pairs={{0,32},{1,33},{2,34},{3,35},{4,36},{5,37},{6,38},{7,39},{8,40},{9,... | collective-permute-start | bytes 1179656 | tf_op jit(solution)/shard_map/ppermute | solution.py:44
  91.4 19.4 %collective-permute-start.32 = (bf16[512,1024]{1,0:T(8,128)(2,1)S(1)}, bf16[512,1024]{1,0:T(8,128)(2,1)S(1)}, u32[]{:S(2)}, u32[]{:S(2)}) collective-permute-start(bf16[512,1024]{1,0:T(8,128)(2,1)S(1)} %add_convert_fusion), channel_id=1, source_target_pairs={{0,96},{1,97},{2,98},{3,99},{4,100},{5,101},{6,102},{7,103},{8,104... | collective-permute-start | bytes 3145736 | tf_op jit(solution)/shard_map/ppermute | solution.py:44
  95.1 15.7 %collective-permute-start.31 = (bf16[512,1024]{1,0:T(8,128)(2,1)S(1)}, bf16[512,1024]{1,0:T(8,128)(2,1)S(1)}, u32[]{:S(2)}, u32[]{:S(2)}) collective-permute-start(bf16[512,1024]{1,0:T(8,128)(2,1)S(1)} %convolution_convert_fusion), channel_id=1, source_target_pairs={{0,16},{1,17},{2,18},{3,19},{4,20},{5,21},{6,22},{7,23},{8,24},{9,... | collective-permute-start | bytes 3145736 | tf_op jit(solution)/shard_map/ppermute | solution.py:44
  95.5 8.0 %copy-start.4 = (f32[96,96]{1,0:T(8,128)S(1)}, f32[96,96]{1,0:T(8,128)}, u32[]{:S(2)}) copy-start(f32[96,96]{1,0:T(8,128)} %constant.8.clone) | copy-start | bytes 110596
  95.6 7.9 %collective-permute-start.27 = (bf16[96,2048]{1,0:T(8,128)(2,1)S(1)}, bf16[96,2048]{1,0:T(8,128)(2,1)S(1)}, u32[]{:S(2)}, u32[]{:S(2)}) collective-permute-start(bf16[96,2048]{1,0:T(8,128)(2,1)S(1)} %pad_maximum_fusion.1), channel_id=1, source_target_pairs={{0,4},{1,5},{2,6},{3,7},{4,0},{5,1},{6,2},{7,3},{8,12},{9,13},{10,... | collective-permute-start | bytes 1179656 | tf_op jit(solution)/shard_map/ppermute | solution.py:44
  104.3 12.3 %collective-permute-start.28 = (bf16[48,2048]{1,0:T(8,128)(2,1)S(1)}, bf16[48,2048]{1,0:T(8,128)(2,1)S(1)}, u32[]{:S(2)}, u32[]{:S(2)}) collective-permute-start(bf16[48,2048]{1,0:T(8,128)(2,1)S(1)} %slice.208), channel_id=1, source_target_pairs={{0,3},{1,2},{2,1},{3,0},{4,7},{5,6},{6,5},{7,4},{8,11},{9,10},{10,... | collective-permute-start | bytes 589832 | tf_op jit(solution)/shard_map/ppermute | solution.py:44
  111.3 13.1 %collective-permute-start.34 = (bf16[256,1024]{1,0:T(8,128)(2,1)S(1)}, bf16[256,1024]{1,0:T(8,128)(2,1)S(1)}, u32[]{:S(2)}, u32[]{:S(2)}) collective-permute-start(bf16[256,1024]{1,0:T(8,128)(2,1)S(1)} %fusion.4), channel_id=1, source_target_pairs={{0,32},{1,33},{2,34},{3,35},{4,36},{5,37},{6,38},{7,39},{8,40},{9,... | collective-permute-start | bytes 1572872 | tf_op jit(solution)/shard_map/ppermute | solution.py:44
  116.7 9.1 %collective-permute-start.36 = (bf16[12,2048]{1,0:T(8,128)(2,1)S(1)}, bf16[12,2048]{1,0:T(8,128)(2,1)S(1)}, u32[]{:S(2)}, u32[]{:S(2)}) collective-permute-start(bf16[12,2048]{1,0:T(8,128)(2,1)S(1)} %get-tuple-element.83), channel_id=1, source_target_pairs={{0,129},{1,128},{2,131},{3,130},{4,133},{5,132},{6,135},{7,134},{8... | collective-permute-start | bytes 147464 | tf_op jit(solution)/shard_map/ppermute | solution.py:44
  117.8 8.0 %collective-permute-start.35 = (bf16[12,2048]{1,0:T(8,128)(2,1)S(1)}, bf16[12,2048]{1,0:T(8,128)(2,1)S(1)}, u32[]{:S(2)}, u32[]{:S(2)}) collective-permute-start(bf16[12,2048]{1,0:T(8,128)(2,1)S(1)} %get-tuple-element.84), channel_id=1, source_target_pairs={{0,1},{1,0},{2,3},{3,2},{4,5},{5,4},{6,7},{7,6},{8,9},{9,8},{10,11... | collective-permute-start | bytes 147464 | tf_op jit(solution)/shard_map/ppermute | solution.py:44
  120.1 4.3 %collective-permute-start.33 = (bf16[12,2048]{1,0:T(8,128)(2,1)S(1)}, bf16[12,2048]{1,0:T(8,128)(2,1)S(1)}, u32[]{:S(2)}, u32[]{:S(2)}) collective-permute-start(bf16[12,2048]{1,0:T(8,128)(2,1)S(1)} %get-tuple-element.85), channel_id=1, source_target_pairs={{0,128},{1,129},{2,130},{3,131},{4,132},{5,133},{6,134},{7,135},{8... | collective-permute-start | bytes 147464 | tf_op jit(solution)/shard_map/ppermute | solution.py:44

commit v4 on v3

--- a/solution.py
+++ b/solution.py
@@ -304,6 +304,95 @@
     )(first, second, mine, theirs)
 
 
+def weight_kernel(first, count, inputs, grad, *refs):
+    added, outs = refs[:count], refs[count:]
+    for n in range(len(outs)):
+        size = outs[n].shape[0]
+        for at in range(0, size, 256):
+            result = lax.dot_general(
+                inputs[:, first + n * size + at : first + n * size + min(at + 256, size)],
+                grad[...],
+                (((0,), (0,)), ((), ())),
+                preferred_element_type=F32,
+            )
+            wide = result.shape[0]
+            for m in range(0, wide if added else 0, 128):
+                piece = added[(at + m) // 128][...].astype(F32)
+                outs[n][at + m : at + m + 128] = (result[m : m + 128] + piece).astype(BF16)
+            if not added:
+                outs[n][at : at + wide] = result.astype(BF16)
+
+
+def weight_product(inputs, grad, first, last, added=(), size=None):
+    size = size or last - first
+    outs = (array((size, grad.shape[1]), BF16),) * ((last - first) // size)
+    return call(
+        functools.partial(weight_kernel, first, len(added)),
+        outs,
+        [VMEM] * (2 + len(added)),
+        (VMEM,) * len(outs),
+    )(inputs, grad, *added)
+
+
+def part_kernel(side, first, mine, theirs, out):
+    group, rows = first.shape[0] // 2, first.shape[0] // 4
+    width = FIRST[1] - FIRST[0]
+    spans = columns_of(FIRST, mine.shape[1] // 2)
+    for k in range(8):
+        held = (mine, theirs)[k // 4]
+        for z in range(2):
+            at = z * group + side * rows
+            out[z * rows : (z + 1) * rows, 256 * k : 256 * (k + 1)] = sum(
+                lax.dot_general(
+                    first[at : at + rows, m * width : (m + 1) * width],
+                    held[256 * (k % 4) : 256 * (k % 4 + 1), span],
+                    (((1,), (1,)), ((), ())),
+                    preferred_element_type=F32,
+                )
+                for m, span in enumerate(spans)
+            )
+
+
+def backward_part(side, first, mine, theirs):
+    out = array((first.shape[0] // 2, 2 * mine.shape[0]), F32)
+    return call(functools.partial(part_kernel, side), out, [VMEM] * 3, VMEM)(first, mine, theirs)
+
+
+def rest_kernel(side, before, second, mine, theirs, out, grads):
+    group, rows = second.shape[0] // 2, second.shape[0] // 4
+    width = SECOND[1] - SECOND[0]
+    spans = columns_of(SECOND, mine.shape[1] // 2)
+    for z in range(2):
+        at = z * group + side * rows
+        grads[z * rows : (z + 1) * rows] = second[at : at + rows]
+    for k in range(8):
+        held = (mine, theirs)[k // 4]
+        to = slice(256 * k, 256 * (k + 1))
+        out[:, to] = sum(
+            (
+                lax.dot_general(
+                    grads[:, m * width : (m + 1) * width],
+                    held[256 * (k % 4) : 256 * (k % 4 + 1), span],
+                    (((1,), (1,)), ((), ())),
+                    preferred_element_type=F32,
+                )
+                for m, span in enumerate(spans)
+            ),
+            before[:, to],
+        ).astype(BF16)
+
+
+def backward_rest(side, before, second, mine, theirs):
+    rows = second.shape[0] // 2
+    return call(
+        functools.partial(rest_kernel, side),
+        array((rows, 2 * mine.shape[0]), BF16),
+        [VMEM] * 4,
+        VMEM,
+        [pltpu.VMEM((rows, second.shape[1]), BF16)],
+    )(before, second, mine, theirs)
+
+
 def finish_kernel(scale, first, second, first_last, second_last, gate, up):
     hidden = gate.shape[1]
     for chunk, total, last in ((FIRST, first, first_last), (SECOND, second, second_last)):
@@ -372,26 +461,25 @@
             inputs[:, first:last], grad, (((0,), (0,)), ((), ())), preferred_element_type=F32
         )
 
-    def show(value):
-        (value,) = fence(value.astype(BF16))
-        pieces = [send(value[at : at + 128], TO_CORE) for at in range(0, value.shape[0], 128)]
-        return jnp.concatenate(pieces, axis=0)
-
     first = gradient(FIRST, kept_first, sent_first, upstream, other_upstream)
-    high = show(product(1536, 2048, first))
-    passed = add(product(512, 1024, first), high).astype(BF16)
+    high = [send(piece, TO_CORE) for piece in weight_product(inputs, first, 1536, 2048, size=128)]
+    (passed,) = weight_product(inputs, first, 512, 1024, high)
     first_b = send(passed, Y_B)
+    (low,) = weight_product(inputs, after(first, passed), 1024, 1536)
+    first_low = send(low, TO_CORE)
+    part_away = backward_part(1, after(first, low), mine, theirs)
+    sent_second = after(sent_second, part_away)
 
     second = gradient(SECOND, kept_second, sent_second, upstream, other_upstream)
-    back_away = backward(1, first, second, mine, theirs)
+    back_away = backward_rest(1, part_away, second, mine, theirs)
     back_sent = send(back_away, X_B)
-    back = backward(0, first, after(second, first_b, back_away), mine, theirs)
-    first_low = send(product(1024, 1536, after(first, back_away)).astype(BF16), TO_CORE)
+    high = weight_product(inputs, after(second, back_away), 1536, 2048, size=128)
+    back = backward(0, first, after(second, first_b, *high), mine, theirs)
+    high = [send(piece, TO_CORE) for piece in high]
     second = after(second, back)
-    high = show(product(1536, 2048, second))
-    passed = add(product(512, 1024, second), high).astype(BF16)
+    (passed,) = weight_product(inputs, second, 512, 1024, high)
     second_b = send(passed, Y_B)
-    low = product(1024, 1536, after(second, passed)).astype(BF16)
+    (low,) = weight_product(inputs, after(second, passed), 1024, 1536)
     second_low = send(low, TO_CORE)
     back_sent = after(back_sent, low)
 
@@ -405,7 +493,7 @@
     passed = jnp.concatenate([back[part:half], back[half + part :]], axis=0).astype(BF16)
     kept = jnp.concatenate([back[:part], back[half : half + part]], axis=0)
     arrived = send(passed, X_A)
-    first_last = send(second_sum(first, first_low, first_b), Y_A)
+    first_last = send(second_sum(first, first_low, after(first_b, passed)), Y_A)
     four = jnp.dot(
         by_group.T.astype(np.float32),
         add(kept, arrived),

time: 127 us -> 125 us (0.984); the launches traced: 126 us -> 122 us
  Pallas kernels: 15.9 us -> 20.9 us
  matrix products: 6.99 us -> 3 us
  starting transfers between devices: 51 us -> 47.6 us
  waiting for transfers between devices: 50.5 us -> 48.8 us
    pallas_call x0 -> x8, Pallas kernels: none -> 7.54 us  [the longest x6 3.99 us: weight_product(): call(functools.partial(weight_kernel, first, len(added)), outs, [VMEM] *...]
    dot_general x10 -> x4, matrix products: 5.74 us -> 1.75 us  [product(): lax.dot_general(inputs[:, first:last], grad, (((0,), (0,)), ((), ())), pr...]
    ppermute x37, starting transfers between devices: 51 us -> 47.6 us  [send(): return lax.ppermute(value, BOTH, pairs)]
    pallas_call x2 -> x1, Pallas kernels: 5.05 us -> 2.52 us  [backward(): call(functools.partial(backward_kernel, side), array((rows, 2 * mine.shap...]
    ppermute x37, waiting for transfers between devices: 50.5 us -> 48.8 us  [send(): return lax.ppermute(value, BOTH, pairs)]
  transfers between devices with their start and end apart: 37 -> 37, of which waited for: 16 -> 17; matrix products, arithmetic and copies ran while one was open for 6% -> 3% of each run, Pallas kernels for 9% -> 13%
where the time goes in v4:
time: 125 us; the launch traced here: 122 us
  waiting for transfers between devices  48.8 us (39%)
  starting transfers between devices  47.6 us (38%)
  Pallas kernels  20.9 us (17%)
  matrix products  3 us (2%)
    ppermute x37, waiting for transfers between devices, send(): return lax.ppermute(value, BOTH, pairs)  48.8 us
    ppermute x37, starting transfers between devices, send(): return lax.ppermute(value, BOTH, pairs)  47.6 us
    pallas_call x6, Pallas kernels, weight_product(): call(functools.partial(weight_kernel, first, len(added)), outs, [VMEM] *...  3.99 us
    pallas_call x1, Pallas kernels, first_products(): call(first_kernel, outs, [VMEM] * 3 + [ANY] * len(pieces), (VMEM,) * 4, [...  3.15 us
    pallas_call x1, Pallas kernels, backward(): call(functools.partial(backward_kernel, side), array((rows, 2 * mine.shap...  2.52 us
  transfers between devices with their start and end apart: 37, of which 17 were waited for; matrix products, arithmetic and copies ran while one was open for 3% of the time, Pallas kernels for 13%

profile of v4, /device:TPU:64, one launch (start us, length us, event | category | flops | bytes accessed | tf_op | source)
XLA Modules:
  0.0 122.3 jit_solution(4514181607091037524)
XLA Ops:
  0.7 1.2 shard_map.103.refs_0_
  1.9 1.7 %collective-permute-start.4 = (bf16[256,1792]{1,0:T(8,128)(2,1)S(1)}, bf16[256,1792]{1,0:T(8,128)(2,1)S(1)}, u32[]{:S(2)}, u32[]{:S(2)}) collective-permute-start(bf16[256,1792]{1,0:T(8,128)(2,1)S(1)} %shard_map.103.refs_0_), channel_id=1, source_target_pairs={{0,32},{1,33},{2,34},{3,35},{4,36},{5,37},{6,38},{7,39},{8,40},{9,... | collective-permute-start | bytes 2752520 | tf_op jit(solution)/shard_map/ppermute | solution.py:44
  3.7 2.0 %collective-permute-start = (bf16[12,2048]{1,0:T(8,128)(2,1)S(1)}, bf16[12,2048]{1,0:T(8,128)(2,1)S(1)}, u32[]{:S(2)}, u32[]{:S(2)}) collective-permute-start(bf16[12,2048]{1,0:T(8,128)(2,1)S(1)} %get-tuple-element.49), channel_id=1, source_target_pairs={{0,128},{1,129},{2,130},{3,131},{4,132},{5,133},{6,134},{7,135},{8... | collective-permute-start | bytes 147464 | tf_op jit(solution)/shard_map/ppermute | solution.py:44
  5.7 1.6 %collective-permute-start.2 = (bf16[12,2048]{1,0:T(8,128)(2,1)S(1)}, bf16[12,2048]{1,0:T(8,128)(2,1)S(1)}, u32[]{:S(2)}, u32[]{:S(2)}) collective-permute-start(bf16[12,2048]{1,0:T(8,128)(2,1)S(1)} %get-tuple-element.49), channel_id=1, source_target_pairs={{0,129},{1,128},{2,131},{3,130},{4,133},{5,132},{6,135},{7,134},{8... | collective-permute-start | bytes 147464 | tf_op jit(solution)/shard_map/ppermute | solution.py:44
  7.3 2.2 %collective-permute-start.6 = (bf16[256,1792]{1,0:T(8,128)(2,1)S(1)}, bf16[256,1792]{1,0:T(8,128)(2,1)S(1)}, u32[]{:S(2)}, u32[]{:S(2)}) collective-permute-start(bf16[256,1792]{1,0:T(8,128)(2,1)S(1)} %shard_map.103.refs_0_), channel_id=1, source_target_pairs={{0,96},{1,97},{2,98},{3,99},{4,100},{5,101},{6,102},{7,103},{8,104... | collective-permute-start | bytes 2752520 | tf_op jit(solution)/shard_map/ppermute | solution.py:44
  9.5 1.5 %collective-permute-done.1 = bf16[12,2048]{1,0:T(8,128)(2,1)S(1)} collective-permute-done((bf16[12,2048]{1,0:T(8,128)(2,1)S(1)}, bf16[12,2048]{1,0:T(8,128)(2,1)S(1)}, u32[]{:S(2)}, u32[]{:S(2)}) %collective-permute-start.1) | collective-permute-done | bytes 49184 | tf_op jit(solution)/shard_map/ppermute | solution.py:44
  11.0 5.7 %collective-permute-start.7 = (bf16[256,1792]{1,0:T(8,128)(2,1)S(1)}, bf16[256,1792]{1,0:T(8,128)(2,1)S(1)}, u32[]{:S(2)}, u32[]{:S(2)}) collective-permute-start(bf16[256,1792]{1,0:T(8,128)(2,1)S(1)} %shard_map.103.refs_0_), channel_id=1, source_target_pairs={{0,16},{1,17},{2,18},{3,19},{4,20},{5,21},{6,22},{7,23},{8,24},{9,... | collective-permute-start | bytes 2752520 | tf_op jit(solution)/shard_map/ppermute | solution.py:44
  16.7 0.5 collective-permute-start.3
  17.3 1.1 collective-permute-done.4.refs_1_.refs_0_
  18.3 5.3 %collective-permute-start.10 = (bf16[256,1792]{1,0:T(8,128)(2,1)S(1)}, bf16[256,1792]{1,0:T(8,128)(2,1)S(1)}, u32[]{:S(2)}, u32[]{:S(2)}) collective-permute-start(bf16[256,1792]{1,0:T(8,128)(2,1)S(1)} %collective-permute-done.4.refs_1_.refs_0_), channel_id=1, source_target_pairs={{0,96},{1,97},{2,98},{3,99},{4,100},{5,101},{6,102},{7,103},{8,104... | collective-permute-start | bytes 2752520 | tf_op jit(solution)/shard_map/ppermute | solution.py:44
  23.9 1.1 collective-permute-done.3
  25.2 1.6 %collective-permute-start.5 = (bf16[96,2048]{1,0:T(8,128)(2,1)S(1)}, bf16[96,2048]{1,0:T(8,128)(2,1)S(1)}, u32[]{:S(2)}, u32[]{:S(2)}) collective-permute-start(bf16[96,2048]{1,0:T(8,128)(2,1)S(1)} %fusion.1), channel_id=1, source_target_pairs={{0,4},{1,5},{2,6},{3,7},{4,0},{5,1},{6,2},{7,3},{8,12},{9,13},{10,... | collective-permute-start | bytes 1179656 | tf_op jit(solution)/shard_map/ppermute | solution.py:44
  27.1 2.3 %collective-permute-start.9 = (bf16[192,896]{1,0:T(8,128)(2,1)S(1)}, bf16[192,896]{1,0:T(8,128)(2,1)S(1)}, u32[]{:S(2)}, u32[]{:S(2)}) collective-permute-start(bf16[192,896]{1,0:T(8,128)(2,1)S(1)} %shard_map.105.own_stream), channel_id=1, source_target_pairs={{0,128},{1,129},{2,130},{3,131},{4,132},{5,133},{6,134},{7,135},{8... | collective-permute-start | bytes 1032200 | tf_op jit(solution)/shard_map/ppermute | solution.py:44
  29.4 3.7 %collective-permute-done.5 = bf16[96,2048]{1,0:T(8,128)(2,1)S(1)} collective-permute-done((bf16[96,2048]{1,0:T(8,128)(2,1)S(1)}, bf16[96,2048]{1,0:T(8,128)(2,1)S(1)}, u32[]{:S(2)}, u32[]{:S(2)}) %collective-permute-start.5) | collective-permute-done | bytes 393248 | tf_op jit(solution)/shard_map/ppermute | solution.py:44
  33.1 2.8 %collective-permute-start.8 = (bf16[192,2048]{1,0:T(8,128)(2,1)S(1)}, bf16[192,2048]{1,0:T(8,128)(2,1)S(1)}, u32[]{:S(2)}, u32[]{:S(2)}) collective-permute-start(bf16[192,2048]{1,0:T(8,128)(2,1)S(1)} %pad_maximum_fusion.near), channel_id=1, source_target_pairs={{0,12},{1,13},{2,14},{3,15},{4,8},{5,9},{6,10},{7,11},{8,4},{9,5},... | collective-permute-start | bytes 2359304 | tf_op jit(solution)/shard_map/ppermute | solution.py:44
  36.5 0.9 shard_map.106.mine
  37.6 0.6 collective-permute-start.11
  38.3 0.5 collective-permute-start.13
  38.8 7.6 %collective-permute-done.8.away = bf16[192,2048]{1,0:T(8,128)(2,1)S(1)} collective-permute-done((bf16[192,2048]{1,0:T(8,128)(2,1)S(1)}, bf16[192,2048]{1,0:T(8,128)(2,1)S(1)}, u32[]{:S(2)}, u32[]{:S(2)}) %collective-permute-start.8) | collective-permute-done | bytes 786464 | tf_op jit(solution)/shard_map/ppermute | solution.py:44
  46.4 3.2 %shard_map.108 = (bf16[384,2048]{1,0:T(8,128)(2,1)S(1)}, bf16[1024,1792]{1,0:T(8,128)(2,1)S(1)}, f32[384,768]{1,0:T(8,128)S(1)}, bf16[384,768]{1,0:T(8,128)(2,1)S(1)}) custom-call(bf16[192,2048]{1,0:T(8,128)(2,1)S(1)} %pad_maximum_fusion.near, bf16[192,2048]{1,0:T(8,128)(2,1)S(1)} %collective-permute-done.8.away, bf16[1024,1792]{1,0:T(8,128)(2,1)S(1)} %shard_map.106.mine, ...), custom_call_target="tpu_custom_call" | custom-call | tf_op jit(solution)/shard_map/pallas_call | solution.py:240
  49.6 2.5 %collective-permute-start.15 = (bf16[384,768]{1,0:T(8,128)(2,1)S(1)}, bf16[384,768]{1,0:T(8,128)(2,1)S(1)}, u32[]{:S(2)}, u32[]{:S(2)}) collective-permute-start(bf16[384,768]{1,0:T(8,128)(2,1)S(1)} %get-tuple-element.61), channel_id=1, source_target_pairs={{0,128},{1,129},{2,130},{3,131},{4,132},{5,133},{6,134},{7,135},{8... | collective-permute-start | bytes 1769480 | tf_op jit(solution)/shard_map/ppermute | solution.py:44
  52.1 1.8 %shard_map.109 = (f32[384,1024]{1,0:T(8,128)S(1)}, bf16[384,1024]{1,0:T(8,128)(2,1)S(1)}) custom-call(bf16[384,2048]{1,0:T(8,128)(2,1)S(1)} %get-tuple-element.62.rows.inputs, bf16[1024,1792]{1,0:T(8,128)(2,1)S(1)} %shard_map.106.mine, bf16[1024,1792]{1,0:T(8,128)(2,1)S(1)} %get-tuple-element.63.theirs), custom_call_target="tpu_custom_call" | custom-call | tf_op jit(solution)/shard_map/pallas_call | solution.py:259
  54.0 12.3 %collective-permute-done.15.sent = bf16[384,768]{1,0:T(8,128)(2,1)S(1)} collective-permute-done((bf16[384,768]{1,0:T(8,128)(2,1)S(1)}, bf16[384,768]{1,0:T(8,128)(2,1)S(1)}, u32[]{:S(2)}, u32[]{:S(2)}) %collective-permute-start.15) | collective-permute-done | bytes 589856 | tf_op jit(solution)/shard_map/ppermute | solution.py:44
  66.7 0.6 shard_map.111
  67.4 0.5 collective-permute-start.18
  69.7 0.6 shard_map.112
  70.4 0.6 shard_map.113
  71.0 2.0 %shard_map.114.before = f32[192,2048]{1,0:T(8,128)S(1)} custom-call(bf16[384,768]{1,0:T(8,128)(2,1)S(1)} %shard_map.110.grad.first, bf16[1024,1792]{1,0:T(8,128)(2,1)S(1)} %shard_map.106.mine, bf16[1024,1792]{1,0:T(8,128)(2,1)S(1)} %get-tuple-element.63.theirs), custom_call_target="tpu_custom_call" | custom-call | tf_op jit(solution)/shard_map/pallas_call | solution.py:358
  73.0 5.7 %collective-permute-done.16.sent = bf16[384,1024]{1,0:T(8,128)(2,1)S(1)} collective-permute-done((bf16[384,1024]{1,0:T(8,128)(2,1)S(1)}, bf16[384,1024]{1,0:T(8,128)(2,1)S(1)}, u32[]{:S(2)}, u32[]{:S(2)}) %collective-permute-start.16) | collective-permute-done | bytes 786464 | tf_op jit(solution)/shard_map/ppermute | solution.py:44
  79.2 1.5 %shard_map.116 = bf16[192,2048]{1,0:T(8,128)(2,1)S(1)} custom-call(f32[192,2048]{1,0:T(8,128)S(1)} %shard_map.114.before, bf16[384,1024]{1,0:T(8,128)(2,1)S(1)} %shard_map.115.second.grad, bf16[1024,1792]{1,0:T(8,128)(2,1)S(1)} %shard_map.106.mine, bf16[1024,1792]{1,0:T(8,128)(2,1)S(1)} %get-tuple-element.63.theirs), custom_call_target="tpu_custom_call" | custom-call | tf_op jit(solution)/shard_map/pallas_call | solution.py:387
  80.7 2.5 %collective-permute-start.22 = (bf16[192,2048]{1,0:T(8,128)(2,1)S(1)}, bf16[192,2048]{1,0:T(8,128)(2,1)S(1)}, u32[]{:S(2)}, u32[]{:S(2)}) collective-permute-start(bf16[192,2048]{1,0:T(8,128)(2,1)S(1)} %shard_map.116), channel_id=1, source_target_pairs={{0,12},{1,13},{2,14},{3,15},{4,8},{5,9},{6,10},{7,11},{8,4},{9,5},... | collective-permute-start | bytes 2359304 | tf_op jit(solution)/shard_map/ppermute | solution.py:44
  83.2 0.7 shard_map.117
  84.0 0.5 collective-permute-start.24
  85.0 2.5 %shard_map.118 = bf16[192,2048]{1,0:T(8,128)(2,1)S(1)} custom-call(bf16[384,768]{1,0:T(8,128)(2,1)S(1)} %shard_map.110.grad.first, bf16[384,1024]{1,0:T(8,128)(2,1)S(1)} %shard_map.115.second.grad, bf16[1024,1792]{1,0:T(8,128)(2,1)S(1)} %shard_map.106.mine, bf16[1024,1792]{1,0:T(8,128)(2,1)S(1)} %get-tuple-element.63.theirs), custom_call_target="tpu_custom_call" | custom-call | tf_op jit(solution)/shard_map/pallas_call | solution.py:298
  87.8 0.7 shard_map.119
  88.5 3.3 %collective-permute-start.32 = (bf16[512,1024]{1,0:T(8,128)(2,1)S(1)}, bf16[512,1024]{1,0:T(8,128)(2,1)S(1)}, u32[]{:S(2)}, u32[]{:S(2)}) collective-permute-start(bf16[512,1024]{1,0:T(8,128)(2,1)S(1)} %shard_map.119), channel_id=1, source_target_pairs={{0,96},{1,97},{2,98},{3,99},{4,100},{5,101},{6,102},{7,103},{8,104... | collective-permute-start | bytes 3145736 | tf_op jit(solution)/shard_map/ppermute | solution.py:44
  91.8 0.7 shard_map.120
  92.7 1.3 %collective-permute-done.22 = bf16[192,2048]{1,0:T(8,128)(2,1)S(1)} collective-permute-done((bf16[192,2048]{1,0:T(8,128)(2,1)S(1)}, bf16[192,2048]{1,0:T(8,128)(2,1)S(1)}, u32[]{:S(2)}, u32[]{:S(2)}) %collective-permute-start.22) | collective-permute-done | bytes 786464 | tf_op jit(solution)/shard_map/ppermute | solution.py:44
  95.5 6.8 %collective-permute-done.27 = bf16[96,2048]{1,0:T(8,128)(2,1)S(1)} collective-permute-done((bf16[96,2048]{1,0:T(8,128)(2,1)S(1)}, bf16[96,2048]{1,0:T(8,128)(2,1)S(1)}, u32[]{:S(2)}, u32[]{:S(2)}) %collective-permute-start.27) | collective-permute-done | bytes 393248 | tf_op jit(solution)/shard_map/ppermute | solution.py:44
  102.2 0.8 fusion.8
  103.1 5.8 %collective-permute-start.28 = (bf16[48,2048]{1,0:T(8,128)(2,1)S(1)}, bf16[48,2048]{1,0:T(8,128)(2,1)S(1)}, u32[]{:S(2)}, u32[]{:S(2)}) collective-permute-start(bf16[48,2048]{1,0:T(8,128)(2,1)S(1)} %slice.140), channel_id=1, source_target_pairs={{0,3},{1,2},{2,1},{3,0},{4,7},{5,6},{6,5},{7,4},{8,11},{9,10},{10,... | collective-permute-start | bytes 589832 | tf_op jit(solution)/shard_map/ppermute | solution.py:44
  109.5 4.7 %collective-permute-done.28 = bf16[48,2048]{1,0:T(8,128)(2,1)S(1)} collective-permute-done((bf16[48,2048]{1,0:T(8,128)(2,1)S(1)}, bf16[48,2048]{1,0:T(8,128)(2,1)S(1)}, u32[]{:S(2)}, u32[]{:S(2)}) %collective-permute-start.28) | collective-permute-done | bytes 196640 | tf_op jit(solution)/shard_map/ppermute | solution.py:44
  114.3 0.8 collective-permute-start.33
  115.2 1.8 %collective-permute-start.35 = (bf16[12,2048]{1,0:T(8,128)(2,1)S(1)}, bf16[12,2048]{1,0:T(8,128)(2,1)S(1)}, u32[]{:S(2)}, u32[]{:S(2)}) collective-permute-start(bf16[12,2048]{1,0:T(8,128)(2,1)S(1)} %get-tuple-element.100), channel_id=1, source_target_pairs={{0,1},{1,0},{2,3},{3,2},{4,5},{5,4},{6,7},{7,6},{8,9},{9,8},{10,11... | collective-permute-start | bytes 147464 | tf_op jit(solution)/shard_map/ppermute | solution.py:44
  116.9 1.0 collective-permute-start.36
  118.7 1.4 %shard_map.122 = (f32[256,896]{1,0:T(8,128)}, f32[256,896]{1,0:T(8,128)}) custom-call(f32[256,768]{1,0:T(8,128)S(1)} %fusion.6.first, f32[256,1024]{1,0:T(8,128)S(1)} %fusion.2.second, bf16[256,768]{1,0:T(8,128)(2,1)S(1)} %collective-permute-done.30.first_last, bf16[256,1024]{1,0:T(8,128)(2,1)S(1)} %collective-permute-done.34.second_last), custom_call_target="tpu_custom_call" | custom-call | tf_op jit(solution)/shard_map/pallas_call | solution.py:407
  120.4 1.2 collective-permute-done.36.from_both
  121.6 0.7 shard_map.121
  (79 shorter events, 8.8 us)
Async XLA Ops:
  0.6 23.0 %copy-start.5 = (bf16[96,48]{1,0:T(8,128)(2,1)S(1)}, bf16[96,48]{1,0:T(8,128)(2,1)}, u32[]{:S(2)}) copy-start(bf16[96,48]{1,0:T(8,128)(2,1)} %constant.11) | copy-start | bytes 27652
  0.6 24.3 %copy-start.6 = (bf16[96,48]{1,0:T(8,128)(2,1)S(1)}, bf16[96,48]{1,0:T(8,128)(2,1)}, u32[]{:S(2)}) copy-start(bf16[96,48]{1,0:T(8,128)(2,1)} %constant.12) | copy-start | bytes 27652
  0.7 2.9 %copy-start.1 = (bf16[12,4096]{1,0:T(8,128)(2,1)S(1)}, bf16[12,4096]{1,0:T(8,128)(2,1)}, u32[]{:S(2)}) copy-start(bf16[12,4096]{1,0:T(8,128)(2,1)} %codes) | copy-start | bytes 294916
  0.7 2.9 %copy-start.3 = (bf16[12,32]{1,0:T(8,128)(2,1)S(1)}, bf16[12,32]{1,0:T(8,128)(2,1)}, u32[]{:S(2)}) copy-start(bf16[12,32]{1,0:T(8,128)(2,1)} %scales) | copy-start | bytes 2308
  1.9 24.9 %copy-start = (bf16[192,896]{1,0:T(8,128)(2,1)S(1)}, bf16[192,896]{1,0:T(8,128)(2,1)}, u32[]{:S(2)}) copy-start(bf16[192,896]{1,0:T(8,128)(2,1)} %values.1) | copy-start | bytes 1032196
  1.9 24.9 %copy-start.2 = (s32[32,1,192]{2,1,0:T(1,128)S(1)}, s32[32,1,192]{2,1,0:T(1,128)}, u32[]{:S(2)}) copy-start(s32[32,1,192]{2,1,0:T(1,128)} %constant.7.clone.table) | copy-start | bytes 73732
  1.9 16.4 %collective-permute-start.4 = (bf16[256,1792]{1,0:T(8,128)(2,1)S(1)}, bf16[256,1792]{1,0:T(8,128)(2,1)S(1)}, u32[]{:S(2)}, u32[]{:S(2)}) collective-permute-start(bf16[256,1792]{1,0:T(8,128)(2,1)S(1)} %shard_map.103.refs_0_), channel_id=1, source_target_pairs={{0,32},{1,33},{2,34},{3,35},{4,36},{5,37},{6,38},{7,39},{8,40},{9,... | collective-permute-start | bytes 2752520 | tf_op jit(solution)/shard_map/ppermute | solution.py:44
  3.7 5.8 %collective-permute-start = (bf16[12,2048]{1,0:T(8,128)(2,1)S(1)}, bf16[12,2048]{1,0:T(8,128)(2,1)S(1)}, u32[]{:S(2)}, u32[]{:S(2)}) collective-permute-start(bf16[12,2048]{1,0:T(8,128)(2,1)S(1)} %get-tuple-element.49), channel_id=1, source_target_pairs={{0,128},{1,129},{2,130},{3,131},{4,132},{5,133},{6,134},{7,135},{8... | collective-permute-start | bytes 147464 | tf_op jit(solution)/shard_map/ppermute | solution.py:44
  5.7 5.2 %collective-permute-start.1 = (bf16[12,2048]{1,0:T(8,128)(2,1)S(1)}, bf16[12,2048]{1,0:T(8,128)(2,1)S(1)}, u32[]{:S(2)}, u32[]{:S(2)}) collective-permute-start(bf16[12,2048]{1,0:T(8,128)(2,1)S(1)} %get-tuple-element.48), channel_id=1, source_target_pairs={{0,1},{1,0},{2,3},{3,2},{4,5},{5,4},{6,7},{7,6},{8,9},{9,8},{10,11... | collective-permute-start | bytes 147464 | tf_op jit(solution)/shard_map/ppermute | solution.py:44
  5.7 5.2 %collective-permute-start.2 = (bf16[12,2048]{1,0:T(8,128)(2,1)S(1)}, bf16[12,2048]{1,0:T(8,128)(2,1)S(1)}, u32[]{:S(2)}, u32[]{:S(2)}) collective-permute-start(bf16[12,2048]{1,0:T(8,128)(2,1)S(1)} %get-tuple-element.49), channel_id=1, source_target_pairs={{0,129},{1,128},{2,131},{3,130},{4,133},{5,132},{6,135},{7,134},{8... | collective-permute-start | bytes 147464 | tf_op jit(solution)/shard_map/ppermute | solution.py:44
  7.3 22.1 %collective-permute-start.6 = (bf16[256,1792]{1,0:T(8,128)(2,1)S(1)}, bf16[256,1792]{1,0:T(8,128)(2,1)S(1)}, u32[]{:S(2)}, u32[]{:S(2)}) collective-permute-start(bf16[256,1792]{1,0:T(8,128)(2,1)S(1)} %shard_map.103.refs_0_), channel_id=1, source_target_pairs={{0,96},{1,97},{2,98},{3,99},{4,100},{5,101},{6,102},{7,103},{8,104... | collective-permute-start | bytes 2752520 | tf_op jit(solution)/shard_map/ppermute | solution.py:44
  11.0 18.4 %collective-permute-start.7 = (bf16[256,1792]{1,0:T(8,128)(2,1)S(1)}, bf16[256,1792]{1,0:T(8,128)(2,1)S(1)}, u32[]{:S(2)}, u32[]{:S(2)}) collective-permute-start(bf16[256,1792]{1,0:T(8,128)(2,1)S(1)} %shard_map.103.refs_0_), channel_id=1, source_target_pairs={{0,16},{1,17},{2,18},{3,19},{4,20},{5,21},{6,22},{7,23},{8,24},{9,... | collective-permute-start | bytes 2752520 | tf_op jit(solution)/shard_map/ppermute | solution.py:44
  16.7 8.2 %collective-permute-start.3 = (bf16[48,2048]{1,0:T(8,128)(2,1)S(1)}, bf16[48,2048]{1,0:T(8,128)(2,1)S(1)}, u32[]{:S(2)}, u32[]{:S(2)}) collective-permute-start(bf16[48,2048]{1,0:T(8,128)(2,1)S(1)} %pad_maximum_fusion.2), channel_id=1, source_target_pairs={{0,3},{1,2},{2,1},{3,0},{4,7},{5,6},{6,5},{7,4},{8,11},{9,10},{10,... | collective-permute-start | bytes 589832 | tf_op jit(solution)/shard_map/ppermute | solution.py:44
  18.3 18.1 %collective-permute-start.10 = (bf16[256,1792]{1,0:T(8,128)(2,1)S(1)}, bf16[256,1792]{1,0:T(8,128)(2,1)S(1)}, u32[]{:S(2)}, u32[]{:S(2)}) collective-permute-start(bf16[256,1792]{1,0:T(8,128)(2,1)S(1)} %collective-permute-done.4.refs_1_.refs_0_), channel_id=1, source_target_pairs={{0,96},{1,97},{2,98},{3,99},{4,100},{5,101},{6,102},{7,103},{8,104... | collective-permute-start | bytes 2752520 | tf_op jit(solution)/shard_map/ppermute | solution.py:44
  25.2 7.9 %collective-permute-start.5 = (bf16[96,2048]{1,0:T(8,128)(2,1)S(1)}, bf16[96,2048]{1,0:T(8,128)(2,1)S(1)}, u32[]{:S(2)}, u32[]{:S(2)}) collective-permute-start(bf16[96,2048]{1,0:T(8,128)(2,1)S(1)} %fusion.1), channel_id=1, source_target_pairs={{0,4},{1,5},{2,6},{3,7},{4,0},{5,1},{6,2},{7,3},{8,12},{9,13},{10,... | collective-permute-start | bytes 1179656 | tf_op jit(solution)/shard_map/ppermute | solution.py:44
  27.1 11.2 %collective-permute-start.9 = (bf16[192,896]{1,0:T(8,128)(2,1)S(1)}, bf16[192,896]{1,0:T(8,128)(2,1)S(1)}, u32[]{:S(2)}, u32[]{:S(2)}) collective-permute-start(bf16[192,896]{1,0:T(8,128)(2,1)S(1)} %shard_map.105.own_stream), channel_id=1, source_target_pairs={{0,128},{1,129},{2,130},{3,131},{4,132},{5,133},{6,134},{7,135},{8... | collective-permute-start | bytes 1032200 | tf_op jit(solution)/shard_map/ppermute | solution.py:44
  33.1 13.3 %collective-permute-start.8 = (bf16[192,2048]{1,0:T(8,128)(2,1)S(1)}, bf16[192,2048]{1,0:T(8,128)(2,1)S(1)}, u32[]{:S(2)}, u32[]{:S(2)}) collective-permute-start(bf16[192,2048]{1,0:T(8,128)(2,1)S(1)} %pad_maximum_fusion.near), channel_id=1, source_target_pairs={{0,12},{1,13},{2,14},{3,15},{4,8},{5,9},{6,10},{7,11},{8,4},{9,5},... | collective-permute-start | bytes 2359304 | tf_op jit(solution)/shard_map/ppermute | solution.py:44
  37.4 9.0 %collective-permute-start.14 = (bf16[256,1792]{1,0:T(8,128)(2,1)S(1)}, bf16[256,1792]{1,0:T(8,128)(2,1)S(1)}, u32[]{:S(2)}, u32[]{:S(2)}) collective-permute-start(bf16[256,1792]{1,0:T(8,128)(2,1)S(1)} %collective-permute-done.10.refs_3_), channel_id=1, source_target_pairs={{0,16},{1,17},{2,18},{3,19},{4,20},{5,21},{6,22},{7,23},{8,24},{9,... | collective-permute-start | bytes 2752520 | tf_op jit(solution)/shard_map/ppermute | solution.py:44
  37.6 8.8 %collective-permute-start.11 = (bf16[192,1792]{1,0:T(8,128)(2,1)S(1)}, bf16[192,1792]{1,0:T(8,128)(2,1)S(1)}, u32[]{:S(2)}, u32[]{:S(2)}) collective-permute-start(bf16[192,1792]{1,0:T(8,128)(2,1)S(1)} %get-tuple-element.92), channel_id=1, source_target_pairs={{0,16},{1,17},{2,18},{3,19},{4,20},{5,21},{6,22},{7,23},{8,24},{9,... | collective-permute-start | bytes 2064392 | tf_op jit(solution)/shard_map/ppermute | solution.py:44
  38.2 8.3 %collective-permute-start.12 = (bf16[192,1792]{1,0:T(8,128)(2,1)S(1)}, bf16[192,1792]{1,0:T(8,128)(2,1)S(1)}, u32[]{:S(2)}, u32[]{:S(2)}) collective-permute-start(bf16[192,1792]{1,0:T(8,128)(2,1)S(1)} %get-tuple-element.91), channel_id=1, source_target_pairs={{0,16},{1,17},{2,18},{3,19},{4,20},{5,21},{6,22},{7,23},{8,24},{9,... | collective-permute-start | bytes 2064392 | tf_op jit(solution)/shard_map/ppermute | solution.py:44
  38.3 8.1 %collective-permute-start.13 = (bf16[128,1792]{1,0:T(8,128)(2,1)S(1)}, bf16[128,1792]{1,0:T(8,128)(2,1)S(1)}, u32[]{:S(2)}, u32[]{:S(2)}) collective-permute-start(bf16[128,1792]{1,0:T(8,128)(2,1)S(1)} %slice.104), channel_id=1, source_target_pairs={{0,16},{1,17},{2,18},{3,19},{4,20},{5,21},{6,22},{7,23},{8,24},{9,... | collective-permute-start | bytes 1376264 | tf_op jit(solution)/shard_map/ppermute | solution.py:44
  49.6 16.7 %collective-permute-start.15 = (bf16[384,768]{1,0:T(8,128)(2,1)S(1)}, bf16[384,768]{1,0:T(8,128)(2,1)S(1)}, u32[]{:S(2)}, u32[]{:S(2)}) collective-permute-start(bf16[384,768]{1,0:T(8,128)(2,1)S(1)} %get-tuple-element.61), channel_id=1, source_target_pairs={{0,128},{1,129},{2,130},{3,131},{4,132},{5,133},{6,134},{7,135},{8... | collective-permute-start | bytes 1769480 | tf_op jit(solution)/shard_map/ppermute | solution.py:44
  53.9 24.8 %collective-permute-start.16 = (bf16[384,1024]{1,0:T(8,128)(2,1)S(1)}, bf16[384,1024]{1,0:T(8,128)(2,1)S(1)}, u32[]{:S(2)}, u32[]{:S(2)}) collective-permute-start(bf16[384,1024]{1,0:T(8,128)(2,1)S(1)} %get-tuple-element.67), channel_id=1, source_target_pairs={{0,128},{1,129},{2,130},{3,131},{4,132},{5,133},{6,134},{7,135},{8... | collective-permute-start | bytes 2359304 | tf_op jit(solution)/shard_map/ppermute | solution.py:44
  67.3 1.5 %collective-permute-start.17 = (bf16[128,768]{1,0:T(8,128)(2,1)S(1)}, bf16[128,768]{1,0:T(8,128)(2,1)S(1)}, u32[]{:S(2)}, u32[]{:S(2)}) collective-permute-start(bf16[128,768]{1,0:T(8,128)(2,1)S(1)} %get-tuple-element.68), channel_id=1, source_target_pairs={{0,16},{1,17},{2,18},{3,19},{4,20},{5,21},{6,22},{7,23},{8,24},{9,... | collective-permute-start | bytes 589832 | tf_op jit(solution)/shard_map/ppermute | solution.py:44
  67.4 1.7 %collective-permute-start.18 = (bf16[128,768]{1,0:T(8,128)(2,1)S(1)}, bf16[128,768]{1,0:T(8,128)(2,1)S(1)}, u32[]{:S(2)}, u32[]{:S(2)}) collective-permute-start(bf16[128,768]{1,0:T(8,128)(2,1)S(1)} %get-tuple-element.69), channel_id=1, source_target_pairs={{0,16},{1,17},{2,18},{3,19},{4,20},{5,21},{6,22},{7,23},{8,24},{9,... | collective-permute-start | bytes 589832 | tf_op jit(solution)/shard_map/ppermute | solution.py:44
  67.9 1.5 %collective-permute-start.19 = (bf16[128,768]{1,0:T(8,128)(2,1)S(1)}, bf16[128,768]{1,0:T(8,128)(2,1)S(1)}, u32[]{:S(2)}, u32[]{:S(2)}) collective-permute-start(bf16[128,768]{1,0:T(8,128)(2,1)S(1)} %get-tuple-element.70), channel_id=1, source_target_pairs={{0,16},{1,17},{2,18},{3,19},{4,20},{5,21},{6,22},{7,23},{8,24},{9,... | collective-permute-start | bytes 589832 | tf_op jit(solution)/shard_map/ppermute | solution.py:44
  68.0 1.7 %collective-permute-start.20 = (bf16[128,768]{1,0:T(8,128)(2,1)S(1)}, bf16[128,768]{1,0:T(8,128)(2,1)S(1)}, u32[]{:S(2)}, u32[]{:S(2)}) collective-permute-start(bf16[128,768]{1,0:T(8,128)(2,1)S(1)} %get-tuple-element.71), channel_id=1, source_target_pairs={{0,16},{1,17},{2,18},{3,19},{4,20},{5,21},{6,22},{7,23},{8,24},{9,... | collective-permute-start | bytes 589832 | tf_op jit(solution)/shard_map/ppermute | solution.py:44
  70.3 14.3 %collective-permute-start.21 = (bf16[512,768]{1,0:T(8,128)(2,1)S(1)}, bf16[512,768]{1,0:T(8,128)(2,1)S(1)}, u32[]{:S(2)}, u32[]{:S(2)}) collective-permute-start(bf16[512,768]{1,0:T(8,128)(2,1)S(1)} %shard_map.112), channel_id=1, source_target_pairs={{0,96},{1,97},{2,98},{3,99},{4,100},{5,101},{6,102},{7,103},{8,104... | collective-permute-start | bytes 2359304 | tf_op jit(solution)/shard_map/ppermute | solution.py:44
  80.7 13.3 %collective-permute-start.22 = (bf16[192,2048]{1,0:T(8,128)(2,1)S(1)}, bf16[192,2048]{1,0:T(8,128)(2,1)S(1)}, u32[]{:S(2)}, u32[]{:S(2)}) collective-permute-start(bf16[192,2048]{1,0:T(8,128)(2,1)S(1)} %shard_map.116), channel_id=1, source_target_pairs={{0,12},{1,13},{2,14},{3,15},{4,8},{5,9},{6,10},{7,11},{8,4},{9,5},... | collective-permute-start | bytes 2359304 | tf_op jit(solution)/shard_map/ppermute | solution.py:44
  83.9 3.6 %collective-permute-start.23 = (bf16[128,1024]{1,0:T(8,128)(2,1)S(1)}, bf16[128,1024]{1,0:T(8,128)(2,1)S(1)}, u32[]{:S(2)}, u32[]{:S(2)}) collective-permute-start(bf16[128,1024]{1,0:T(8,128)(2,1)S(1)} %get-tuple-element.76), channel_id=1, source_target_pairs={{0,16},{1,17},{2,18},{3,19},{4,20},{5,21},{6,22},{7,23},{8,24},{9,... | collective-permute-start | bytes 786440 | tf_op jit(solution)/shard_map/ppermute | solution.py:44
  84.0 3.7 %collective-permute-start.24 = (bf16[128,1024]{1,0:T(8,128)(2,1)S(1)}, bf16[128,1024]{1,0:T(8,128)(2,1)S(1)}, u32[]{:S(2)}, u32[]{:S(2)}) collective-permute-start(bf16[128,1024]{1,0:T(8,128)(2,1)S(1)} %get-tuple-element.77), channel_id=1, source_target_pairs={{0,16},{1,17},{2,18},{3,19},{4,20},{5,21},{6,22},{7,23},{8,24},{9,... | collective-permute-start | bytes 786440 | tf_op jit(solution)/shard_map/ppermute | solution.py:44
  84.5 3.2 %collective-permute-start.25 = (bf16[128,1024]{1,0:T(8,128)(2,1)S(1)}, bf16[128,1024]{1,0:T(8,128)(2,1)S(1)}, u32[]{:S(2)}, u32[]{:S(2)}) collective-permute-start(bf16[128,1024]{1,0:T(8,128)(2,1)S(1)} %get-tuple-element.78), channel_id=1, source_target_pairs={{0,16},{1,17},{2,18},{3,19},{4,20},{5,21},{6,22},{7,23},{8,24},{9,... | collective-permute-start | bytes 786440 | tf_op jit(solution)/shard_map/ppermute | solution.py:44
  84.6 3.1 %collective-permute-start.26 = (bf16[128,1024]{1,0:T(8,128)(2,1)S(1)}, bf16[128,1024]{1,0:T(8,128)(2,1)S(1)}, u32[]{:S(2)}, u32[]{:S(2)}) collective-permute-start(bf16[128,1024]{1,0:T(8,128)(2,1)S(1)} %get-tuple-element.79), channel_id=1, source_target_pairs={{0,16},{1,17},{2,18},{3,19},{4,20},{5,21},{6,22},{7,23},{8,24},{9,... | collective-permute-start | bytes 786440 | tf_op jit(solution)/shard_map/ppermute | solution.py:44
  87.6 6.9 %collective-permute-start.29 = (bf16[512,768]{1,0:T(8,128)(2,1)S(1)}, bf16[512,768]{1,0:T(8,128)(2,1)S(1)}, u32[]{:S(2)}, u32[]{:S(2)}) collective-permute-start(bf16[512,768]{1,0:T(8,128)(2,1)S(1)} %shard_map.113), channel_id=1, source_target_pairs={{0,16},{1,17},{2,18},{3,19},{4,20},{5,21},{6,22},{7,23},{8,24},{9,... | collective-permute-start | bytes 2359304 | tf_op jit(solution)/shard_map/ppermute | solution.py:44
  88.5 20.4 %collective-permute-start.32 = (bf16[512,1024]{1,0:T(8,128)(2,1)S(1)}, bf16[512,1024]{1,0:T(8,128)(2,1)S(1)}, u32[]{:S(2)}, u32[]{:S(2)}) collective-permute-start(bf16[512,1024]{1,0:T(8,128)(2,1)S(1)} %shard_map.119), channel_id=1, source_target_pairs={{0,96},{1,97},{2,98},{3,99},{4,100},{5,101},{6,102},{7,103},{8,104... | collective-permute-start | bytes 3145736 | tf_op jit(solution)/shard_map/ppermute | solution.py:44
  92.6 16.3 %collective-permute-start.31 = (bf16[512,1024]{1,0:T(8,128)(2,1)S(1)}, bf16[512,1024]{1,0:T(8,128)(2,1)S(1)}, u32[]{:S(2)}, u32[]{:S(2)}) collective-permute-start(bf16[512,1024]{1,0:T(8,128)(2,1)S(1)} %shard_map.120), channel_id=1, source_target_pairs={{0,16},{1,17},{2,18},{3,19},{4,20},{5,21},{6,22},{7,23},{8,24},{9,... | collective-permute-start | bytes 3145736 | tf_op jit(solution)/shard_map/ppermute | solution.py:44
  94.4 7.9 %collective-permute-start.27 = (bf16[96,2048]{1,0:T(8,128)(2,1)S(1)}, bf16[96,2048]{1,0:T(8,128)(2,1)S(1)}, u32[]{:S(2)}, u32[]{:S(2)}) collective-permute-start(bf16[96,2048]{1,0:T(8,128)(2,1)S(1)} %pad_maximum_fusion.1), channel_id=1, source_target_pairs={{0,4},{1,5},{2,6},{3,7},{4,0},{5,1},{6,2},{7,3},{8,12},{9,13},{10,... | collective-permute-start | bytes 1179656 | tf_op jit(solution)/shard_map/ppermute | solution.py:44
  94.9 7.3 %copy-start.4 = (f32[96,96]{1,0:T(8,128)S(1)}, f32[96,96]{1,0:T(8,128)}, u32[]{:S(2)}) copy-start(f32[96,96]{1,0:T(8,128)} %constant.8.clone) | copy-start | bytes 110596
  94.9 14.6 %collective-permute-start.30 = (bf16[256,768]{1,0:T(8,128)(2,1)S(1)}, bf16[256,768]{1,0:T(8,128)(2,1)S(1)}, u32[]{:S(2)}, u32[]{:S(2)}) collective-permute-start(bf16[256,768]{1,0:T(8,128)(2,1)S(1)} %fusion.7), channel_id=1, source_target_pairs={{0,32},{1,33},{2,34},{3,35},{4,36},{5,37},{6,38},{7,39},{8,40},{9,... | collective-permute-start | bytes 1179656 | tf_op jit(solution)/shard_map/ppermute | solution.py:44
  103.1 11.2 %collective-permute-start.28 = (bf16[48,2048]{1,0:T(8,128)(2,1)S(1)}, bf16[48,2048]{1,0:T(8,128)(2,1)S(1)}, u32[]{:S(2)}, u32[]{:S(2)}) collective-permute-start(bf16[48,2048]{1,0:T(8,128)(2,1)S(1)} %slice.140), channel_id=1, source_target_pairs={{0,3},{1,2},{2,1},{3,0},{4,7},{5,6},{6,5},{7,4},{8,11},{9,10},{10,... | collective-permute-start | bytes 589832 | tf_op jit(solution)/shard_map/ppermute | solution.py:44
  109.4 9.3 %collective-permute-start.34 = (bf16[256,1024]{1,0:T(8,128)(2,1)S(1)}, bf16[256,1024]{1,0:T(8,128)(2,1)S(1)}, u32[]{:S(2)}, u32[]{:S(2)}) collective-permute-start(bf16[256,1024]{1,0:T(8,128)(2,1)S(1)} %fusion.4), channel_id=1, source_target_pairs={{0,32},{1,33},{2,34},{3,35},{4,36},{5,37},{6,38},{7,39},{8,40},{9,... | collective-permute-start | bytes 1572872 | tf_op jit(solution)/shard_map/ppermute | solution.py:44
  114.3 4.4 %collective-permute-start.33 = (bf16[12,2048]{1,0:T(8,128)(2,1)S(1)}, bf16[12,2048]{1,0:T(8,128)(2,1)S(1)}, u32[]{:S(2)}, u32[]{:S(2)}) collective-permute-start(bf16[12,2048]{1,0:T(8,128)(2,1)S(1)} %get-tuple-element.101), channel_id=1, source_target_pairs={{0,128},{1,129},{2,130},{3,131},{4,132},{5,133},{6,134},{7,135},{8... | collective-permute-start | bytes 147464 | tf_op jit(solution)/shard_map/ppermute | solution.py:44
  115.2 5.3 %collective-permute-start.35 = (bf16[12,2048]{1,0:T(8,128)(2,1)S(1)}, bf16[12,2048]{1,0:T(8,128)(2,1)S(1)}, u32[]{:S(2)}, u32[]{:S(2)}) collective-permute-start(bf16[12,2048]{1,0:T(8,128)(2,1)S(1)} %get-tuple-element.100), channel_id=1, source_target_pairs={{0,1},{1,0},{2,3},{3,2},{4,5},{5,4},{6,7},{7,6},{8,9},{9,8},{10,11... | collective-permute-start | bytes 147464 | tf_op jit(solution)/shard_map/ppermute | solution.py:44
  116.9 4.6 %collective-permute-start.36 = (bf16[12,2048]{1,0:T(8,128)(2,1)S(1)}, bf16[12,2048]{1,0:T(8,128)(2,1)S(1)}, u32[]{:S(2)}, u32[]{:S(2)}) collective-permute-start(bf16[12,2048]{1,0:T(8,128)(2,1)S(1)} %get-tuple-element.99), channel_id=1, source_target_pairs={{0,129},{1,128},{2,131},{3,130},{4,133},{5,132},{6,135},{7,134},{8... | collective-permute-start | bytes 147464 | tf_op jit(solution)/shard_map/ppermute | solution.py:44

commit v5 on v4

--- a/solution.py
+++ b/solution.py
@@ -206,24 +206,20 @@
 
 
 def first_kernel(near, away, mine, *refs):
-    pieces, (rows, theirs, kept, given, sems) = refs[:-5], refs[-5:]
-    copies = []
-    at = 0
-    for n, piece in enumerate(pieces):
-        copies.append(pltpu.make_async_copy(piece, theirs.at[at : at + piece.shape[0]], sems.at[n]))
-        at += piece.shape[0]
-    for copy in copies:
-        copy.start()
+    pieces, (rows, kept, given) = refs[:-3], refs[-3:]
     part = near.shape[0] // 4
     for n, values in enumerate((near, away)):
         for q in range(2):
             for z in range(2):
                 to = (4 * z + 2 * n + q) * part
                 rows[to : to + part, :] = values[(2 * q + z) * part : (2 * q + z + 1) * part, :]
-    for copy in copies:
-        copy.wait()
     for span, to in tiles_of(FIRST, mine.shape[1] // 2):
-        result = products(rows, mine, theirs, span)
+        at = mine.shape[0]
+        result = jnp.dot(rows[:, :at], mine[:, span], preferred_element_type=F32)
+        for piece in pieces:
+            end = at + piece.shape[0]
+            result += jnp.dot(rows[:, at:end], piece[:, span], preferred_element_type=F32)
+            at = end
         kept[:, to] = result
         given[:, to] = result.astype(BF16)
 
@@ -233,17 +229,10 @@
     width = 2 * (FIRST[1] - FIRST[0])
     outs = (
         pltpu.VMEM((2 * group, features), BF16),
-        pltpu.VMEM(mine.shape, BF16),
         pltpu.VMEM((2 * group, width), F32),
         pltpu.VMEM((2 * group, width), BF16),
     )
-    return call(
-        first_kernel,
-        outs,
-        [VMEM] * 3 + [ANY] * len(pieces),
-        (VMEM,) * 4,
-        [pltpu.SemaphoreType.DMA((len(pieces),))],
-    )(near, away, mine, *pieces)
+    return call(first_kernel, outs, [VMEM] * (3 + len(pieces)), (VMEM,) * 3)(near, away, mine, *pieces)
 
 
 def second_kernel(rows, mine, theirs, kept, given):
@@ -449,7 +438,8 @@
     upstream = arrange(hidden_grad, rows)
     near, away, other_upstream = fence(near, away, send(upstream, TO_ZL))
 
-    inputs, theirs, kept_first, given = first_products(near, away, mine, theirs)
+    inputs, kept_first, given = first_products(near, away, mine, theirs)
+    theirs = stack(after(theirs[0], given), *theirs[1:])
     sent_first = send(given, TO_ZL)
     kept_second, given = second_products(inputs, mine, theirs)
     sent_second = send(given, TO_ZL)

time: 125 us -> 123 us (0.984)
    ppermute x37, waiting for transfers between devices: 48.8 us -> 47.6 us  [send(): return lax.ppermute(value, BOTH, pairs)]
    pallas_call x2 -> x3, Pallas kernels: 1.39 us -> 2.65 us  [stack(): call(stack_kernel, out, [ANY] * len(pieces), VMEM, [pltpu.SemaphoreType.D...]
  transfers between devices with their start and end apart: 37 -> 37, of which waited for: 17 -> 17; matrix products, arithmetic and copies ran while one was open for 3% -> 3% of each run, Pallas kernels for 13% -> 14%
where the time goes in v5:
time: 123 us; the launch traced here: 121 us
  starting transfers between devices  47.6 us (39%)
  waiting for transfers between devices  47.6 us (39%)
  Pallas kernels  21 us (17%)
  matrix products  3 us (2%)
    ppermute x37, starting transfers between devices, send(): return lax.ppermute(value, BOTH, pairs)  47.6 us
    ppermute x37, waiting for transfers between devices, send(): return lax.ppermute(value, BOTH, pairs)  47.6 us
    pallas_call x6, Pallas kernels, weight_product(): call(functools.partial(weight_kernel, first, len(added)), outs, [VMEM] *...  4 us
    pallas_call x3, Pallas kernels, stack(): call(stack_kernel, out, [ANY] * len(pieces), VMEM, [pltpu.SemaphoreType.D...  2.65 us
    pallas_call x1, Pallas kernels, backward(): call(functools.partial(backward_kernel, side), array((rows, 2 * mine.shap...  2.52 us
  transfers between devices with their start and end apart: 37, of which 17 were waited for; matrix products, arithmetic and copies ran while one was open for 3% of the time, Pallas kernels for 14%

profile of v5, /device:TPU:64, one launch (start us, length us, event | category | flops | bytes accessed | tf_op | source)
XLA Modules:
  0.0 121.1 jit_solution(8584320220302819069)
XLA Ops:
  0.7 1.2 %shard_map.103.refs_0_ = bf16[256,1792]{1,0:T(8,128)(2,1)S(1)} custom-call(bf16[256,896]{1,0:T(8,128)(2,1)} %gate.1, bf16[256,896]{1,0:T(8,128)(2,1)} %up.1), custom_call_target="tpu_custom_call" | custom-call | tf_op jit(solution)/shard_map/pallas_call | solution.py:93
  1.9 1.7 %collective-permute-start.4 = (bf16[256,1792]{1,0:T(8,128)(2,1)S(1)}, bf16[256,1792]{1,0:T(8,128)(2,1)S(1)}, u32[]{:S(2)}, u32[]{:S(2)}) collective-permute-start(bf16[256,1792]{1,0:T(8,128)(2,1)S(1)} %shard_map.103.refs_0_), channel_id=1, source_target_pairs={{0,32},{1,33},{2,34},{3,35},{4,36},{5,37},{6,38},{7,39},{8,40},{9,... | collective-permute-start | bytes 2752520 | tf_op jit(solution)/shard_map/ppermute | solution.py:44
  3.7 2.0 %collective-permute-start = (bf16[12,2048]{1,0:T(8,128)(2,1)S(1)}, bf16[12,2048]{1,0:T(8,128)(2,1)S(1)}, u32[]{:S(2)}, u32[]{:S(2)}) collective-permute-start(bf16[12,2048]{1,0:T(8,128)(2,1)S(1)} %get-tuple-element.49), channel_id=1, source_target_pairs={{0,128},{1,129},{2,130},{3,131},{4,132},{5,133},{6,134},{7,135},{8... | collective-permute-start | bytes 147464 | tf_op jit(solution)/shard_map/ppermute | solution.py:44
  5.7 1.6 %collective-permute-start.2 = (bf16[12,2048]{1,0:T(8,128)(2,1)S(1)}, bf16[12,2048]{1,0:T(8,128)(2,1)S(1)}, u32[]{:S(2)}, u32[]{:S(2)}) collective-permute-start(bf16[12,2048]{1,0:T(8,128)(2,1)S(1)} %get-tuple-element.49), channel_id=1, source_target_pairs={{0,129},{1,128},{2,131},{3,130},{4,133},{5,132},{6,135},{7,134},{8... | collective-permute-start | bytes 147464 | tf_op jit(solution)/shard_map/ppermute | solution.py:44
  7.3 2.2 %collective-permute-start.6 = (bf16[256,1792]{1,0:T(8,128)(2,1)S(1)}, bf16[256,1792]{1,0:T(8,128)(2,1)S(1)}, u32[]{:S(2)}, u32[]{:S(2)}) collective-permute-start(bf16[256,1792]{1,0:T(8,128)(2,1)S(1)} %shard_map.103.refs_0_), channel_id=1, source_target_pairs={{0,96},{1,97},{2,98},{3,99},{4,100},{5,101},{6,102},{7,103},{8,104... | collective-permute-start | bytes 2752520 | tf_op jit(solution)/shard_map/ppermute | solution.py:44
  9.5 1.5 %collective-permute-done.1 = bf16[12,2048]{1,0:T(8,128)(2,1)S(1)} collective-permute-done((bf16[12,2048]{1,0:T(8,128)(2,1)S(1)}, bf16[12,2048]{1,0:T(8,128)(2,1)S(1)}, u32[]{:S(2)}, u32[]{:S(2)}) %collective-permute-start.1) | collective-permute-done | bytes 49184 | tf_op jit(solution)/shard_map/ppermute | solution.py:44
  11.0 5.7 %collective-permute-start.7 = (bf16[256,1792]{1,0:T(8,128)(2,1)S(1)}, bf16[256,1792]{1,0:T(8,128)(2,1)S(1)}, u32[]{:S(2)}, u32[]{:S(2)}) collective-permute-start(bf16[256,1792]{1,0:T(8,128)(2,1)S(1)} %shard_map.103.refs_0_), channel_id=1, source_target_pairs={{0,16},{1,17},{2,18},{3,19},{4,20},{5,21},{6,22},{7,23},{8,24},{9,... | collective-permute-start | bytes 2752520 | tf_op jit(solution)/shard_map/ppermute | solution.py:44
  16.7 0.5 collective-permute-start.3
  17.3 1.1 collective-permute-done.4.refs_1_.refs_0_
  18.3 5.3 %collective-permute-start.10 = (bf16[256,1792]{1,0:T(8,128)(2,1)S(1)}, bf16[256,1792]{1,0:T(8,128)(2,1)S(1)}, u32[]{:S(2)}, u32[]{:S(2)}) collective-permute-start(bf16[256,1792]{1,0:T(8,128)(2,1)S(1)} %collective-permute-done.4.refs_1_.refs_0_), channel_id=1, source_target_pairs={{0,96},{1,97},{2,98},{3,99},{4,100},{5,101},{6,102},{7,103},{8,104... | collective-permute-start | bytes 2752520 | tf_op jit(solution)/shard_map/ppermute | solution.py:44
  23.9 1.1 collective-permute-done.3
  25.2 1.6 %collective-permute-start.5 = (bf16[96,2048]{1,0:T(8,128)(2,1)S(1)}, bf16[96,2048]{1,0:T(8,128)(2,1)S(1)}, u32[]{:S(2)}, u32[]{:S(2)}) collective-permute-start(bf16[96,2048]{1,0:T(8,128)(2,1)S(1)} %fusion.1), channel_id=1, source_target_pairs={{0,4},{1,5},{2,6},{3,7},{4,0},{5,1},{6,2},{7,3},{8,12},{9,13},{10,... | collective-permute-start | bytes 1179656 | tf_op jit(solution)/shard_map/ppermute | solution.py:44
  27.1 2.3 %collective-permute-start.9 = (bf16[192,896]{1,0:T(8,128)(2,1)S(1)}, bf16[192,896]{1,0:T(8,128)(2,1)S(1)}, u32[]{:S(2)}, u32[]{:S(2)}) collective-permute-start(bf16[192,896]{1,0:T(8,128)(2,1)S(1)} %shard_map.105.own_stream), channel_id=1, source_target_pairs={{0,128},{1,129},{2,130},{3,131},{4,132},{5,133},{6,134},{7,135},{8... | collective-permute-start | bytes 1032200 | tf_op jit(solution)/shard_map/ppermute | solution.py:44
  29.4 3.7 %collective-permute-done.5 = bf16[96,2048]{1,0:T(8,128)(2,1)S(1)} collective-permute-done((bf16[96,2048]{1,0:T(8,128)(2,1)S(1)}, bf16[96,2048]{1,0:T(8,128)(2,1)S(1)}, u32[]{:S(2)}, u32[]{:S(2)}) %collective-permute-start.5) | collective-permute-done | bytes 393248 | tf_op jit(solution)/shard_map/ppermute | solution.py:44
  33.1 2.8 %collective-permute-start.8 = (bf16[192,2048]{1,0:T(8,128)(2,1)S(1)}, bf16[192,2048]{1,0:T(8,128)(2,1)S(1)}, u32[]{:S(2)}, u32[]{:S(2)}) collective-permute-start(bf16[192,2048]{1,0:T(8,128)(2,1)S(1)} %pad_maximum_fusion.near), channel_id=1, source_target_pairs={{0,12},{1,13},{2,14},{3,15},{4,8},{5,9},{6,10},{7,11},{8,4},{9,5},... | collective-permute-start | bytes 2359304 | tf_op jit(solution)/shard_map/ppermute | solution.py:44
  36.5 0.9 shard_map.106.mine
  37.6 0.6 collective-permute-start.11
  38.3 0.5 collective-permute-start.13
  38.8 7.6 %collective-permute-done.8.away = bf16[192,2048]{1,0:T(8,128)(2,1)S(1)} collective-permute-done((bf16[192,2048]{1,0:T(8,128)(2,1)S(1)}, bf16[192,2048]{1,0:T(8,128)(2,1)S(1)}, u32[]{:S(2)}, u32[]{:S(2)}) %collective-permute-start.8) | collective-permute-done | bytes 786464 | tf_op jit(solution)/shard_map/ppermute | solution.py:44
  46.4 2.0 %shard_map.108 = (bf16[384,2048]{1,0:T(8,128)(2,1)S(1)}, f32[384,768]{1,0:T(8,128)S(1)}, bf16[384,768]{1,0:T(8,128)(2,1)S(1)}) custom-call(bf16[192,2048]{1,0:T(8,128)(2,1)S(1)} %pad_maximum_fusion.near, bf16[192,2048]{1,0:T(8,128)(2,1)S(1)} %collective-permute-done.8.away, bf16[1024,1792]{1,0:T(8,128)(2,1)S(1)} %shard_map.106.mine, ...), custom_call_target="tpu_custom_call" | custom-call | tf_op jit(solution)/shard_map/pallas_call | solution.py:235
  48.4 2.5 %collective-permute-start.15 = (bf16[384,768]{1,0:T(8,128)(2,1)S(1)}, bf16[384,768]{1,0:T(8,128)(2,1)S(1)}, u32[]{:S(2)}, u32[]{:S(2)}) collective-permute-start(bf16[384,768]{1,0:T(8,128)(2,1)S(1)} %get-tuple-element.61), channel_id=1, source_target_pairs={{0,128},{1,129},{2,130},{3,131},{4,132},{5,133},{6,134},{7,135},{8... | collective-permute-start | bytes 1769480 | tf_op jit(solution)/shard_map/ppermute | solution.py:44
  50.9 1.3 %shard_map.109.theirs = bf16[1024,1792]{1,0:T(8,128)(2,1)S(1)} custom-call(bf16[256,1792]{1,0:T(8,128)(2,1)S(1)} %collective-permute-done.7.refs_0_, bf16[192,1792]{1,0:T(8,128)(2,1)S(1)} %collective-permute-done.11.refs_1_, bf16[192,1792]{1,0:T(8,128)(2,1)S(1)} %collective-permute-done.12.refs_2_, bf16[128,1792]{1,0:T(8,128)(2,1)S(1)} %collective-permute-done.13.refs_3_, ...), custom_call_target="tpu_custom_call" | custom-call | tf_op jit(solution)/shard_map/pallas_call | solution.py:184
  52.2 1.8 %shard_map.110 = (f32[384,1024]{1,0:T(8,128)S(1)}, bf16[384,1024]{1,0:T(8,128)(2,1)S(1)}) custom-call(bf16[384,2048]{1,0:T(8,128)(2,1)S(1)} %get-tuple-element.62.rows.inputs, bf16[1024,1792]{1,0:T(8,128)(2,1)S(1)} %shard_map.106.mine, bf16[1024,1792]{1,0:T(8,128)(2,1)S(1)} %shard_map.109.theirs), custom_call_target="tpu_custom_call" | custom-call | tf_op jit(solution)/shard_map/pallas_call | solution.py:248
  54.1 11.1 %collective-permute-done.15.sent = bf16[384,768]{1,0:T(8,128)(2,1)S(1)} collective-permute-done((bf16[384,768]{1,0:T(8,128)(2,1)S(1)}, bf16[384,768]{1,0:T(8,128)(2,1)S(1)}, u32[]{:S(2)}, u32[]{:S(2)}) %collective-permute-start.15) | collective-permute-done | bytes 589856 | tf_op jit(solution)/shard_map/ppermute | solution.py:44
  65.5 0.6 shard_map.112
  66.2 0.5 collective-permute-start.18
  68.5 0.6 shard_map.113
  69.2 0.6 shard_map.114
  69.8 2.0 %shard_map.115.before = f32[192,2048]{1,0:T(8,128)S(1)} custom-call(bf16[384,768]{1,0:T(8,128)(2,1)S(1)} %shard_map.111.grad.first, bf16[1024,1792]{1,0:T(8,128)(2,1)S(1)} %shard_map.106.mine, bf16[1024,1792]{1,0:T(8,128)(2,1)S(1)} %shard_map.109.theirs), custom_call_target="tpu_custom_call" | custom-call | tf_op jit(solution)/shard_map/pallas_call | solution.py:347
  71.8 5.7 %collective-permute-done.16.sent = bf16[384,1024]{1,0:T(8,128)(2,1)S(1)} collective-permute-done((bf16[384,1024]{1,0:T(8,128)(2,1)S(1)}, bf16[384,1024]{1,0:T(8,128)(2,1)S(1)}, u32[]{:S(2)}, u32[]{:S(2)}) %collective-permute-start.16) | collective-permute-done | bytes 786464 | tf_op jit(solution)/shard_map/ppermute | solution.py:44
  78.0 1.5 %shard_map.117 = bf16[192,2048]{1,0:T(8,128)(2,1)S(1)} custom-call(f32[192,2048]{1,0:T(8,128)S(1)} %shard_map.115.before, bf16[384,1024]{1,0:T(8,128)(2,1)S(1)} %shard_map.116.second.grad, bf16[1024,1792]{1,0:T(8,128)(2,1)S(1)} %shard_map.106.mine, bf16[1024,1792]{1,0:T(8,128)(2,1)S(1)} %shard_map.109.theirs), custom_call_target="tpu_custom_call" | custom-call | tf_op jit(solution)/shard_map/pallas_call | solution.py:376
  79.5 2.5 %collective-permute-start.22 = (bf16[192,2048]{1,0:T(8,128)(2,1)S(1)}, bf16[192,2048]{1,0:T(8,128)(2,1)S(1)}, u32[]{:S(2)}, u32[]{:S(2)}) collective-permute-start(bf16[192,2048]{1,0:T(8,128)(2,1)S(1)} %shard_map.117), channel_id=1, source_target_pairs={{0,12},{1,13},{2,14},{3,15},{4,8},{5,9},{6,10},{7,11},{8,4},{9,5},... | collective-permute-start | bytes 2359304 | tf_op jit(solution)/shard_map/ppermute | solution.py:44
  82.0 0.7 shard_map.118
  83.8 2.5 %shard_map.119 = bf16[192,2048]{1,0:T(8,128)(2,1)S(1)} custom-call(bf16[384,768]{1,0:T(8,128)(2,1)S(1)} %shard_map.111.grad.first, bf16[384,1024]{1,0:T(8,128)(2,1)S(1)} %shard_map.116.second.grad, bf16[1024,1792]{1,0:T(8,128)(2,1)S(1)} %shard_map.106.mine, bf16[1024,1792]{1,0:T(8,128)(2,1)S(1)} %shard_map.109.theirs), custom_call_target="tpu_custom_call" | custom-call | tf_op jit(solution)/shard_map/pallas_call | solution.py:287
  86.6 0.7 shard_map.120
  87.3 3.3 %collective-permute-start.32 = (bf16[512,1024]{1,0:T(8,128)(2,1)S(1)}, bf16[512,1024]{1,0:T(8,128)(2,1)S(1)}, u32[]{:S(2)}, u32[]{:S(2)}) collective-permute-start(bf16[512,1024]{1,0:T(8,128)(2,1)S(1)} %shard_map.120), channel_id=1, source_target_pairs={{0,96},{1,97},{2,98},{3,99},{4,100},{5,101},{6,102},{7,103},{8,104... | collective-permute-start | bytes 3145736 | tf_op jit(solution)/shard_map/ppermute | solution.py:44
  90.6 0.7 shard_map.121
  91.5 1.3 %collective-permute-done.22 = bf16[192,2048]{1,0:T(8,128)(2,1)S(1)} collective-permute-done((bf16[192,2048]{1,0:T(8,128)(2,1)S(1)}, bf16[192,2048]{1,0:T(8,128)(2,1)S(1)}, u32[]{:S(2)}, u32[]{:S(2)}) %collective-permute-start.22) | collective-permute-done | bytes 786464 | tf_op jit(solution)/shard_map/ppermute | solution.py:44
  94.3 6.8 %collective-permute-done.27 = bf16[96,2048]{1,0:T(8,128)(2,1)S(1)} collective-permute-done((bf16[96,2048]{1,0:T(8,128)(2,1)S(1)}, bf16[96,2048]{1,0:T(8,128)(2,1)S(1)}, u32[]{:S(2)}, u32[]{:S(2)}) %collective-permute-start.27) | collective-permute-done | bytes 393248 | tf_op jit(solution)/shard_map/ppermute | solution.py:44
  101.0 0.8 fusion.8
  101.9 5.8 %collective-permute-start.28 = (bf16[48,2048]{1,0:T(8,128)(2,1)S(1)}, bf16[48,2048]{1,0:T(8,128)(2,1)S(1)}, u32[]{:S(2)}, u32[]{:S(2)}) collective-permute-start(bf16[48,2048]{1,0:T(8,128)(2,1)S(1)} %slice.140), channel_id=1, source_target_pairs={{0,3},{1,2},{2,1},{3,0},{4,7},{5,6},{6,5},{7,4},{8,11},{9,10},{10,... | collective-permute-start | bytes 589832 | tf_op jit(solution)/shard_map/ppermute | solution.py:44
  108.3 4.7 %collective-permute-done.28 = bf16[48,2048]{1,0:T(8,128)(2,1)S(1)} collective-permute-done((bf16[48,2048]{1,0:T(8,128)(2,1)S(1)}, bf16[48,2048]{1,0:T(8,128)(2,1)S(1)}, u32[]{:S(2)}, u32[]{:S(2)}) %collective-permute-start.28) | collective-permute-done | bytes 196640 | tf_op jit(solution)/shard_map/ppermute | solution.py:44
  113.1 0.8 collective-permute-start.33
  114.0 1.8 %collective-permute-start.35 = (bf16[12,2048]{1,0:T(8,128)(2,1)S(1)}, bf16[12,2048]{1,0:T(8,128)(2,1)S(1)}, u32[]{:S(2)}, u32[]{:S(2)}) collective-permute-start(bf16[12,2048]{1,0:T(8,128)(2,1)S(1)} %get-tuple-element.100), channel_id=1, source_target_pairs={{0,1},{1,0},{2,3},{3,2},{4,5},{5,4},{6,7},{7,6},{8,9},{9,8},{10,11... | collective-permute-start | bytes 147464 | tf_op jit(solution)/shard_map/ppermute | solution.py:44
  115.7 1.0 collective-permute-start.36
  117.5 1.4 %shard_map.123 = (f32[256,896]{1,0:T(8,128)}, f32[256,896]{1,0:T(8,128)}) custom-call(f32[256,768]{1,0:T(8,128)S(1)} %fusion.6.first, f32[256,1024]{1,0:T(8,128)S(1)} %fusion.2.second, bf16[256,768]{1,0:T(8,128)(2,1)S(1)} %collective-permute-done.30.first_last, bf16[256,1024]{1,0:T(8,128)(2,1)S(1)} %collective-permute-done.34.second_last), custom_call_target="tpu_custom_call" | custom-call | tf_op jit(solution)/shard_map/pallas_call | solution.py:396
  119.2 1.2 collective-permute-done.36.from_both
  120.4 0.7 shard_map.122
  (80 shorter events, 9.3 us)
Async XLA Ops:
  0.6 23.0 %copy-start.5 = (bf16[96,48]{1,0:T(8,128)(2,1)S(1)}, bf16[96,48]{1,0:T(8,128)(2,1)}, u32[]{:S(2)}) copy-start(bf16[96,48]{1,0:T(8,128)(2,1)} %constant.11) | copy-start | bytes 27652
  0.6 24.3 %copy-start.6 = (bf16[96,48]{1,0:T(8,128)(2,1)S(1)}, bf16[96,48]{1,0:T(8,128)(2,1)}, u32[]{:S(2)}) copy-start(bf16[96,48]{1,0:T(8,128)(2,1)} %constant.12) | copy-start | bytes 27652
  0.7 2.9 %copy-start.1 = (bf16[12,4096]{1,0:T(8,128)(2,1)S(1)}, bf16[12,4096]{1,0:T(8,128)(2,1)}, u32[]{:S(2)}) copy-start(bf16[12,4096]{1,0:T(8,128)(2,1)} %codes) | copy-start | bytes 294916
  0.7 2.9 %copy-start.3 = (bf16[12,32]{1,0:T(8,128)(2,1)S(1)}, bf16[12,32]{1,0:T(8,128)(2,1)}, u32[]{:S(2)}) copy-start(bf16[12,32]{1,0:T(8,128)(2,1)} %scales) | copy-start | bytes 2308
  1.9 24.9 %copy-start = (bf16[192,896]{1,0:T(8,128)(2,1)S(1)}, bf16[192,896]{1,0:T(8,128)(2,1)}, u32[]{:S(2)}) copy-start(bf16[192,896]{1,0:T(8,128)(2,1)} %values.1) | copy-start | bytes 1032196
  1.9 24.9 %copy-start.2 = (s32[32,1,192]{2,1,0:T(1,128)S(1)}, s32[32,1,192]{2,1,0:T(1,128)}, u32[]{:S(2)}) copy-start(s32[32,1,192]{2,1,0:T(1,128)} %constant.7.clone.table) | copy-start | bytes 73732
  1.9 16.4 %collective-permute-start.4 = (bf16[256,1792]{1,0:T(8,128)(2,1)S(1)}, bf16[256,1792]{1,0:T(8,128)(2,1)S(1)}, u32[]{:S(2)}, u32[]{:S(2)}) collective-permute-start(bf16[256,1792]{1,0:T(8,128)(2,1)S(1)} %shard_map.103.refs_0_), channel_id=1, source_target_pairs={{0,32},{1,33},{2,34},{3,35},{4,36},{5,37},{6,38},{7,39},{8,40},{9,... | collective-permute-start | bytes 2752520 | tf_op jit(solution)/shard_map/ppermute | solution.py:44
  3.7 5.8 %collective-permute-start = (bf16[12,2048]{1,0:T(8,128)(2,1)S(1)}, bf16[12,2048]{1,0:T(8,128)(2,1)S(1)}, u32[]{:S(2)}, u32[]{:S(2)}) collective-permute-start(bf16[12,2048]{1,0:T(8,128)(2,1)S(1)} %get-tuple-element.49), channel_id=1, source_target_pairs={{0,128},{1,129},{2,130},{3,131},{4,132},{5,133},{6,134},{7,135},{8... | collective-permute-start | bytes 147464 | tf_op jit(solution)/shard_map/ppermute | solution.py:44
  5.7 5.2 %collective-permute-start.1 = (bf16[12,2048]{1,0:T(8,128)(2,1)S(1)}, bf16[12,2048]{1,0:T(8,128)(2,1)S(1)}, u32[]{:S(2)}, u32[]{:S(2)}) collective-permute-start(bf16[12,2048]{1,0:T(8,128)(2,1)S(1)} %get-tuple-element.48), channel_id=1, source_target_pairs={{0,1},{1,0},{2,3},{3,2},{4,5},{5,4},{6,7},{7,6},{8,9},{9,8},{10,11... | collective-permute-start | bytes 147464 | tf_op jit(solution)/shard_map/ppermute | solution.py:44
  5.7 5.2 %collective-permute-start.2 = (bf16[12,2048]{1,0:T(8,128)(2,1)S(1)}, bf16[12,2048]{1,0:T(8,128)(2,1)S(1)}, u32[]{:S(2)}, u32[]{:S(2)}) collective-permute-start(bf16[12,2048]{1,0:T(8,128)(2,1)S(1)} %get-tuple-element.49), channel_id=1, source_target_pairs={{0,129},{1,128},{2,131},{3,130},{4,133},{5,132},{6,135},{7,134},{8... | collective-permute-start | bytes 147464 | tf_op jit(solution)/shard_map/ppermute | solution.py:44
  7.3 22.1 %collective-permute-start.6 = (bf16[256,1792]{1,0:T(8,128)(2,1)S(1)}, bf16[256,1792]{1,0:T(8,128)(2,1)S(1)}, u32[]{:S(2)}, u32[]{:S(2)}) collective-permute-start(bf16[256,1792]{1,0:T(8,128)(2,1)S(1)} %shard_map.103.refs_0_), channel_id=1, source_target_pairs={{0,96},{1,97},{2,98},{3,99},{4,100},{5,101},{6,102},{7,103},{8,104... | collective-permute-start | bytes 2752520 | tf_op jit(solution)/shard_map/ppermute | solution.py:44
  11.0 18.4 %collective-permute-start.7 = (bf16[256,1792]{1,0:T(8,128)(2,1)S(1)}, bf16[256,1792]{1,0:T(8,128)(2,1)S(1)}, u32[]{:S(2)}, u32[]{:S(2)}) collective-permute-start(bf16[256,1792]{1,0:T(8,128)(2,1)S(1)} %shard_map.103.refs_0_), channel_id=1, source_target_pairs={{0,16},{1,17},{2,18},{3,19},{4,20},{5,21},{6,22},{7,23},{8,24},{9,... | collective-permute-start | bytes 2752520 | tf_op jit(solution)/shard_map/ppermute | solution.py:44
  16.7 8.2 %collective-permute-start.3 = (bf16[48,2048]{1,0:T(8,128)(2,1)S(1)}, bf16[48,2048]{1,0:T(8,128)(2,1)S(1)}, u32[]{:S(2)}, u32[]{:S(2)}) collective-permute-start(bf16[48,2048]{1,0:T(8,128)(2,1)S(1)} %pad_maximum_fusion.2), channel_id=1, source_target_pairs={{0,3},{1,2},{2,1},{3,0},{4,7},{5,6},{6,5},{7,4},{8,11},{9,10},{10,... | collective-permute-start | bytes 589832 | tf_op jit(solution)/shard_map/ppermute | solution.py:44
  18.3 18.1 %collective-permute-start.10 = (bf16[256,1792]{1,0:T(8,128)(2,1)S(1)}, bf16[256,1792]{1,0:T(8,128)(2,1)S(1)}, u32[]{:S(2)}, u32[]{:S(2)}) collective-permute-start(bf16[256,1792]{1,0:T(8,128)(2,1)S(1)} %collective-permute-done.4.refs_1_.refs_0_), channel_id=1, source_target_pairs={{0,96},{1,97},{2,98},{3,99},{4,100},{5,101},{6,102},{7,103},{8,104... | collective-permute-start | bytes 2752520 | tf_op jit(solution)/shard_map/ppermute | solution.py:44
  25.2 7.9 %collective-permute-start.5 = (bf16[96,2048]{1,0:T(8,128)(2,1)S(1)}, bf16[96,2048]{1,0:T(8,128)(2,1)S(1)}, u32[]{:S(2)}, u32[]{:S(2)}) collective-permute-start(bf16[96,2048]{1,0:T(8,128)(2,1)S(1)} %fusion.1), channel_id=1, source_target_pairs={{0,4},{1,5},{2,6},{3,7},{4,0},{5,1},{6,2},{7,3},{8,12},{9,13},{10,... | collective-permute-start | bytes 1179656 | tf_op jit(solution)/shard_map/ppermute | solution.py:44
  27.1 11.2 %collective-permute-start.9 = (bf16[192,896]{1,0:T(8,128)(2,1)S(1)}, bf16[192,896]{1,0:T(8,128)(2,1)S(1)}, u32[]{:S(2)}, u32[]{:S(2)}) collective-permute-start(bf16[192,896]{1,0:T(8,128)(2,1)S(1)} %shard_map.105.own_stream), channel_id=1, source_target_pairs={{0,128},{1,129},{2,130},{3,131},{4,132},{5,133},{6,134},{7,135},{8... | collective-permute-start | bytes 1032200 | tf_op jit(solution)/shard_map/ppermute | solution.py:44
  33.1 13.3 %collective-permute-start.8 = (bf16[192,2048]{1,0:T(8,128)(2,1)S(1)}, bf16[192,2048]{1,0:T(8,128)(2,1)S(1)}, u32[]{:S(2)}, u32[]{:S(2)}) collective-permute-start(bf16[192,2048]{1,0:T(8,128)(2,1)S(1)} %pad_maximum_fusion.near), channel_id=1, source_target_pairs={{0,12},{1,13},{2,14},{3,15},{4,8},{5,9},{6,10},{7,11},{8,4},{9,5},... | collective-permute-start | bytes 2359304 | tf_op jit(solution)/shard_map/ppermute | solution.py:44
  37.4 9.0 %collective-permute-start.14 = (bf16[256,1792]{1,0:T(8,128)(2,1)S(1)}, bf16[256,1792]{1,0:T(8,128)(2,1)S(1)}, u32[]{:S(2)}, u32[]{:S(2)}) collective-permute-start(bf16[256,1792]{1,0:T(8,128)(2,1)S(1)} %collective-permute-done.10.refs_3_), channel_id=1, source_target_pairs={{0,16},{1,17},{2,18},{3,19},{4,20},{5,21},{6,22},{7,23},{8,24},{9,... | collective-permute-start | bytes 2752520 | tf_op jit(solution)/shard_map/ppermute | solution.py:44
  37.6 8.8 %collective-permute-start.11 = (bf16[192,1792]{1,0:T(8,128)(2,1)S(1)}, bf16[192,1792]{1,0:T(8,128)(2,1)S(1)}, u32[]{:S(2)}, u32[]{:S(2)}) collective-permute-start(bf16[192,1792]{1,0:T(8,128)(2,1)S(1)} %get-tuple-element.92), channel_id=1, source_target_pairs={{0,16},{1,17},{2,18},{3,19},{4,20},{5,21},{6,22},{7,23},{8,24},{9,... | collective-permute-start | bytes 2064392 | tf_op jit(solution)/shard_map/ppermute | solution.py:44
  38.2 8.3 %collective-permute-start.12 = (bf16[192,1792]{1,0:T(8,128)(2,1)S(1)}, bf16[192,1792]{1,0:T(8,128)(2,1)S(1)}, u32[]{:S(2)}, u32[]{:S(2)}) collective-permute-start(bf16[192,1792]{1,0:T(8,128)(2,1)S(1)} %get-tuple-element.91), channel_id=1, source_target_pairs={{0,16},{1,17},{2,18},{3,19},{4,20},{5,21},{6,22},{7,23},{8,24},{9,... | collective-permute-start | bytes 2064392 | tf_op jit(solution)/shard_map/ppermute | solution.py:44
  38.3 8.1 %collective-permute-start.13 = (bf16[128,1792]{1,0:T(8,128)(2,1)S(1)}, bf16[128,1792]{1,0:T(8,128)(2,1)S(1)}, u32[]{:S(2)}, u32[]{:S(2)}) collective-permute-start(bf16[128,1792]{1,0:T(8,128)(2,1)S(1)} %slice.104), channel_id=1, source_target_pairs={{0,16},{1,17},{2,18},{3,19},{4,20},{5,21},{6,22},{7,23},{8,24},{9,... | collective-permute-start | bytes 1376264 | tf_op jit(solution)/shard_map/ppermute | solution.py:44
  48.4 16.7 %collective-permute-start.15 = (bf16[384,768]{1,0:T(8,128)(2,1)S(1)}, bf16[384,768]{1,0:T(8,128)(2,1)S(1)}, u32[]{:S(2)}, u32[]{:S(2)}) collective-permute-start(bf16[384,768]{1,0:T(8,128)(2,1)S(1)} %get-tuple-element.61), channel_id=1, source_target_pairs={{0,128},{1,129},{2,130},{3,131},{4,132},{5,133},{6,134},{7,135},{8... | collective-permute-start | bytes 1769480 | tf_op jit(solution)/shard_map/ppermute | solution.py:44
  54.0 23.6 %collective-permute-start.16 = (bf16[384,1024]{1,0:T(8,128)(2,1)S(1)}, bf16[384,1024]{1,0:T(8,128)(2,1)S(1)}, u32[]{:S(2)}, u32[]{:S(2)}) collective-permute-start(bf16[384,1024]{1,0:T(8,128)(2,1)S(1)} %get-tuple-element.67), channel_id=1, source_target_pairs={{0,128},{1,129},{2,130},{3,131},{4,132},{5,133},{6,134},{7,135},{8... | collective-permute-start | bytes 2359304 | tf_op jit(solution)/shard_map/ppermute | solution.py:44
  66.1 1.5 %collective-permute-start.17 = (bf16[128,768]{1,0:T(8,128)(2,1)S(1)}, bf16[128,768]{1,0:T(8,128)(2,1)S(1)}, u32[]{:S(2)}, u32[]{:S(2)}) collective-permute-start(bf16[128,768]{1,0:T(8,128)(2,1)S(1)} %get-tuple-element.68), channel_id=1, source_target_pairs={{0,16},{1,17},{2,18},{3,19},{4,20},{5,21},{6,22},{7,23},{8,24},{9,... | collective-permute-start | bytes 589832 | tf_op jit(solution)/shard_map/ppermute | solution.py:44
  66.2 1.7 %collective-permute-start.18 = (bf16[128,768]{1,0:T(8,128)(2,1)S(1)}, bf16[128,768]{1,0:T(8,128)(2,1)S(1)}, u32[]{:S(2)}, u32[]{:S(2)}) collective-permute-start(bf16[128,768]{1,0:T(8,128)(2,1)S(1)} %get-tuple-element.69), channel_id=1, source_target_pairs={{0,16},{1,17},{2,18},{3,19},{4,20},{5,21},{6,22},{7,23},{8,24},{9,... | collective-permute-start | bytes 589832 | tf_op jit(solution)/shard_map/ppermute | solution.py:44
  66.7 1.5 %collective-permute-start.19 = (bf16[128,768]{1,0:T(8,128)(2,1)S(1)}, bf16[128,768]{1,0:T(8,128)(2,1)S(1)}, u32[]{:S(2)}, u32[]{:S(2)}) collective-permute-start(bf16[128,768]{1,0:T(8,128)(2,1)S(1)} %get-tuple-element.70), channel_id=1, source_target_pairs={{0,16},{1,17},{2,18},{3,19},{4,20},{5,21},{6,22},{7,23},{8,24},{9,... | collective-permute-start | bytes 589832 | tf_op jit(solution)/shard_map/ppermute | solution.py:44
  66.8 1.7 %collective-permute-start.20 = (bf16[128,768]{1,0:T(8,128)(2,1)S(1)}, bf16[128,768]{1,0:T(8,128)(2,1)S(1)}, u32[]{:S(2)}, u32[]{:S(2)}) collective-permute-start(bf16[128,768]{1,0:T(8,128)(2,1)S(1)} %get-tuple-element.71), channel_id=1, source_target_pairs={{0,16},{1,17},{2,18},{3,19},{4,20},{5,21},{6,22},{7,23},{8,24},{9,... | collective-permute-start | bytes 589832 | tf_op jit(solution)/shard_map/ppermute | solution.py:44
  69.1 14.3 %collective-permute-start.21 = (bf16[512,768]{1,0:T(8,128)(2,1)S(1)}, bf16[512,768]{1,0:T(8,128)(2,1)S(1)}, u32[]{:S(2)}, u32[]{:S(2)}) collective-permute-start(bf16[512,768]{1,0:T(8,128)(2,1)S(1)} %shard_map.113), channel_id=1, source_target_pairs={{0,96},{1,97},{2,98},{3,99},{4,100},{5,101},{6,102},{7,103},{8,104... | collective-permute-start | bytes 2359304 | tf_op jit(solution)/shard_map/ppermute | solution.py:44
  79.5 13.3 %collective-permute-start.22 = (bf16[192,2048]{1,0:T(8,128)(2,1)S(1)}, bf16[192,2048]{1,0:T(8,128)(2,1)S(1)}, u32[]{:S(2)}, u32[]{:S(2)}) collective-permute-start(bf16[192,2048]{1,0:T(8,128)(2,1)S(1)} %shard_map.117), channel_id=1, source_target_pairs={{0,12},{1,13},{2,14},{3,15},{4,8},{5,9},{6,10},{7,11},{8,4},{9,5},... | collective-permute-start | bytes 2359304 | tf_op jit(solution)/shard_map/ppermute | solution.py:44
  82.7 3.6 %collective-permute-start.23 = (bf16[128,1024]{1,0:T(8,128)(2,1)S(1)}, bf16[128,1024]{1,0:T(8,128)(2,1)S(1)}, u32[]{:S(2)}, u32[]{:S(2)}) collective-permute-start(bf16[128,1024]{1,0:T(8,128)(2,1)S(1)} %get-tuple-element.76), channel_id=1, source_target_pairs={{0,16},{1,17},{2,18},{3,19},{4,20},{5,21},{6,22},{7,23},{8,24},{9,... | collective-permute-start | bytes 786440 | tf_op jit(solution)/shard_map/ppermute | solution.py:44
  82.8 3.7 %collective-permute-start.24 = (bf16[128,1024]{1,0:T(8,128)(2,1)S(1)}, bf16[128,1024]{1,0:T(8,128)(2,1)S(1)}, u32[]{:S(2)}, u32[]{:S(2)}) collective-permute-start(bf16[128,1024]{1,0:T(8,128)(2,1)S(1)} %get-tuple-element.77), channel_id=1, source_target_pairs={{0,16},{1,17},{2,18},{3,19},{4,20},{5,21},{6,22},{7,23},{8,24},{9,... | collective-permute-start | bytes 786440 | tf_op jit(solution)/shard_map/ppermute | solution.py:44
  83.3 3.2 %collective-permute-start.25 = (bf16[128,1024]{1,0:T(8,128)(2,1)S(1)}, bf16[128,1024]{1,0:T(8,128)(2,1)S(1)}, u32[]{:S(2)}, u32[]{:S(2)}) collective-permute-start(bf16[128,1024]{1,0:T(8,128)(2,1)S(1)} %get-tuple-element.78), channel_id=1, source_target_pairs={{0,16},{1,17},{2,18},{3,19},{4,20},{5,21},{6,22},{7,23},{8,24},{9,... | collective-permute-start | bytes 786440 | tf_op jit(solution)/shard_map/ppermute | solution.py:44
  83.4 3.1 %collective-permute-start.26 = (bf16[128,1024]{1,0:T(8,128)(2,1)S(1)}, bf16[128,1024]{1,0:T(8,128)(2,1)S(1)}, u32[]{:S(2)}, u32[]{:S(2)}) collective-permute-start(bf16[128,1024]{1,0:T(8,128)(2,1)S(1)} %get-tuple-element.79), channel_id=1, source_target_pairs={{0,16},{1,17},{2,18},{3,19},{4,20},{5,21},{6,22},{7,23},{8,24},{9,... | collective-permute-start | bytes 786440 | tf_op jit(solution)/shard_map/ppermute | solution.py:44
  86.4 6.9 %collective-permute-start.29 = (bf16[512,768]{1,0:T(8,128)(2,1)S(1)}, bf16[512,768]{1,0:T(8,128)(2,1)S(1)}, u32[]{:S(2)}, u32[]{:S(2)}) collective-permute-start(bf16[512,768]{1,0:T(8,128)(2,1)S(1)} %shard_map.114), channel_id=1, source_target_pairs={{0,16},{1,17},{2,18},{3,19},{4,20},{5,21},{6,22},{7,23},{8,24},{9,... | collective-permute-start | bytes 2359304 | tf_op jit(solution)/shard_map/ppermute | solution.py:44
  87.3 20.4 %collective-permute-start.32 = (bf16[512,1024]{1,0:T(8,128)(2,1)S(1)}, bf16[512,1024]{1,0:T(8,128)(2,1)S(1)}, u32[]{:S(2)}, u32[]{:S(2)}) collective-permute-start(bf16[512,1024]{1,0:T(8,128)(2,1)S(1)} %shard_map.120), channel_id=1, source_target_pairs={{0,96},{1,97},{2,98},{3,99},{4,100},{5,101},{6,102},{7,103},{8,104... | collective-permute-start | bytes 3145736 | tf_op jit(solution)/shard_map/ppermute | solution.py:44
  91.4 16.3 %collective-permute-start.31 = (bf16[512,1024]{1,0:T(8,128)(2,1)S(1)}, bf16[512,1024]{1,0:T(8,128)(2,1)S(1)}, u32[]{:S(2)}, u32[]{:S(2)}) collective-permute-start(bf16[512,1024]{1,0:T(8,128)(2,1)S(1)} %shard_map.121), channel_id=1, source_target_pairs={{0,16},{1,17},{2,18},{3,19},{4,20},{5,21},{6,22},{7,23},{8,24},{9,... | collective-permute-start | bytes 3145736 | tf_op jit(solution)/shard_map/ppermute | solution.py:44
  93.2 7.9 %collective-permute-start.27 = (bf16[96,2048]{1,0:T(8,128)(2,1)S(1)}, bf16[96,2048]{1,0:T(8,128)(2,1)S(1)}, u32[]{:S(2)}, u32[]{:S(2)}) collective-permute-start(bf16[96,2048]{1,0:T(8,128)(2,1)S(1)} %pad_maximum_fusion.1), channel_id=1, source_target_pairs={{0,4},{1,5},{2,6},{3,7},{4,0},{5,1},{6,2},{7,3},{8,12},{9,13},{10,... | collective-permute-start | bytes 1179656 | tf_op jit(solution)/shard_map/ppermute | solution.py:44
  93.7 7.3 %copy-start.4 = (f32[96,96]{1,0:T(8,128)S(1)}, f32[96,96]{1,0:T(8,128)}, u32[]{:S(2)}) copy-start(f32[96,96]{1,0:T(8,128)} %constant.8.clone) | copy-start | bytes 110596
  93.7 14.6 %collective-permute-start.30 = (bf16[256,768]{1,0:T(8,128)(2,1)S(1)}, bf16[256,768]{1,0:T(8,128)(2,1)S(1)}, u32[]{:S(2)}, u32[]{:S(2)}) collective-permute-start(bf16[256,768]{1,0:T(8,128)(2,1)S(1)} %fusion.7), channel_id=1, source_target_pairs={{0,32},{1,33},{2,34},{3,35},{4,36},{5,37},{6,38},{7,39},{8,40},{9,... | collective-permute-start | bytes 1179656 | tf_op jit(solution)/shard_map/ppermute | solution.py:44
  101.9 11.2 %collective-permute-start.28 = (bf16[48,2048]{1,0:T(8,128)(2,1)S(1)}, bf16[48,2048]{1,0:T(8,128)(2,1)S(1)}, u32[]{:S(2)}, u32[]{:S(2)}) collective-permute-start(bf16[48,2048]{1,0:T(8,128)(2,1)S(1)} %slice.140), channel_id=1, source_target_pairs={{0,3},{1,2},{2,1},{3,0},{4,7},{5,6},{6,5},{7,4},{8,11},{9,10},{10,... | collective-permute-start | bytes 589832 | tf_op jit(solution)/shard_map/ppermute | solution.py:44
  108.2 9.3 %collective-permute-start.34 = (bf16[256,1024]{1,0:T(8,128)(2,1)S(1)}, bf16[256,1024]{1,0:T(8,128)(2,1)S(1)}, u32[]{:S(2)}, u32[]{:S(2)}) collective-permute-start(bf16[256,1024]{1,0:T(8,128)(2,1)S(1)} %fusion.4), channel_id=1, source_target_pairs={{0,32},{1,33},{2,34},{3,35},{4,36},{5,37},{6,38},{7,39},{8,40},{9,... | collective-permute-start | bytes 1572872 | tf_op jit(solution)/shard_map/ppermute | solution.py:44
  113.1 4.4 %collective-permute-start.33 = (bf16[12,2048]{1,0:T(8,128)(2,1)S(1)}, bf16[12,2048]{1,0:T(8,128)(2,1)S(1)}, u32[]{:S(2)}, u32[]{:S(2)}) collective-permute-start(bf16[12,2048]{1,0:T(8,128)(2,1)S(1)} %get-tuple-element.101), channel_id=1, source_target_pairs={{0,128},{1,129},{2,130},{3,131},{4,132},{5,133},{6,134},{7,135},{8... | collective-permute-start | bytes 147464 | tf_op jit(solution)/shard_map/ppermute | solution.py:44
  114.0 5.3 %collective-permute-start.35 = (bf16[12,2048]{1,0:T(8,128)(2,1)S(1)}, bf16[12,2048]{1,0:T(8,128)(2,1)S(1)}, u32[]{:S(2)}, u32[]{:S(2)}) collective-permute-start(bf16[12,2048]{1,0:T(8,128)(2,1)S(1)} %get-tuple-element.100), channel_id=1, source_target_pairs={{0,1},{1,0},{2,3},{3,2},{4,5},{5,4},{6,7},{7,6},{8,9},{9,8},{10,11... | collective-permute-start | bytes 147464 | tf_op jit(solution)/shard_map/ppermute | solution.py:44
  115.7 4.6 %collective-permute-start.36 = (bf16[12,2048]{1,0:T(8,128)(2,1)S(1)}, bf16[12,2048]{1,0:T(8,128)(2,1)S(1)}, u32[]{:S(2)}, u32[]{:S(2)}) collective-permute-start(bf16[12,2048]{1,0:T(8,128)(2,1)S(1)} %get-tuple-element.99), channel_id=1, source_target_pairs={{0,129},{1,128},{2,131},{3,130},{4,133},{5,132},{6,135},{7,134},{8... | collective-permute-start | bytes 147464 | tf_op jit(solution)/shard_map/ppermute | solution.py:44

commit v6 on v5

--- a/solution.py
+++ b/solution.py
@@ -488,7 +488,7 @@
         by_group.T.astype(np.float32),
         add(kept, arrived),
         preferred_element_type=F32,
-        precision=lax.Precision.HIGHEST,
+        precision=lax.Precision.HIGH,
     )
     part = 4 * rows
     passed = second_sum(second, second_low, second_b)

time: 123 us -> 123 us (level)
  transfers between devices with their start and end apart: 37 -> 37, of which waited for: 17 -> 19; matrix products, arithmetic and copies ran while one was open for 3% -> 3% of each run, Pallas kernels for 14% -> 14%
where the time goes in v6:
time: 123 us; the launch traced here: 121 us
  starting transfers between devices  47.6 us (39%)
  waiting for transfers between devices  47.5 us (39%)
  Pallas kernels  21 us (17%)
  matrix products  2.69 us (2%)
    ppermute x37, starting transfers between devices, send(): return lax.ppermute(value, BOTH, pairs)  47.6 us
    ppermute x37, waiting for transfers between devices, send(): return lax.ppermute(value, BOTH, pairs)  47.5 us
    pallas_call x6, Pallas kernels, weight_product(): call(functools.partial(weight_kernel, first, len(added)), outs, [VMEM] *...  4 us
    pallas_call x3, Pallas kernels, stack(): call(stack_kernel, out, [ANY] * len(pieces), VMEM, [pltpu.SemaphoreType.D...  2.65 us
    pallas_call x1, Pallas kernels, backward(): call(functools.partial(backward_kernel, side), array((rows, 2 * mine.shap...  2.52 us
  transfers between devices with their start and end apart: 37, of which 19 were waited for; matrix products, arithmetic and copies ran while one was open for 3% of the time, Pallas kernels for 14%

profile of v6, /device:TPU:64, one launch (start us, length us, event | category | flops | bytes accessed | tf_op | source)
XLA Modules:
  0.0 120.7 jit_solution(15637864789375039501)
XLA Ops:
  0.7 1.2 %shard_map.103.refs_0_ = bf16[256,1792]{1,0:T(8,128)(2,1)S(1)} custom-call(bf16[256,896]{1,0:T(8,128)(2,1)} %gate.1, bf16[256,896]{1,0:T(8,128)(2,1)} %up.1), custom_call_target="tpu_custom_call" | custom-call | tf_op jit(solution)/shard_map/pallas_call | solution.py:93
  1.9 1.7 %collective-permute-start.4 = (bf16[256,1792]{1,0:T(8,128)(2,1)S(1)}, bf16[256,1792]{1,0:T(8,128)(2,1)S(1)}, u32[]{:S(2)}, u32[]{:S(2)}) collective-permute-start(bf16[256,1792]{1,0:T(8,128)(2,1)S(1)} %shard_map.103.refs_0_), channel_id=1, source_target_pairs={{0,32},{1,33},{2,34},{3,35},{4,36},{5,37},{6,38},{7,39},{8,40},{9,... | collective-permute-start | bytes 2752520 | tf_op jit(solution)/shard_map/ppermute | solution.py:44
  3.7 2.0 %collective-permute-start = (bf16[12,2048]{1,0:T(8,128)(2,1)S(1)}, bf16[12,2048]{1,0:T(8,128)(2,1)S(1)}, u32[]{:S(2)}, u32[]{:S(2)}) collective-permute-start(bf16[12,2048]{1,0:T(8,128)(2,1)S(1)} %get-tuple-element.49), channel_id=1, source_target_pairs={{0,128},{1,129},{2,130},{3,131},{4,132},{5,133},{6,134},{7,135},{8... | collective-permute-start | bytes 147464 | tf_op jit(solution)/shard_map/ppermute | solution.py:44
  5.7 1.6 %collective-permute-start.2 = (bf16[12,2048]{1,0:T(8,128)(2,1)S(1)}, bf16[12,2048]{1,0:T(8,128)(2,1)S(1)}, u32[]{:S(2)}, u32[]{:S(2)}) collective-permute-start(bf16[12,2048]{1,0:T(8,128)(2,1)S(1)} %get-tuple-element.49), channel_id=1, source_target_pairs={{0,129},{1,128},{2,131},{3,130},{4,133},{5,132},{6,135},{7,134},{8... | collective-permute-start | bytes 147464 | tf_op jit(solution)/shard_map/ppermute | solution.py:44
  7.3 2.2 %collective-permute-start.6 = (bf16[256,1792]{1,0:T(8,128)(2,1)S(1)}, bf16[256,1792]{1,0:T(8,128)(2,1)S(1)}, u32[]{:S(2)}, u32[]{:S(2)}) collective-permute-start(bf16[256,1792]{1,0:T(8,128)(2,1)S(1)} %shard_map.103.refs_0_), channel_id=1, source_target_pairs={{0,96},{1,97},{2,98},{3,99},{4,100},{5,101},{6,102},{7,103},{8,104... | collective-permute-start | bytes 2752520 | tf_op jit(solution)/shard_map/ppermute | solution.py:44
  9.5 1.5 %collective-permute-done.1 = bf16[12,2048]{1,0:T(8,128)(2,1)S(1)} collective-permute-done((bf16[12,2048]{1,0:T(8,128)(2,1)S(1)}, bf16[12,2048]{1,0:T(8,128)(2,1)S(1)}, u32[]{:S(2)}, u32[]{:S(2)}) %collective-permute-start.1) | collective-permute-done | bytes 49184 | tf_op jit(solution)/shard_map/ppermute | solution.py:44
  11.0 5.7 %collective-permute-start.7 = (bf16[256,1792]{1,0:T(8,128)(2,1)S(1)}, bf16[256,1792]{1,0:T(8,128)(2,1)S(1)}, u32[]{:S(2)}, u32[]{:S(2)}) collective-permute-start(bf16[256,1792]{1,0:T(8,128)(2,1)S(1)} %shard_map.103.refs_0_), channel_id=1, source_target_pairs={{0,16},{1,17},{2,18},{3,19},{4,20},{5,21},{6,22},{7,23},{8,24},{9,... | collective-permute-start | bytes 2752520 | tf_op jit(solution)/shard_map/ppermute | solution.py:44
  16.7 0.5 collective-permute-start.3
  17.3 1.1 collective-permute-done.4.refs_1_.refs_0_
  18.3 5.3 %collective-permute-start.10 = (bf16[256,1792]{1,0:T(8,128)(2,1)S(1)}, bf16[256,1792]{1,0:T(8,128)(2,1)S(1)}, u32[]{:S(2)}, u32[]{:S(2)}) collective-permute-start(bf16[256,1792]{1,0:T(8,128)(2,1)S(1)} %collective-permute-done.4.refs_1_.refs_0_), channel_id=1, source_target_pairs={{0,96},{1,97},{2,98},{3,99},{4,100},{5,101},{6,102},{7,103},{8,104... | collective-permute-start | bytes 2752520 | tf_op jit(solution)/shard_map/ppermute | solution.py:44
  23.9 1.1 collective-permute-done.3
  25.2 1.6 %collective-permute-start.5 = (bf16[96,2048]{1,0:T(8,128)(2,1)S(1)}, bf16[96,2048]{1,0:T(8,128)(2,1)S(1)}, u32[]{:S(2)}, u32[]{:S(2)}) collective-permute-start(bf16[96,2048]{1,0:T(8,128)(2,1)S(1)} %fusion.1), channel_id=1, source_target_pairs={{0,4},{1,5},{2,6},{3,7},{4,0},{5,1},{6,2},{7,3},{8,12},{9,13},{10,... | collective-permute-start | bytes 1179656 | tf_op jit(solution)/shard_map/ppermute | solution.py:44
  27.1 2.3 %collective-permute-start.9 = (bf16[192,896]{1,0:T(8,128)(2,1)S(1)}, bf16[192,896]{1,0:T(8,128)(2,1)S(1)}, u32[]{:S(2)}, u32[]{:S(2)}) collective-permute-start(bf16[192,896]{1,0:T(8,128)(2,1)S(1)} %shard_map.105.own_stream), channel_id=1, source_target_pairs={{0,128},{1,129},{2,130},{3,131},{4,132},{5,133},{6,134},{7,135},{8... | collective-permute-start | bytes 1032200 | tf_op jit(solution)/shard_map/ppermute | solution.py:44
  29.4 3.7 %collective-permute-done.5 = bf16[96,2048]{1,0:T(8,128)(2,1)S(1)} collective-permute-done((bf16[96,2048]{1,0:T(8,128)(2,1)S(1)}, bf16[96,2048]{1,0:T(8,128)(2,1)S(1)}, u32[]{:S(2)}, u32[]{:S(2)}) %collective-permute-start.5) | collective-permute-done | bytes 393248 | tf_op jit(solution)/shard_map/ppermute | solution.py:44
  33.1 2.8 %collective-permute-start.8 = (bf16[192,2048]{1,0:T(8,128)(2,1)S(1)}, bf16[192,2048]{1,0:T(8,128)(2,1)S(1)}, u32[]{:S(2)}, u32[]{:S(2)}) collective-permute-start(bf16[192,2048]{1,0:T(8,128)(2,1)S(1)} %pad_maximum_fusion.near), channel_id=1, source_target_pairs={{0,12},{1,13},{2,14},{3,15},{4,8},{5,9},{6,10},{7,11},{8,4},{9,5},... | collective-permute-start | bytes 2359304 | tf_op jit(solution)/shard_map/ppermute | solution.py:44
  36.5 0.9 shard_map.106.mine
  37.6 0.6 collective-permute-start.11
  38.3 0.5 collective-permute-start.13
  38.8 7.6 %collective-permute-done.8.away = bf16[192,2048]{1,0:T(8,128)(2,1)S(1)} collective-permute-done((bf16[192,2048]{1,0:T(8,128)(2,1)S(1)}, bf16[192,2048]{1,0:T(8,128)(2,1)S(1)}, u32[]{:S(2)}, u32[]{:S(2)}) %collective-permute-start.8) | collective-permute-done | bytes 786464 | tf_op jit(solution)/shard_map/ppermute | solution.py:44
  46.4 2.0 %shard_map.108 = (bf16[384,2048]{1,0:T(8,128)(2,1)S(1)}, f32[384,768]{1,0:T(8,128)S(1)}, bf16[384,768]{1,0:T(8,128)(2,1)S(1)}) custom-call(bf16[192,2048]{1,0:T(8,128)(2,1)S(1)} %pad_maximum_fusion.near, bf16[192,2048]{1,0:T(8,128)(2,1)S(1)} %collective-permute-done.8.away, bf16[1024,1792]{1,0:T(8,128)(2,1)S(1)} %shard_map.106.mine, ...), custom_call_target="tpu_custom_call" | custom-call | tf_op jit(solution)/shard_map/pallas_call | solution.py:235
  48.4 2.5 %collective-permute-start.15 = (bf16[384,768]{1,0:T(8,128)(2,1)S(1)}, bf16[384,768]{1,0:T(8,128)(2,1)S(1)}, u32[]{:S(2)}, u32[]{:S(2)}) collective-permute-start(bf16[384,768]{1,0:T(8,128)(2,1)S(1)} %get-tuple-element.61), channel_id=1, source_target_pairs={{0,128},{1,129},{2,130},{3,131},{4,132},{5,133},{6,134},{7,135},{8... | collective-permute-start | bytes 1769480 | tf_op jit(solution)/shard_map/ppermute | solution.py:44
  50.9 1.3 %shard_map.109.theirs = bf16[1024,1792]{1,0:T(8,128)(2,1)S(1)} custom-call(bf16[256,1792]{1,0:T(8,128)(2,1)S(1)} %collective-permute-done.7.refs_0_, bf16[192,1792]{1,0:T(8,128)(2,1)S(1)} %collective-permute-done.11.refs_1_, bf16[192,1792]{1,0:T(8,128)(2,1)S(1)} %collective-permute-done.12.refs_2_, bf16[128,1792]{1,0:T(8,128)(2,1)S(1)} %collective-permute-done.13.refs_3_, ...), custom_call_target="tpu_custom_call" | custom-call | tf_op jit(solution)/shard_map/pallas_call | solution.py:184
  52.2 1.8 %shard_map.110 = (f32[384,1024]{1,0:T(8,128)S(1)}, bf16[384,1024]{1,0:T(8,128)(2,1)S(1)}) custom-call(bf16[384,2048]{1,0:T(8,128)(2,1)S(1)} %get-tuple-element.62.rows.inputs, bf16[1024,1792]{1,0:T(8,128)(2,1)S(1)} %shard_map.106.mine, bf16[1024,1792]{1,0:T(8,128)(2,1)S(1)} %shard_map.109.theirs), custom_call_target="tpu_custom_call" | custom-call | tf_op jit(solution)/shard_map/pallas_call | solution.py:248
  54.1 11.1 %collective-permute-done.15.sent = bf16[384,768]{1,0:T(8,128)(2,1)S(1)} collective-permute-done((bf16[384,768]{1,0:T(8,128)(2,1)S(1)}, bf16[384,768]{1,0:T(8,128)(2,1)S(1)}, u32[]{:S(2)}, u32[]{:S(2)}) %collective-permute-start.15) | collective-permute-done | bytes 589856 | tf_op jit(solution)/shard_map/ppermute | solution.py:44
  65.5 0.6 shard_map.112
  66.2 0.5 collective-permute-start.18
  68.5 0.6 shard_map.113
  69.2 0.6 shard_map.114
  69.8 2.0 %shard_map.115.before = f32[192,2048]{1,0:T(8,128)S(1)} custom-call(bf16[384,768]{1,0:T(8,128)(2,1)S(1)} %shard_map.111.grad.first, bf16[1024,1792]{1,0:T(8,128)(2,1)S(1)} %shard_map.106.mine, bf16[1024,1792]{1,0:T(8,128)(2,1)S(1)} %shard_map.109.theirs), custom_call_target="tpu_custom_call" | custom-call | tf_op jit(solution)/shard_map/pallas_call | solution.py:347
  71.8 5.7 %collective-permute-done.16.sent = bf16[384,1024]{1,0:T(8,128)(2,1)S(1)} collective-permute-done((bf16[384,1024]{1,0:T(8,128)(2,1)S(1)}, bf16[384,1024]{1,0:T(8,128)(2,1)S(1)}, u32[]{:S(2)}, u32[]{:S(2)}) %collective-permute-start.16) | collective-permute-done | bytes 786464 | tf_op jit(solution)/shard_map/ppermute | solution.py:44
  78.0 1.5 %shard_map.117 = bf16[192,2048]{1,0:T(8,128)(2,1)S(1)} custom-call(f32[192,2048]{1,0:T(8,128)S(1)} %shard_map.115.before, bf16[384,1024]{1,0:T(8,128)(2,1)S(1)} %shard_map.116.second.grad, bf16[1024,1792]{1,0:T(8,128)(2,1)S(1)} %shard_map.106.mine, bf16[1024,1792]{1,0:T(8,128)(2,1)S(1)} %shard_map.109.theirs), custom_call_target="tpu_custom_call" | custom-call | tf_op jit(solution)/shard_map/pallas_call | solution.py:376
  79.5 2.5 %collective-permute-start.22 = (bf16[192,2048]{1,0:T(8,128)(2,1)S(1)}, bf16[192,2048]{1,0:T(8,128)(2,1)S(1)}, u32[]{:S(2)}, u32[]{:S(2)}) collective-permute-start(bf16[192,2048]{1,0:T(8,128)(2,1)S(1)} %shard_map.117), channel_id=1, source_target_pairs={{0,12},{1,13},{2,14},{3,15},{4,8},{5,9},{6,10},{7,11},{8,4},{9,5},... | collective-permute-start | bytes 2359304 | tf_op jit(solution)/shard_map/ppermute | solution.py:44
  82.0 0.7 shard_map.118
  82.8 0.5 collective-permute-start.24
  83.8 2.5 %shard_map.119 = bf16[192,2048]{1,0:T(8,128)(2,1)S(1)} custom-call(bf16[384,768]{1,0:T(8,128)(2,1)S(1)} %shard_map.111.grad.first, bf16[384,1024]{1,0:T(8,128)(2,1)S(1)} %shard_map.116.second.grad, bf16[1024,1792]{1,0:T(8,128)(2,1)S(1)} %shard_map.106.mine, bf16[1024,1792]{1,0:T(8,128)(2,1)S(1)} %shard_map.109.theirs), custom_call_target="tpu_custom_call" | custom-call | tf_op jit(solution)/shard_map/pallas_call | solution.py:287
  86.6 0.7 shard_map.120
  87.3 3.3 %collective-permute-start.32 = (bf16[512,1024]{1,0:T(8,128)(2,1)S(1)}, bf16[512,1024]{1,0:T(8,128)(2,1)S(1)}, u32[]{:S(2)}, u32[]{:S(2)}) collective-permute-start(bf16[512,1024]{1,0:T(8,128)(2,1)S(1)} %shard_map.120), channel_id=1, source_target_pairs={{0,96},{1,97},{2,98},{3,99},{4,100},{5,101},{6,102},{7,103},{8,104... | collective-permute-start | bytes 3145736 | tf_op jit(solution)/shard_map/ppermute | solution.py:44
  90.6 0.7 shard_map.121
  91.5 1.3 %collective-permute-done.22 = bf16[192,2048]{1,0:T(8,128)(2,1)S(1)} collective-permute-done((bf16[192,2048]{1,0:T(8,128)(2,1)S(1)}, bf16[192,2048]{1,0:T(8,128)(2,1)S(1)}, u32[]{:S(2)}, u32[]{:S(2)}) %collective-permute-start.22) | collective-permute-done | bytes 786464 | tf_op jit(solution)/shard_map/ppermute | solution.py:44
  94.3 6.8 %collective-permute-done.27 = bf16[96,2048]{1,0:T(8,128)(2,1)S(1)} collective-permute-done((bf16[96,2048]{1,0:T(8,128)(2,1)S(1)}, bf16[96,2048]{1,0:T(8,128)(2,1)S(1)}, u32[]{:S(2)}, u32[]{:S(2)}) %collective-permute-start.27) | collective-permute-done | bytes 393248 | tf_op jit(solution)/shard_map/ppermute | solution.py:44
  101.6 5.8 %collective-permute-start.28 = (bf16[48,2048]{1,0:T(8,128)(2,1)S(1)}, bf16[48,2048]{1,0:T(8,128)(2,1)S(1)}, u32[]{:S(2)}, u32[]{:S(2)}) collective-permute-start(bf16[48,2048]{1,0:T(8,128)(2,1)S(1)} %slice.140), channel_id=1, source_target_pairs={{0,3},{1,2},{2,1},{3,0},{4,7},{5,6},{6,5},{7,4},{8,11},{9,10},{10,... | collective-permute-start | bytes 589832 | tf_op jit(solution)/shard_map/ppermute | solution.py:44
  108.2 4.4 %collective-permute-done.28 = bf16[48,2048]{1,0:T(8,128)(2,1)S(1)} collective-permute-done((bf16[48,2048]{1,0:T(8,128)(2,1)S(1)}, bf16[48,2048]{1,0:T(8,128)(2,1)S(1)}, u32[]{:S(2)}, u32[]{:S(2)}) %collective-permute-start.28) | collective-permute-done | bytes 196640 | tf_op jit(solution)/shard_map/ppermute | solution.py:44
  112.8 0.9 collective-permute-start.33
  113.7 1.8 %collective-permute-start.35 = (bf16[12,2048]{1,0:T(8,128)(2,1)S(1)}, bf16[12,2048]{1,0:T(8,128)(2,1)S(1)}, u32[]{:S(2)}, u32[]{:S(2)}) collective-permute-start(bf16[12,2048]{1,0:T(8,128)(2,1)S(1)} %get-tuple-element.100), channel_id=1, source_target_pairs={{0,1},{1,0},{2,3},{3,2},{4,5},{5,4},{6,7},{7,6},{8,9},{9,8},{10,11... | collective-permute-start | bytes 147464 | tf_op jit(solution)/shard_map/ppermute | solution.py:44
  115.4 0.9 collective-permute-start.36
  117.4 1.4 %shard_map.123 = (f32[256,896]{1,0:T(8,128)}, f32[256,896]{1,0:T(8,128)}) custom-call(f32[256,768]{1,0:T(8,128)S(1)} %fusion.6.first, f32[256,1024]{1,0:T(8,128)S(1)} %fusion.2.second, bf16[256,768]{1,0:T(8,128)(2,1)S(1)} %collective-permute-done.30.first_last, bf16[256,1024]{1,0:T(8,128)(2,1)S(1)} %collective-permute-done.34.second_last), custom_call_target="tpu_custom_call" | custom-call | tf_op jit(solution)/shard_map/pallas_call | solution.py:396
  118.9 1.1 collective-permute-done.36.from_both
  120.0 0.7 shard_map.122
  (80 shorter events, 9.6 us)
Async XLA Ops:
  0.6 23.0 %copy-start.5 = (bf16[96,48]{1,0:T(8,128)(2,1)S(1)}, bf16[96,48]{1,0:T(8,128)(2,1)}, u32[]{:S(2)}) copy-start(bf16[96,48]{1,0:T(8,128)(2,1)} %constant.11) | copy-start | bytes 27652
  0.6 24.3 %copy-start.6 = (bf16[96,48]{1,0:T(8,128)(2,1)S(1)}, bf16[96,48]{1,0:T(8,128)(2,1)}, u32[]{:S(2)}) copy-start(bf16[96,48]{1,0:T(8,128)(2,1)} %constant.12) | copy-start | bytes 27652
  0.7 2.9 %copy-start.1 = (bf16[12,4096]{1,0:T(8,128)(2,1)S(1)}, bf16[12,4096]{1,0:T(8,128)(2,1)}, u32[]{:S(2)}) copy-start(bf16[12,4096]{1,0:T(8,128)(2,1)} %codes) | copy-start | bytes 294916
  0.7 2.9 %copy-start.3 = (bf16[12,32]{1,0:T(8,128)(2,1)S(1)}, bf16[12,32]{1,0:T(8,128)(2,1)}, u32[]{:S(2)}) copy-start(bf16[12,32]{1,0:T(8,128)(2,1)} %scales) | copy-start | bytes 2308
  1.9 24.9 %copy-start = (bf16[192,896]{1,0:T(8,128)(2,1)S(1)}, bf16[192,896]{1,0:T(8,128)(2,1)}, u32[]{:S(2)}) copy-start(bf16[192,896]{1,0:T(8,128)(2,1)} %values.1) | copy-start | bytes 1032196
  1.9 24.9 %copy-start.2 = (s32[32,1,192]{2,1,0:T(1,128)S(1)}, s32[32,1,192]{2,1,0:T(1,128)}, u32[]{:S(2)}) copy-start(s32[32,1,192]{2,1,0:T(1,128)} %constant.7.clone.table) | copy-start | bytes 73732
  1.9 16.4 %collective-permute-start.4 = (bf16[256,1792]{1,0:T(8,128)(2,1)S(1)}, bf16[256,1792]{1,0:T(8,128)(2,1)S(1)}, u32[]{:S(2)}, u32[]{:S(2)}) collective-permute-start(bf16[256,1792]{1,0:T(8,128)(2,1)S(1)} %shard_map.103.refs_0_), channel_id=1, source_target_pairs={{0,32},{1,33},{2,34},{3,35},{4,36},{5,37},{6,38},{7,39},{8,40},{9,... | collective-permute-start | bytes 2752520 | tf_op jit(solution)/shard_map/ppermute | solution.py:44
  3.7 5.8 %collective-permute-start = (bf16[12,2048]{1,0:T(8,128)(2,1)S(1)}, bf16[12,2048]{1,0:T(8,128)(2,1)S(1)}, u32[]{:S(2)}, u32[]{:S(2)}) collective-permute-start(bf16[12,2048]{1,0:T(8,128)(2,1)S(1)} %get-tuple-element.49), channel_id=1, source_target_pairs={{0,128},{1,129},{2,130},{3,131},{4,132},{5,133},{6,134},{7,135},{8... | collective-permute-start | bytes 147464 | tf_op jit(solution)/shard_map/ppermute | solution.py:44
  5.7 5.2 %collective-permute-start.1 = (bf16[12,2048]{1,0:T(8,128)(2,1)S(1)}, bf16[12,2048]{1,0:T(8,128)(2,1)S(1)}, u32[]{:S(2)}, u32[]{:S(2)}) collective-permute-start(bf16[12,2048]{1,0:T(8,128)(2,1)S(1)} %get-tuple-element.48), channel_id=1, source_target_pairs={{0,1},{1,0},{2,3},{3,2},{4,5},{5,4},{6,7},{7,6},{8,9},{9,8},{10,11... | collective-permute-start | bytes 147464 | tf_op jit(solution)/shard_map/ppermute | solution.py:44
  5.7 5.2 %collective-permute-start.2 = (bf16[12,2048]{1,0:T(8,128)(2,1)S(1)}, bf16[12,2048]{1,0:T(8,128)(2,1)S(1)}, u32[]{:S(2)}, u32[]{:S(2)}) collective-permute-start(bf16[12,2048]{1,0:T(8,128)(2,1)S(1)} %get-tuple-element.49), channel_id=1, source_target_pairs={{0,129},{1,128},{2,131},{3,130},{4,133},{5,132},{6,135},{7,134},{8... | collective-permute-start | bytes 147464 | tf_op jit(solution)/shard_map/ppermute | solution.py:44
  7.3 22.1 %collective-permute-start.6 = (bf16[256,1792]{1,0:T(8,128)(2,1)S(1)}, bf16[256,1792]{1,0:T(8,128)(2,1)S(1)}, u32[]{:S(2)}, u32[]{:S(2)}) collective-permute-start(bf16[256,1792]{1,0:T(8,128)(2,1)S(1)} %shard_map.103.refs_0_), channel_id=1, source_target_pairs={{0,96},{1,97},{2,98},{3,99},{4,100},{5,101},{6,102},{7,103},{8,104... | collective-permute-start | bytes 2752520 | tf_op jit(solution)/shard_map/ppermute | solution.py:44
  11.0 18.4 %collective-permute-start.7 = (bf16[256,1792]{1,0:T(8,128)(2,1)S(1)}, bf16[256,1792]{1,0:T(8,128)(2,1)S(1)}, u32[]{:S(2)}, u32[]{:S(2)}) collective-permute-start(bf16[256,1792]{1,0:T(8,128)(2,1)S(1)} %shard_map.103.refs_0_), channel_id=1, source_target_pairs={{0,16},{1,17},{2,18},{3,19},{4,20},{5,21},{6,22},{7,23},{8,24},{9,... | collective-permute-start | bytes 2752520 | tf_op jit(solution)/shard_map/ppermute | solution.py:44
  16.7 8.2 %collective-permute-start.3 = (bf16[48,2048]{1,0:T(8,128)(2,1)S(1)}, bf16[48,2048]{1,0:T(8,128)(2,1)S(1)}, u32[]{:S(2)}, u32[]{:S(2)}) collective-permute-start(bf16[48,2048]{1,0:T(8,128)(2,1)S(1)} %pad_maximum_fusion.2), channel_id=1, source_target_pairs={{0,3},{1,2},{2,1},{3,0},{4,7},{5,6},{6,5},{7,4},{8,11},{9,10},{10,... | collective-permute-start | bytes 589832 | tf_op jit(solution)/shard_map/ppermute | solution.py:44
  18.3 18.1 %collective-permute-start.10 = (bf16[256,1792]{1,0:T(8,128)(2,1)S(1)}, bf16[256,1792]{1,0:T(8,128)(2,1)S(1)}, u32[]{:S(2)}, u32[]{:S(2)}) collective-permute-start(bf16[256,1792]{1,0:T(8,128)(2,1)S(1)} %collective-permute-done.4.refs_1_.refs_0_), channel_id=1, source_target_pairs={{0,96},{1,97},{2,98},{3,99},{4,100},{5,101},{6,102},{7,103},{8,104... | collective-permute-start | bytes 2752520 | tf_op jit(solution)/shard_map/ppermute | solution.py:44
  25.2 7.9 %collective-permute-start.5 = (bf16[96,2048]{1,0:T(8,128)(2,1)S(1)}, bf16[96,2048]{1,0:T(8,128)(2,1)S(1)}, u32[]{:S(2)}, u32[]{:S(2)}) collective-permute-start(bf16[96,2048]{1,0:T(8,128)(2,1)S(1)} %fusion.1), channel_id=1, source_target_pairs={{0,4},{1,5},{2,6},{3,7},{4,0},{5,1},{6,2},{7,3},{8,12},{9,13},{10,... | collective-permute-start | bytes 1179656 | tf_op jit(solution)/shard_map/ppermute | solution.py:44
  27.1 11.2 %collective-permute-start.9 = (bf16[192,896]{1,0:T(8,128)(2,1)S(1)}, bf16[192,896]{1,0:T(8,128)(2,1)S(1)}, u32[]{:S(2)}, u32[]{:S(2)}) collective-permute-start(bf16[192,896]{1,0:T(8,128)(2,1)S(1)} %shard_map.105.own_stream), channel_id=1, source_target_pairs={{0,128},{1,129},{2,130},{3,131},{4,132},{5,133},{6,134},{7,135},{8... | collective-permute-start | bytes 1032200 | tf_op jit(solution)/shard_map/ppermute | solution.py:44
  33.1 13.3 %collective-permute-start.8 = (bf16[192,2048]{1,0:T(8,128)(2,1)S(1)}, bf16[192,2048]{1,0:T(8,128)(2,1)S(1)}, u32[]{:S(2)}, u32[]{:S(2)}) collective-permute-start(bf16[192,2048]{1,0:T(8,128)(2,1)S(1)} %pad_maximum_fusion.near), channel_id=1, source_target_pairs={{0,12},{1,13},{2,14},{3,15},{4,8},{5,9},{6,10},{7,11},{8,4},{9,5},... | collective-permute-start | bytes 2359304 | tf_op jit(solution)/shard_map/ppermute | solution.py:44
  37.4 9.0 %collective-permute-start.14 = (bf16[256,1792]{1,0:T(8,128)(2,1)S(1)}, bf16[256,1792]{1,0:T(8,128)(2,1)S(1)}, u32[]{:S(2)}, u32[]{:S(2)}) collective-permute-start(bf16[256,1792]{1,0:T(8,128)(2,1)S(1)} %collective-permute-done.10.refs_3_), channel_id=1, source_target_pairs={{0,16},{1,17},{2,18},{3,19},{4,20},{5,21},{6,22},{7,23},{8,24},{9,... | collective-permute-start | bytes 2752520 | tf_op jit(solution)/shard_map/ppermute | solution.py:44
  37.6 8.8 %collective-permute-start.11 = (bf16[192,1792]{1,0:T(8,128)(2,1)S(1)}, bf16[192,1792]{1,0:T(8,128)(2,1)S(1)}, u32[]{:S(2)}, u32[]{:S(2)}) collective-permute-start(bf16[192,1792]{1,0:T(8,128)(2,1)S(1)} %get-tuple-element.92), channel_id=1, source_target_pairs={{0,16},{1,17},{2,18},{3,19},{4,20},{5,21},{6,22},{7,23},{8,24},{9,... | collective-permute-start | bytes 2064392 | tf_op jit(solution)/shard_map/ppermute | solution.py:44
  38.2 8.3 %collective-permute-start.12 = (bf16[192,1792]{1,0:T(8,128)(2,1)S(1)}, bf16[192,1792]{1,0:T(8,128)(2,1)S(1)}, u32[]{:S(2)}, u32[]{:S(2)}) collective-permute-start(bf16[192,1792]{1,0:T(8,128)(2,1)S(1)} %get-tuple-element.91), channel_id=1, source_target_pairs={{0,16},{1,17},{2,18},{3,19},{4,20},{5,21},{6,22},{7,23},{8,24},{9,... | collective-permute-start | bytes 2064392 | tf_op jit(solution)/shard_map/ppermute | solution.py:44
  38.3 8.1 %collective-permute-start.13 = (bf16[128,1792]{1,0:T(8,128)(2,1)S(1)}, bf16[128,1792]{1,0:T(8,128)(2,1)S(1)}, u32[]{:S(2)}, u32[]{:S(2)}) collective-permute-start(bf16[128,1792]{1,0:T(8,128)(2,1)S(1)} %slice.104), channel_id=1, source_target_pairs={{0,16},{1,17},{2,18},{3,19},{4,20},{5,21},{6,22},{7,23},{8,24},{9,... | collective-permute-start | bytes 1376264 | tf_op jit(solution)/shard_map/ppermute | solution.py:44
  48.4 16.7 %collective-permute-start.15 = (bf16[384,768]{1,0:T(8,128)(2,1)S(1)}, bf16[384,768]{1,0:T(8,128)(2,1)S(1)}, u32[]{:S(2)}, u32[]{:S(2)}) collective-permute-start(bf16[384,768]{1,0:T(8,128)(2,1)S(1)} %get-tuple-element.61), channel_id=1, source_target_pairs={{0,128},{1,129},{2,130},{3,131},{4,132},{5,133},{6,134},{7,135},{8... | collective-permute-start | bytes 1769480 | tf_op jit(solution)/shard_map/ppermute | solution.py:44
  54.0 23.6 %collective-permute-start.16 = (bf16[384,1024]{1,0:T(8,128)(2,1)S(1)}, bf16[384,1024]{1,0:T(8,128)(2,1)S(1)}, u32[]{:S(2)}, u32[]{:S(2)}) collective-permute-start(bf16[384,1024]{1,0:T(8,128)(2,1)S(1)} %get-tuple-element.67), channel_id=1, source_target_pairs={{0,128},{1,129},{2,130},{3,131},{4,132},{5,133},{6,134},{7,135},{8... | collective-permute-start | bytes 2359304 | tf_op jit(solution)/shard_map/ppermute | solution.py:44
  66.1 1.5 %collective-permute-start.17 = (bf16[128,768]{1,0:T(8,128)(2,1)S(1)}, bf16[128,768]{1,0:T(8,128)(2,1)S(1)}, u32[]{:S(2)}, u32[]{:S(2)}) collective-permute-start(bf16[128,768]{1,0:T(8,128)(2,1)S(1)} %get-tuple-element.68), channel_id=1, source_target_pairs={{0,16},{1,17},{2,18},{3,19},{4,20},{5,21},{6,22},{7,23},{8,24},{9,... | collective-permute-start | bytes 589832 | tf_op jit(solution)/shard_map/ppermute | solution.py:44
  66.2 1.7 %collective-permute-start.18 = (bf16[128,768]{1,0:T(8,128)(2,1)S(1)}, bf16[128,768]{1,0:T(8,128)(2,1)S(1)}, u32[]{:S(2)}, u32[]{:S(2)}) collective-permute-start(bf16[128,768]{1,0:T(8,128)(2,1)S(1)} %get-tuple-element.69), channel_id=1, source_target_pairs={{0,16},{1,17},{2,18},{3,19},{4,20},{5,21},{6,22},{7,23},{8,24},{9,... | collective-permute-start | bytes 589832 | tf_op jit(solution)/shard_map/ppermute | solution.py:44
  66.7 1.5 %collective-permute-start.19 = (bf16[128,768]{1,0:T(8,128)(2,1)S(1)}, bf16[128,768]{1,0:T(8,128)(2,1)S(1)}, u32[]{:S(2)}, u32[]{:S(2)}) collective-permute-start(bf16[128,768]{1,0:T(8,128)(2,1)S(1)} %get-tuple-element.70), channel_id=1, source_target_pairs={{0,16},{1,17},{2,18},{3,19},{4,20},{5,21},{6,22},{7,23},{8,24},{9,... | collective-permute-start | bytes 589832 | tf_op jit(solution)/shard_map/ppermute | solution.py:44
  66.8 1.7 %collective-permute-start.20 = (bf16[128,768]{1,0:T(8,128)(2,1)S(1)}, bf16[128,768]{1,0:T(8,128)(2,1)S(1)}, u32[]{:S(2)}, u32[]{:S(2)}) collective-permute-start(bf16[128,768]{1,0:T(8,128)(2,1)S(1)} %get-tuple-element.71), channel_id=1, source_target_pairs={{0,16},{1,17},{2,18},{3,19},{4,20},{5,21},{6,22},{7,23},{8,24},{9,... | collective-permute-start | bytes 589832 | tf_op jit(solution)/shard_map/ppermute | solution.py:44
  69.1 14.3 %collective-permute-start.21 = (bf16[512,768]{1,0:T(8,128)(2,1)S(1)}, bf16[512,768]{1,0:T(8,128)(2,1)S(1)}, u32[]{:S(2)}, u32[]{:S(2)}) collective-permute-start(bf16[512,768]{1,0:T(8,128)(2,1)S(1)} %shard_map.113), channel_id=1, source_target_pairs={{0,96},{1,97},{2,98},{3,99},{4,100},{5,101},{6,102},{7,103},{8,104... | collective-permute-start | bytes 2359304 | tf_op jit(solution)/shard_map/ppermute | solution.py:44
  79.5 13.3 %collective-permute-start.22 = (bf16[192,2048]{1,0:T(8,128)(2,1)S(1)}, bf16[192,2048]{1,0:T(8,128)(2,1)S(1)}, u32[]{:S(2)}, u32[]{:S(2)}) collective-permute-start(bf16[192,2048]{1,0:T(8,128)(2,1)S(1)} %shard_map.117), channel_id=1, source_target_pairs={{0,12},{1,13},{2,14},{3,15},{4,8},{5,9},{6,10},{7,11},{8,4},{9,5},... | collective-permute-start | bytes 2359304 | tf_op jit(solution)/shard_map/ppermute | solution.py:44
  82.7 3.6 %collective-permute-start.23 = (bf16[128,1024]{1,0:T(8,128)(2,1)S(1)}, bf16[128,1024]{1,0:T(8,128)(2,1)S(1)}, u32[]{:S(2)}, u32[]{:S(2)}) collective-permute-start(bf16[128,1024]{1,0:T(8,128)(2,1)S(1)} %get-tuple-element.76), channel_id=1, source_target_pairs={{0,16},{1,17},{2,18},{3,19},{4,20},{5,21},{6,22},{7,23},{8,24},{9,... | collective-permute-start | bytes 786440 | tf_op jit(solution)/shard_map/ppermute | solution.py:44
  82.8 3.7 %collective-permute-start.24 = (bf16[128,1024]{1,0:T(8,128)(2,1)S(1)}, bf16[128,1024]{1,0:T(8,128)(2,1)S(1)}, u32[]{:S(2)}, u32[]{:S(2)}) collective-permute-start(bf16[128,1024]{1,0:T(8,128)(2,1)S(1)} %get-tuple-element.77), channel_id=1, source_target_pairs={{0,16},{1,17},{2,18},{3,19},{4,20},{5,21},{6,22},{7,23},{8,24},{9,... | collective-permute-start | bytes 786440 | tf_op jit(solution)/shard_map/ppermute | solution.py:44
  83.3 3.2 %collective-permute-start.25 = (bf16[128,1024]{1,0:T(8,128)(2,1)S(1)}, bf16[128,1024]{1,0:T(8,128)(2,1)S(1)}, u32[]{:S(2)}, u32[]{:S(2)}) collective-permute-start(bf16[128,1024]{1,0:T(8,128)(2,1)S(1)} %get-tuple-element.78), channel_id=1, source_target_pairs={{0,16},{1,17},{2,18},{3,19},{4,20},{5,21},{6,22},{7,23},{8,24},{9,... | collective-permute-start | bytes 786440 | tf_op jit(solution)/shard_map/ppermute | solution.py:44
  83.4 3.1 %collective-permute-start.26 = (bf16[128,1024]{1,0:T(8,128)(2,1)S(1)}, bf16[128,1024]{1,0:T(8,128)(2,1)S(1)}, u32[]{:S(2)}, u32[]{:S(2)}) collective-permute-start(bf16[128,1024]{1,0:T(8,128)(2,1)S(1)} %get-tuple-element.79), channel_id=1, source_target_pairs={{0,16},{1,17},{2,18},{3,19},{4,20},{5,21},{6,22},{7,23},{8,24},{9,... | collective-permute-start | bytes 786440 | tf_op jit(solution)/shard_map/ppermute | solution.py:44
  86.4 6.9 %collective-permute-start.29 = (bf16[512,768]{1,0:T(8,128)(2,1)S(1)}, bf16[512,768]{1,0:T(8,128)(2,1)S(1)}, u32[]{:S(2)}, u32[]{:S(2)}) collective-permute-start(bf16[512,768]{1,0:T(8,128)(2,1)S(1)} %shard_map.114), channel_id=1, source_target_pairs={{0,16},{1,17},{2,18},{3,19},{4,20},{5,21},{6,22},{7,23},{8,24},{9,... | collective-permute-start | bytes 2359304 | tf_op jit(solution)/shard_map/ppermute | solution.py:44
  87.3 20.3 %collective-permute-start.32 = (bf16[512,1024]{1,0:T(8,128)(2,1)S(1)}, bf16[512,1024]{1,0:T(8,128)(2,1)S(1)}, u32[]{:S(2)}, u32[]{:S(2)}) collective-permute-start(bf16[512,1024]{1,0:T(8,128)(2,1)S(1)} %shard_map.120), channel_id=1, source_target_pairs={{0,96},{1,97},{2,98},{3,99},{4,100},{5,101},{6,102},{7,103},{8,104... | collective-permute-start | bytes 3145736 | tf_op jit(solution)/shard_map/ppermute | solution.py:44
  91.4 16.0 %collective-permute-start.31 = (bf16[512,1024]{1,0:T(8,128)(2,1)S(1)}, bf16[512,1024]{1,0:T(8,128)(2,1)S(1)}, u32[]{:S(2)}, u32[]{:S(2)}) collective-permute-start(bf16[512,1024]{1,0:T(8,128)(2,1)S(1)} %shard_map.121), channel_id=1, source_target_pairs={{0,16},{1,17},{2,18},{3,19},{4,20},{5,21},{6,22},{7,23},{8,24},{9,... | collective-permute-start | bytes 3145736 | tf_op jit(solution)/shard_map/ppermute | solution.py:44
  93.2 7.9 %collective-permute-start.27 = (bf16[96,2048]{1,0:T(8,128)(2,1)S(1)}, bf16[96,2048]{1,0:T(8,128)(2,1)S(1)}, u32[]{:S(2)}, u32[]{:S(2)}) collective-permute-start(bf16[96,2048]{1,0:T(8,128)(2,1)S(1)} %pad_maximum_fusion.1), channel_id=1, source_target_pairs={{0,4},{1,5},{2,6},{3,7},{4,0},{5,1},{6,2},{7,3},{8,12},{9,13},{10,... | collective-permute-start | bytes 1179656 | tf_op jit(solution)/shard_map/ppermute | solution.py:44
  93.7 7.3 %copy-start.4 = (f32[96,96]{1,0:T(8,128)S(1)}, f32[96,96]{1,0:T(8,128)}, u32[]{:S(2)}) copy-start(f32[96,96]{1,0:T(8,128)} %constant.8.clone) | copy-start | bytes 110596
  93.7 14.5 %collective-permute-start.30 = (bf16[256,768]{1,0:T(8,128)(2,1)S(1)}, bf16[256,768]{1,0:T(8,128)(2,1)S(1)}, u32[]{:S(2)}, u32[]{:S(2)}) collective-permute-start(bf16[256,768]{1,0:T(8,128)(2,1)S(1)} %fusion.7), channel_id=1, source_target_pairs={{0,32},{1,33},{2,34},{3,35},{4,36},{5,37},{6,38},{7,39},{8,40},{9,... | collective-permute-start | bytes 1179656 | tf_op jit(solution)/shard_map/ppermute | solution.py:44
  101.6 11.1 %collective-permute-start.28 = (bf16[48,2048]{1,0:T(8,128)(2,1)S(1)}, bf16[48,2048]{1,0:T(8,128)(2,1)S(1)}, u32[]{:S(2)}, u32[]{:S(2)}) collective-permute-start(bf16[48,2048]{1,0:T(8,128)(2,1)S(1)} %slice.140), channel_id=1, source_target_pairs={{0,3},{1,2},{2,1},{3,0},{4,7},{5,6},{6,5},{7,4},{8,11},{9,10},{10,... | collective-permute-start | bytes 589832 | tf_op jit(solution)/shard_map/ppermute | solution.py:44
  108.1 9.3 %collective-permute-start.34 = (bf16[256,1024]{1,0:T(8,128)(2,1)S(1)}, bf16[256,1024]{1,0:T(8,128)(2,1)S(1)}, u32[]{:S(2)}, u32[]{:S(2)}) collective-permute-start(bf16[256,1024]{1,0:T(8,128)(2,1)S(1)} %fusion.4), channel_id=1, source_target_pairs={{0,32},{1,33},{2,34},{3,35},{4,36},{5,37},{6,38},{7,39},{8,40},{9,... | collective-permute-start | bytes 1572872 | tf_op jit(solution)/shard_map/ppermute | solution.py:44
  112.8 4.5 %collective-permute-start.33 = (bf16[12,2048]{1,0:T(8,128)(2,1)S(1)}, bf16[12,2048]{1,0:T(8,128)(2,1)S(1)}, u32[]{:S(2)}, u32[]{:S(2)}) collective-permute-start(bf16[12,2048]{1,0:T(8,128)(2,1)S(1)} %get-tuple-element.101), channel_id=1, source_target_pairs={{0,128},{1,129},{2,130},{3,131},{4,132},{5,133},{6,134},{7,135},{8... | collective-permute-start | bytes 147464 | tf_op jit(solution)/shard_map/ppermute | solution.py:44
  113.7 5.3 %collective-permute-start.35 = (bf16[12,2048]{1,0:T(8,128)(2,1)S(1)}, bf16[12,2048]{1,0:T(8,128)(2,1)S(1)}, u32[]{:S(2)}, u32[]{:S(2)}) collective-permute-start(bf16[12,2048]{1,0:T(8,128)(2,1)S(1)} %get-tuple-element.100), channel_id=1, source_target_pairs={{0,1},{1,0},{2,3},{3,2},{4,5},{5,4},{6,7},{7,6},{8,9},{9,8},{10,11... | collective-permute-start | bytes 147464 | tf_op jit(solution)/shard_map/ppermute | solution.py:44
  115.4 4.6 %collective-permute-start.36 = (bf16[12,2048]{1,0:T(8,128)(2,1)S(1)}, bf16[12,2048]{1,0:T(8,128)(2,1)S(1)}, u32[]{:S(2)}, u32[]{:S(2)}) collective-permute-start(bf16[12,2048]{1,0:T(8,128)(2,1)S(1)} %get-tuple-element.99), channel_id=1, source_target_pairs={{0,129},{1,128},{2,131},{3,130},{4,133},{5,132},{6,135},{7,134},{8... | collective-permute-start | bytes 147464 | tf_op jit(solution)/shard_map/ppermute | solution.py:44
